TPU v7x, 128 devices: a whole 4x4x4 slice. The times are simulated.
128 devices in a mesh: dp: 32 (over x, z_lo, y), tensor: 4 (over z_hi, core).
Axes of the slice: x: 4, y: 4, z: 4 (z_hi: 2, z_lo: 2; z = z_hi * 2 + z_lo), core: 2. Of those that a mesh axis runs over, the one named last changes fastest.
Arguments:
- tokens_in: bfloat16 [32, 512, 1024], P('dp'), may hold values from -6 to 6
- cotangent: bfloat16 [32, 512, 1024], P('dp'), may hold values from -6 to 6
- segment_ids: int32 [32, 512], P('dp'), may hold values from 0 to 3, never falling along the last dimension, each value on 1 to 256 neighbouring positions
- in_weight: float32 [3, 1024, 1024], P(None, 'dp', 'tensor'), may hold values from -0.1875 to 0.1875
- out_weight: float32 [1024, 1024], P('tensor', 'dp'), may hold values from -0.1875 to 0.1875
- gate_up_weight: float32 [2, 1024, 4608], P(None, 'dp', 'tensor'), may hold values from -0.1875 to 0.1875
- down_weight: float32 [4608, 1024], P('tensor', 'dp'), may hold values from -0.09375 to 0.09375
- conv_weight: float32 [3, 1024], P(None, 'tensor'), may hold values from -3 to 3
- norm_gains: float32 [2, 1024], P(None, 'dp'), may hold values from 0.5 to 1.5
- in_first: float32 [3, 1024, 1024], P(None, 'dp', 'tensor'), may hold values from -84.48 to 84.48
- in_second: float32 [3, 1024, 1024], P(None, 'dp', 'tensor'), may hold values from 861.7984 to 3440.64
- out_first: float32 [1024, 1024], P('tensor', 'dp'), may hold values from -107.52 to 107.52
- out_second: float32 [1024, 1024], P('tensor', 'dp'), may hold values from 1458.176 to 5832.704
- gate_up_first: float32 [2, 1024, 4608], P(None, 'dp', 'tensor'), may hold values from -25.6 to 25.6
- gate_up_second: float32 [2, 1024, 4608], P(None, 'dp', 'tensor'), may hold values from 77.0048 to 311.296
- down_first: float32 [4608, 1024], P('tensor', 'dp'), may hold values from -42.24 to 42.24
- down_second: float32 [4608, 1024], P('tensor', 'dp'), may hold values from 212.992 to 851.968
- conv_first: float32 [3, 1024], P(None, 'tensor'), may hold values from -107.52 to 107.52
- conv_second: float32 [3, 1024], P(None, 'tensor'), may hold values from 1458.176 to 5832.704
- gains_first: float32 [2, 1024], P(None, 'dp'), may hold values from -84.48 to 84.48
- gains_second: float32 [2, 1024], P(None, 'dp'), may hold values from 861.7984 to 3440.64
Outputs:
- block_out: float32 [32, 512, 1024], P('dp')
- tokens_grad: float32 [32, 512, 1024], P('dp')
- in_weight_new: float32 [3, 1024, 1024], P(None, 'dp', 'tensor')
- in_first_new: float32 [3, 1024, 1024], P(None, 'dp', 'tensor')
- in_second_new: float32 [3, 1024, 1024], P(None, 'dp', 'tensor')
- out_weight_new: float32 [1024, 1024], P('tensor', 'dp')
- out_first_new: float32 [1024, 1024], P('tensor', 'dp')
- out_second_new: float32 [1024, 1024], P('tensor', 'dp')
- gate_up_weight_new: float32 [2, 1024, 4608], P(None, 'dp', 'tensor')
- gate_up_first_new: float32 [2, 1024, 4608], P(None, 'dp', 'tensor')
- gate_up_second_new: float32 [2, 1024, 4608], P(None, 'dp', 'tensor')
- down_weight_new: float32 [4608, 1024], P('tensor', 'dp')
- down_first_new: float32 [4608, 1024], P('tensor', 'dp')
- down_second_new: float32 [4608, 1024], P('tensor', 'dp')
- conv_weight_new: float32 [3, 1024], P(None, 'tensor')
- conv_first_new: float32 [3, 1024], P(None, 'tensor')
- conv_second_new: float32 [3, 1024], P(None, 'tensor')
- norm_gains_new: float32 [2, 1024], P(None, 'dp')
- gains_first_new: float32 [2, 1024], P(None, 'dp')
- gains_second_new: float32 [2, 1024], P(None, 'dp')
Inputs may be any that keep to these rules, and one draw needn't show every extreme that they name: `segment_ids`: segment ids never fall along a sequence; each document has 1 to 256 tokens and one has exactly 256.
All inputs are finite; a program needn't handle non-finite values.
Results may differ from a plain program's by a relative error of at most 0.012.
The roundings to bfloat16 on the way count: a program that leaves them out, or rounds other values in their place, can miss the bound.
Values may be sent and summed in bfloat16 or wider, within the bound.
No kernel may reach another device: no remote copies, remote signals or barrier semaphores. Data moves between devices by JAX's collectives and lax.ppermute only.
A program may use at most 128 MiB of HBM per device.

v0:
```python
import jax
import jax.numpy as jnp
from jax import lax
from jax.sharding import PartitionSpec as P

D = 1024
FF = 4608
ADAM_STEP = 10


epsilon_norm = 1e-05
epsilon_adam = 1e-08
beta_one = 0.9
beta_two = 0.95


def rms_gain(values, gain_row):
    return (
        values
        * lax.rsqrt(jnp.mean(values * values, axis=-1, keepdims=True) + epsilon_norm)
        * gain_row
    )


def adam_step(master, gradient, first, second, step_rate, decay_rate):
    first_new = beta_one * first + (1.0 - beta_one) * gradient
    second_new = beta_two * second + (1.0 - beta_two) * gradient * gradient
    first_hat = first_new / (1.0 - beta_one**ADAM_STEP)
    second_hat = second_new / (1.0 - beta_two**ADAM_STEP)
    master_new = master - step_rate * (
        first_hat / (jnp.sqrt(second_hat) + epsilon_adam) + decay_rate * master
    )
    return (master_new, first_new, second_new)


def shards(
    tokens_in,
    cotangent,
    segment_ids,
    in_weight,
    out_weight,
    gate_up_weight,
    down_weight,
    conv_weight,
    norm_gains,
    in_first,
    in_second,
    out_first,
    out_second,
    gate_up_first,
    gate_up_second,
    down_first,
    down_second,
    conv_first,
    conv_second,
    gains_first,
    gains_second,
):
    rows, length, width = tokens_in.shape
    count = rows * length
    in_full, out_full, gate_up_full, down_full, gains_full = (
        lax.all_gather(in_weight.astype(jnp.bfloat16), "dp", axis=1, tiled=True),
        lax.all_gather(out_weight.astype(jnp.bfloat16), "dp", axis=1, tiled=True),
        lax.all_gather(gate_up_weight.astype(jnp.bfloat16), "dp", axis=1, tiled=True),
        lax.all_gather(down_weight.astype(jnp.bfloat16), "dp", axis=1, tiled=True),
        lax.all_gather(norm_gains.astype(jnp.bfloat16), "dp", axis=1, tiled=True),
    )
    gains_value = gains_full.astype(jnp.float32)
    flat = tokens_in.reshape(count, width).astype(jnp.float32)
    seg_flat = segment_ids.reshape(count)
    place = lax.iota(jnp.int32, count) % length
    mask_one = ((place >= 1) & (seg_flat == jnp.roll(seg_flat, 1)))[:, None]
    mask_two = ((place >= 2) & (seg_flat == jnp.roll(seg_flat, 2)))[:, None]

    def mixer_local(projected, taps):
        product = projected[0] * projected[2]
        conv_sum = taps[0] * product + taps[1] * jnp.where(
            mask_one, jnp.roll(product, 1, axis=0), 0.0
        )
        conv_sum = conv_sum + taps[2] * jnp.where(mask_two, jnp.roll(product, 2, axis=0), 0.0)
        return projected[1] * conv_sum

    normed_one_f, norm_one_pull = jax.vjp(rms_gain, flat, gains_value[0])
    normed_one = normed_one_f.astype(jnp.bfloat16)
    projected = jnp.einsum("td,kdc->ktc", normed_one, in_full, preferred_element_type=jnp.float32)
    gated_f, mixer_pull = jax.vjp(mixer_local, projected, conv_weight)
    gated = gated_f.astype(jnp.bfloat16)
    branch = lax.psum(jnp.dot(gated, out_full, preferred_element_type=jnp.float32), "tensor")
    middle = flat + branch
    normed_two_f, norm_two_pull = jax.vjp(rms_gain, middle, gains_value[1])
    normed_two = normed_two_f.astype(jnp.bfloat16)
    gate_up = jnp.einsum(
        "td,kdf->ktf", normed_two, gate_up_full, preferred_element_type=jnp.float32
    )

    def swish_gate(gate_part, up_part):
        return jax.nn.silu(gate_part) * up_part

    hidden_f, swish_pull = jax.vjp(swish_gate, gate_up[0], gate_up[1])
    hidden = hidden_f.astype(jnp.bfloat16)
    ffn_out = lax.psum(
        jnp.dot(hidden, down_full, preferred_element_type=jnp.float32).astype(jnp.bfloat16),
        "tensor",
    ).astype(jnp.float32)
    result = middle + ffn_out
    back_out = cotangent.reshape(count, width)
    grad_down = jnp.einsum("tf,td->fd", hidden, back_out, preferred_element_type=jnp.float32)
    back_hidden = jnp.einsum("td,fd->tf", back_out, down_full, preferred_element_type=jnp.float32)
    back_gate, back_up = swish_pull(back_hidden)
    back_gate_up = jnp.stack([back_gate, back_up]).astype(jnp.bfloat16)
    grad_gate_up = jnp.einsum(
        "td,ktf->kdf", normed_two, back_gate_up, preferred_element_type=jnp.float32
    )
    back_normed_two = lax.psum(
        jnp.einsum("ktf,kdf->td", back_gate_up, gate_up_full, preferred_element_type=jnp.float32),
        "tensor",
    )
    back_middle_norm, grad_gain_two = norm_two_pull(back_normed_two)
    back_middle = back_out.astype(jnp.float32) + back_middle_norm
    back_branch = back_middle.astype(jnp.bfloat16)
    grad_out = jnp.einsum("tc,td->cd", gated, back_branch, preferred_element_type=jnp.float32)
    back_gated = jnp.einsum("td,cd->tc", back_branch, out_full, preferred_element_type=jnp.float32)
    back_projected_f, grad_conv = mixer_pull(back_gated)
    back_projected = back_projected_f.astype(jnp.bfloat16)
    grad_in = jnp.einsum(
        "td,ktc->kdc", normed_one, back_projected, preferred_element_type=jnp.float32
    )
    back_normed_one = lax.psum(
        jnp.einsum(
            "ktc,kdc->td", back_projected, in_full, preferred_element_type=jnp.float32
        ).astype(jnp.bfloat16),
        "tensor",
    ).astype(jnp.float32)
    back_tokens_norm, grad_gain_one = norm_one_pull(back_normed_one)
    back_tokens = back_middle + back_tokens_norm
    grad_gains = jnp.stack([grad_gain_one, grad_gain_two])
    red_in, red_out, red_gate_up, red_down, red_gains = (
        lax.psum_scatter(grad_in, "dp", scatter_dimension=1, tiled=True),
        lax.psum_scatter(grad_out, "dp", scatter_dimension=1, tiled=True),
        lax.psum_scatter(grad_gate_up, "dp", scatter_dimension=1, tiled=True),
        lax.psum_scatter(grad_down, "dp", scatter_dimension=1, tiled=True),
        lax.psum_scatter(grad_gains, "dp", scatter_dimension=1, tiled=True),
    )
    conv_total = lax.psum(grad_conv, "dp")
    rate_wide = 0.8 / D**0.5
    rate_down = 0.8 / FF**0.5
    in_new = adam_step(in_weight, red_in, in_first, in_second, rate_wide, 0.1)
    out_new = adam_step(out_weight, red_out, out_first, out_second, rate_wide, 0.1)
    gate_up_new = adam_step(
        gate_up_weight, red_gate_up, gate_up_first, gate_up_second, rate_wide, 0.1
    )
    down_new = adam_step(down_weight, red_down, down_first, down_second, rate_down, 0.1)
    conv_new = adam_step(conv_weight, conv_total, conv_first, conv_second, 1.0, 0.0)
    gains_new = adam_step(norm_gains, red_gains, gains_first, gains_second, 0.3, 0.0)
    return (
        result.reshape(rows, length, width),
        back_tokens.reshape(rows, length, width),
        in_new[0],
        in_new[1],
        in_new[2],
        out_new[0],
        out_new[1],
        out_new[2],
        gate_up_new[0],
        gate_up_new[1],
        gate_up_new[2],
        down_new[0],
        down_new[1],
        down_new[2],
        conv_new[0],
        conv_new[1],
        conv_new[2],
        gains_new[0],
        gains_new[1],
        gains_new[2],
    )


def solution(mesh):
    in_specs = (
        P("dp", None, None),
        P("dp", None, None),
        P("dp", None),
        P(None, "dp", "tensor"),
        P("tensor", "dp"),
        P(None, "dp", "tensor"),
        P("tensor", "dp"),
        P(None, "tensor"),
        P(None, "dp"),
        P(None, "dp", "tensor"),
        P(None, "dp", "tensor"),
        P("tensor", "dp"),
        P("tensor", "dp"),
        P(None, "dp", "tensor"),
        P(None, "dp", "tensor"),
        P("tensor", "dp"),
        P("tensor", "dp"),
        P(None, "tensor"),
        P(None, "tensor"),
        P(None, "dp"),
        P(None, "dp"),
    )
    out_specs = (
        P("dp", None, None),
        P("dp", None, None),
        P(None, "dp", "tensor"),
        P(None, "dp", "tensor"),
        P(None, "dp", "tensor"),
        P("tensor", "dp"),
        P("tensor", "dp"),
        P("tensor", "dp"),
        P(None, "dp", "tensor"),
        P(None, "dp", "tensor"),
        P(None, "dp", "tensor"),
        P("tensor", "dp"),
        P("tensor", "dp"),
        P("tensor", "dp"),
        P(None, "tensor"),
        P(None, "tensor"),
        P(None, "tensor"),
        P(None, "dp"),
        P(None, "dp"),
        P(None, "dp"),
    )
    return jax.shard_map(shards, mesh=mesh, in_specs=in_specs, out_specs=out_specs, check_vma=False)
```

profile of v0, /device:TPU:0, one launch (start us, length us, event | category | flops | bytes accessed | tf_op | source)
XLA Modules:
  0.0 1573.5 jit_solution(7697891751018365114)
XLA Ops:
  10.8 81.5 %all-gather = bf16[32,32,2]{1,2,0:T(2,128)(2,1)S(1)} all-gather(bf16[1,32,2]{1,2,0:T(2,128)(2,1)S(1)} %convert_bitcast_fusion), channel_id=1, replica_groups=mesh['dp'=32,'tensor'=4] {'dp'}, dimensions={0}, use_global_device_ids=true | all-gather | bytes 4224 | tf_op jit(solution)/shard_map/all_gather | solution.py:66
  97.8 78.4 %all_gather.17 = bf16[256,1024]{0,1:T(8,128)(2,1)S(1)} all-gather(bf16[256,32]{0,1:T(8,128)(2,1)S(1)} %convert_element_type.70), channel_id=1, replica_groups=mesh['dp'=32,'tensor'=4] {'dp'}, dimensions={1}, use_global_device_ids=true | all-gather | bytes 540672 | tf_op jit(solution)/shard_map/all_gather | solution.py:63
  176.2 2.8 convolution_bitcast_fusion.4
  182.9 56.3 %all-reduce.19.cloned.1.call-done = f32[512,1024]{1,0:T(8,128)} async-done(((f32[512,1024]{1,0:T(8,128)}), f32[512,1024]{1,0:T(8,128)}) %all-reduce.19.cloned.1.call-update) | async-done | bytes 2097168 | tf_op jit(solution)/shard_map/psum | solution.py:88
  242.0 157.1 %all-gather.7.cloned.1.call-done = bf16[2,1024,1152]{2,1,0:T(8,128)(2,1)} async-done(((bf16[2,32,1152]{2,1,0:T(8,128)(2,1)}), bf16[2,1024,1152]{2,1,0:T(8,128)(2,1)}) %all-gather.7.cloned.1.call-update) | async-done | bytes 4718608 | tf_op jit(solution)/shard_map/all_gather | solution.py:64
  399.1 5.1 convolution_bitcast_fusion.1
  406.4 4.0 fusion.18
  410.4 169.7 %reduce-scatter.8.cloned.1.call-done = f32[1152,32]{0,1:T(8,128)} async-done(((f32[1152,1024]{0,1:T(8,128)}), f32[1152,32]{0,1:T(8,128)}) %reduce-scatter.8.cloned.1.call-update) | async-done | bytes 147472 | tf_op jit(solution)/shard_map/reduce_scatter | solution.py:141
  582.1 150.0 %all-gather.9.cloned.1.call-done = bf16[1152,1024]{0,1:T(8,128)(2,1)} async-done(((bf16[1152,32]{0,1:T(8,128)(2,1)}), bf16[1152,1024]{0,1:T(8,128)(2,1)}) %all-gather.9.cloned.1.call-update) | async-done | bytes 2359312 | tf_op jit(solution)/shard_map/all_gather | solution.py:65
  732.1 5.4 fusion.20
  738.9 6.3 convolution_bitcast_fusion.3
  745.5 5.7 convolution_convert_fusion
  751.1 52.9 %all-reduce.21.cloned.1.call-done = f32[512,1024]{1,0:T(8,128)} async-done(((f32[512,1024]{1,0:T(8,128)}), f32[512,1024]{1,0:T(8,128)}) %all-reduce.21.cloned.1.call-update) | async-done | bytes 2097168 | tf_op jit(solution)/shard_map/psum | solution.py:114
  813.7 3.1 fusion.26
  816.9 6.9 convolution_bitcast_fusion
  823.7 15.0 copy.100
  838.7 33.4 %all-reduce.25.cloned.1.call-done = (bf16[512,1024]{1,0:T(8,128)(2,1)}, bf16[512,1024]{1,0:T(8,128)(2,1)}) async-done(((bf16[512,1024]{1,0:T(8,128)(2,1)}, bf16[512,1024]{1,0:T(8,128)(2,1)}), (bf16[512,1024]{1,0:T(8,128)(2,1)}, bf16[512,1024]{1,0:T(8,128)(2,1)})) %all-reduce.25.cloned.1.call-update) | async-done | bytes 2097168 | tf_op jit(solution)/shard_map/psum | solution.py:101
  875.4 4.2 convolution_bitcast_fusion.2
  879.7 5.0 copy.95
  886.6 81.9 %psum.39 = f32[3,256]{1,0:T(4,128)S(1)} all-reduce(f32[3,256]{1,0:T(4,128)S(1)} %pad_add_fusion), channel_id=1, replica_groups=mesh['dp'=32,'tensor'=4] {'dp'}, use_global_device_ids=true, to_apply=%region_15.16 | all-reduce | flops 768 | bytes 6144 | tf_op jit(solution)/shard_map/psum | solution.py:144
  969.1 65.9 %reduce-scatter.6.cloned.1.call-done = f32[256,32]{0,1:T(8,128)} async-done(((f32[256,1024]{0,1:T(8,128)}), f32[256,32]{0,1:T(8,128)}) %reduce-scatter.6.cloned.1.call-update) | async-done | bytes 32784 | tf_op jit(solution)/shard_map/reduce_scatter | solution.py:139
  1036.4 5.3 fusion.13
  1041.7 151.5 %reduce-scatter.10.cloned.1.call-done = f32[32,2]{1,0:T(8,128)} async-done(((f32[1024,2]{1,0:T(8,128)}), f32[32,2]{1,0:T(8,128)}) %reduce-scatter.10.cloned.1.call-update) | async-done | bytes 272
  1195.3 365.6 %all-reduce.23.cloned.1.call-done = (f32[3,1024,256]{2,0,1:T(4,128)}, f32[2,1024,1152]{2,0,1:T(2,128)}) async-done(((f32[3,1024,256]{2,0,1:T(4,128)}, f32[2,1024,1152]{2,0,1:T(2,128)}), (f32[3,1024,256]{2,0,1:T(4,128)}, f32[2,1024,1152]{2,0,1:T(2,128)})) %all-reduce.23.cloned.1.call-update) | async-done | bytes 12582928
  (174 shorter events, 45.2 us)
Async XLA Ops:
  7.2 169.0 %all-gather.5.cloned.1.call-start = ((), (), s32[]{:S(2)}) async-start(), calls=%async_computation.3 | async-start | bytes 1622016 | tf_op jit(solution)/shard_map/all_gather | solution.py:62
  8.8 230.4 %all-reduce.19.cloned.1.call-start = ((), (), s32[]{:S(2)}) async-start(), calls=%async_computation.4 | async-start | bytes 4194304 | tf_op jit(solution)/shard_map/psum | solution.py:88
  96.8 82.2 %copy-start.45 = (pred[512]{0:T(512)(128)(4,1)}, pred[512]{0:T(512)(128)(4,1)S(1)}, u32[]{:S(2)}) copy-start(pred[512]{0:T(512)(128)(4,1)S(1)} %get-tuple-element.128) | copy-start | bytes 1540
  97.7 301.3 %copy-start.18 = (f32[1,1024]{1,0:T(1,128)}, f32[1,1024]{1,0:T(1,128)S(1)}, u32[]{:S(2)}) copy-start(f32[1,1024]{1,0:T(1,128)S(1)} %get-tuple-element.122) | copy-start | bytes 12292
  182.1 217.0 %all-gather.7.cloned.1.call-start = ((), (), s32[]{:S(2)}) async-start(), calls=%async_computation.5 | async-start | bytes 4866048 | tf_op jit(solution)/shard_map/all_gather | solution.py:64
  182.9 397.2 %reduce-scatter.8.cloned.1.call-start = ((), (), s32[]{:S(2)}) async-start(), calls=%async_computation.9 | async-start | bytes 4866048 | tf_op jit(solution)/shard_map/reduce_scatter | solution.py:141
  242.0 162.2 %copy-start.24 = (f32[512]{0:T(512)}, f32[512]{0:T(512)S(1)}, u32[]{:S(2)}) copy-start(f32[512]{0:T(512)S(1)} %fusion.49) | copy-start | bytes 6148
  410.3 169.8 %copy-start.16 = (f32[1152,32]{0,1:T(8,128)S(1)}, f32[1152,32]{0,1:T(8,128)}, u32[]{:S(2)}) copy-start(f32[1152,32]{0,1:T(8,128)} %param.27) | copy-start | bytes 442372
  410.3 321.7 %all-gather.9.cloned.1.call-start = ((), (), s32[]{:S(2)}) async-start(), calls=%async_computation.6 | async-start | bytes 2433024 | tf_op jit(solution)/shard_map/all_gather | solution.py:65
  582.0 222.0 %all-reduce.21.cloned.1.call-start = ((), (), s32[]{:S(2)}) async-start(), calls=%async_computation.7 | async-start | bytes 4194304 | tf_op jit(solution)/shard_map/psum | solution.py:114
  745.3 126.9 %all-reduce.25.cloned.1.call-start = ((), (), s32[]{:S(2)}) async-start(), calls=%async_computation.12 | async-start | bytes 4194304 | tf_op jit(solution)/shard_map/psum | solution.py:101
  813.6 221.4 %reduce-scatter.6.cloned.1.call-start = ((), (), s32[]{:S(2)}) async-start(), calls=%async_computation.8 | async-start | bytes 1081344 | tf_op jit(solution)/shard_map/reduce_scatter | solution.py:139
  816.8 376.4 %reduce-scatter.10.cloned.1.call-start = ((), (), s32[]{:S(2)}) async-start(), calls=%async_computation.10 | async-start | bytes 540672
  875.4 685.5 %all-reduce.23.cloned.1.call-start = ((), (), s32[]{:S(2)}) async-start(), calls=%async_computation.11 | async-start | bytes 27262976
  884.7 83.8 %copy-start.34 = (f32[3,256]{1,0:T(4,128)S(1)}, f32[3,256]{1,0:T(4,128)}, u32[]{:S(2)}) copy-start(f32[3,256]{1,0:T(4,128)} %param.28) | copy-start | bytes 9220
  884.7 83.8 %copy-start.47 = (f32[3,256]{1,0:T(4,128)S(1)}, f32[3,256]{1,0:T(4,128)}, u32[]{:S(2)}) copy-start(f32[3,256]{1,0:T(4,128)} %param.38) | copy-start | bytes 9220
  884.7 83.8 %copy-start.48 = (f32[3,256]{1,0:T(4,128)S(1)}, f32[3,256]{1,0:T(4,128)}, u32[]{:S(2)}) copy-start(f32[3,256]{1,0:T(4,128)} %param.39) | copy-start | bytes 9220
  884.7 84.4 %copy-start.27 = (f32[512]{0:T(512)S(1)}, f32[512]{0:T(512)}, u32[]{:S(2)}) copy-start(f32[512]{0:T(512)} %copy-done.26) | copy-start | bytes 6148
  884.7 150.3 %copy-start.17 = (f32[256,32]{0,1:T(8,128)S(1)}, f32[256,32]{0,1:T(8,128)}, u32[]{:S(2)}) copy-start(f32[256,32]{0,1:T(8,128)} %param.25) | copy-start | bytes 98308
  884.7 150.3 %copy-start.22 = (f32[256,32]{0,1:T(8,128)S(1)}, f32[256,32]{0,1:T(8,128)}, u32[]{:S(2)}) copy-start(f32[256,32]{0,1:T(8,128)} %param.32) | copy-start | bytes 98308
  884.7 150.3 %copy-start.23 = (f32[256,32]{0,1:T(8,128)S(1)}, f32[256,32]{0,1:T(8,128)}, u32[]{:S(2)}) copy-start(f32[256,32]{0,1:T(8,128)} %param.33) | copy-start | bytes 98308
  1036.4 157.6 %copy-start.49 = (f32[2,32]{1,0:T(2,128)S(1)}, f32[2,32]{1,0:T(2,128)}, u32[]{:S(2)}) copy-start(f32[2,32]{1,0:T(2,128)} %param.29) | copy-start | bytes 772
  1036.4 526.4 %copy-start.15 = (f32[3,32,256]{2,1,0:T(8,128)S(1)}, f32[3,32,256]{2,1,0:T(8,128)}, u32[]{:S(2)}) copy-start(f32[3,32,256]{2,1,0:T(8,128)} %param.24) | copy-start | bytes 294916
  1036.4 528.1 %copy-start.7 = (f32[2,32,1152]{2,1,0:T(8,128)S(1)}, f32[2,32,1152]{2,1,0:T(8,128)}, u32[]{:S(2)}) copy-start(f32[2,32,1152]{2,1,0:T(8,128)} %param.26) | copy-start | bytes 884740
  (39 other events, 856.4 us)
Sparse Core Ops, SparseCore 0:
  10.2 154.6 all-gather.4
  182.2 56.9 all-reduce.18
  241.5 157.4 all-gather.6
  410.5 169.5 reduce-scatter.7
  582.3 149.7 all-gather.8
  745.3 58.6 all-reduce.20
  813.7 58.3 all-reduce.24
  874.6 160.3 reduce-scatter.5
  1037.4 155.7 reduce-scatter.9
  1195.8 364.9 all-reduce.22
where the time goes:
time: 1570 us
  waiting for transfers between devices  1200 us (76%)
  blocking collectives  242 us (15%)
  matrix products  48.1 us (3%)
  local copies, waits for them, and re-layouts  35.1 us (2%)
  other arithmetic  29.9 us (2%)
    unnamed x12, waiting for transfers between devices  517 us
    reduce_scatter x1, waiting for transfers between devices, shards(): lax.psum_scatter(grad_down, 'dp', scatter_dimension=1, tiled=True)  170 us
    all_gather x1, waiting for transfers between devices, shards(): lax.all_gather(gate_up_weight.astype(jnp.bfloat16), 'dp', axis=1, tiled=T...  157 us
    all_gather x1, waiting for transfers between devices, shards(): lax.all_gather(down_weight.astype(jnp.bfloat16), 'dp', axis=1, tiled=True)  150 us
    psum x1, blocking collectives, shards(): conv_total = lax.psum(grad_conv, 'dp')  81.9 us
    all_gather x1, blocking collectives, shards(): lax.all_gather(norm_gains.astype(jnp.bfloat16), 'dp', axis=1, tiled=True)  81.5 us
    all_gather x1, blocking collectives, shards(): lax.all_gather(out_weight.astype(jnp.bfloat16), 'dp', axis=1, tiled=True)  78.4 us
    reduce_scatter x1, waiting for transfers between devices, shards(): lax.psum_scatter(grad_out, 'dp', scatter_dimension=1, tiled=True)  65.9 us
  transfers between devices with their start and end apart: 10, of which 9 were waited for; matrix products, arithmetic and copies ran while one was open for 4% of the time, Pallas kernels for 0%

commit v1 on v0

--- a/solution.py
+++ b/solution.py
@@ -6,6 +6,9 @@
 D = 1024
 FF = 4608
 ADAM_STEP = 10
+N_DP = 32
+CORE_PAIRS = [(0, 1), (1, 0), (2, 3), (3, 2)]
+HIGH_PAIRS = [(0, 2), (2, 0), (1, 3), (3, 1)]
 
 
 epsilon_norm = 1e-05
@@ -31,6 +34,31 @@
         first_hat / (jnp.sqrt(second_hat) + epsilon_adam) + decay_rate * master
     )
     return (master_new, first_new, second_new)
+
+
+def spread(block):
+    copies = jnp.broadcast_to(block[None], (N_DP,) + block.shape)
+    return lax.all_to_all(copies, "dp", 0, 0, tiled=True).reshape(-1, block.shape[1])
+
+
+def collect(grad):
+    parts = grad.astype(jnp.bfloat16).reshape(N_DP, -1, grad.shape[1])
+    parts = lax.all_to_all(parts, "dp", 0, 0, tiled=True)
+    return jnp.sum(parts.astype(jnp.float32), axis=0)
+
+
+def tensor_sum(part):
+    core = lax.axis_index("tensor") % 2
+    half = part.shape[0] // 2
+    own = lax.dynamic_slice_in_dim(part, core * half, half, 0)
+    other = lax.dynamic_slice_in_dim(part, (1 - core) * half, half, 0)
+    pair = own + lax.ppermute(other, "tensor", CORE_PAIRS)
+    pair = pair.astype(jnp.bfloat16)
+    far = lax.ppermute(pair, "tensor", HIGH_PAIRS)
+    total = pair.astype(jnp.float32) + far.astype(jnp.float32)
+    twin = lax.ppermute(total, "tensor", CORE_PAIRS)
+    first = core == 0
+    return jnp.concatenate([jnp.where(first, total, twin), jnp.where(first, twin, total)], axis=0)
 
 
 def shards(
@@ -58,14 +86,26 @@
 ):
     rows, length, width = tokens_in.shape
     count = rows * length
-    in_full, out_full, gate_up_full, down_full, gains_full = (
-        lax.all_gather(in_weight.astype(jnp.bfloat16), "dp", axis=1, tiled=True),
-        lax.all_gather(out_weight.astype(jnp.bfloat16), "dp", axis=1, tiled=True),
-        lax.all_gather(gate_up_weight.astype(jnp.bfloat16), "dp", axis=1, tiled=True),
-        lax.all_gather(down_weight.astype(jnp.bfloat16), "dp", axis=1, tiled=True),
-        lax.all_gather(norm_gains.astype(jnp.bfloat16), "dp", axis=1, tiled=True),
-    )
-    gains_value = gains_full.astype(jnp.float32)
+    taps_n, channels = conv_weight.shape
+    units = gate_up_weight.shape[2]
+    gains_full = lax.all_to_all(
+        jnp.broadcast_to(norm_gains[None], (N_DP,) + norm_gains.shape), "dp", 0, 0, tiled=True
+    )
+    low_mix = jnp.concatenate(
+        [in_weight[0], in_weight[1], in_weight[2], out_weight.T], axis=1
+    ).astype(jnp.bfloat16)
+    low_gate_up = jnp.concatenate([gate_up_weight[0], gate_up_weight[1]], axis=1).astype(
+        jnp.bfloat16
+    )
+    low_down = down_weight.T.astype(jnp.bfloat16)
+    mix_full = spread(low_mix)
+    gate_up_full = spread(low_gate_up)
+    down_full = spread(low_down)
+    in_full = mix_full[:, : 3 * channels]
+    out_full = mix_full[:, 3 * channels :]
+    gains_value = (
+        gains_full.transpose(1, 0, 2).reshape(2, width).astype(jnp.bfloat16).astype(jnp.float32)
+    )
     flat = tokens_in.reshape(count, width).astype(jnp.float32)
     seg_flat = segment_ids.reshape(count)
     place = lax.iota(jnp.int32, count) % length
@@ -73,75 +113,67 @@
     mask_two = ((place >= 2) & (seg_flat == jnp.roll(seg_flat, 2)))[:, None]
 
     def mixer_local(projected, taps):
-        product = projected[0] * projected[2]
+        b_part = projected[:, :channels]
+        c_part = projected[:, channels : 2 * channels]
+        product = b_part * projected[:, 2 * channels :]
         conv_sum = taps[0] * product + taps[1] * jnp.where(
             mask_one, jnp.roll(product, 1, axis=0), 0.0
         )
         conv_sum = conv_sum + taps[2] * jnp.where(mask_two, jnp.roll(product, 2, axis=0), 0.0)
-        return projected[1] * conv_sum
+        return c_part * conv_sum
+
+    def product_of(spec, left, right):
+        return jnp.einsum(spec, left, right, preferred_element_type=jnp.float32)
 
     normed_one_f, norm_one_pull = jax.vjp(rms_gain, flat, gains_value[0])
     normed_one = normed_one_f.astype(jnp.bfloat16)
-    projected = jnp.einsum("td,kdc->ktc", normed_one, in_full, preferred_element_type=jnp.float32)
+    projected = product_of("td,dc->tc", normed_one, in_full)
     gated_f, mixer_pull = jax.vjp(mixer_local, projected, conv_weight)
     gated = gated_f.astype(jnp.bfloat16)
-    branch = lax.psum(jnp.dot(gated, out_full, preferred_element_type=jnp.float32), "tensor")
-    middle = flat + branch
+    middle = flat + tensor_sum(product_of("tc,dc->td", gated, out_full))
     normed_two_f, norm_two_pull = jax.vjp(rms_gain, middle, gains_value[1])
     normed_two = normed_two_f.astype(jnp.bfloat16)
-    gate_up = jnp.einsum(
-        "td,kdf->ktf", normed_two, gate_up_full, preferred_element_type=jnp.float32
-    )
-
-    def swish_gate(gate_part, up_part):
-        return jax.nn.silu(gate_part) * up_part
-
-    hidden_f, swish_pull = jax.vjp(swish_gate, gate_up[0], gate_up[1])
+    gate_up = product_of("td,df->tf", normed_two, gate_up_full)
+
+    def swish_gate(both):
+        return jax.nn.silu(both[:, :units]) * both[:, units:]
+
+    hidden_f, swish_pull = jax.vjp(swish_gate, gate_up)
     hidden = hidden_f.astype(jnp.bfloat16)
-    ffn_out = lax.psum(
-        jnp.dot(hidden, down_full, preferred_element_type=jnp.float32).astype(jnp.bfloat16),
-        "tensor",
-    ).astype(jnp.float32)
-    result = middle + ffn_out
     back_out = cotangent.reshape(count, width)
-    grad_down = jnp.einsum("tf,td->fd", hidden, back_out, preferred_element_type=jnp.float32)
-    back_hidden = jnp.einsum("td,fd->tf", back_out, down_full, preferred_element_type=jnp.float32)
-    back_gate, back_up = swish_pull(back_hidden)
-    back_gate_up = jnp.stack([back_gate, back_up]).astype(jnp.bfloat16)
-    grad_gate_up = jnp.einsum(
-        "td,ktf->kdf", normed_two, back_gate_up, preferred_element_type=jnp.float32
-    )
-    back_normed_two = lax.psum(
-        jnp.einsum("ktf,kdf->td", back_gate_up, gate_up_full, preferred_element_type=jnp.float32),
-        "tensor",
-    )
+    back_hidden = product_of("td,df->tf", back_out, down_full)
+    back_gate_up = swish_pull(back_hidden)[0].astype(jnp.bfloat16)
+    back_normed_two = tensor_sum(product_of("tf,df->td", back_gate_up, gate_up_full))
+    red_down = collect(product_of("td,tf->df", back_out, hidden))
+    red_gate_up = collect(product_of("td,tf->df", normed_two, back_gate_up))
+    result = middle + tensor_sum(product_of("tf,df->td", hidden, down_full))
     back_middle_norm, grad_gain_two = norm_two_pull(back_normed_two)
     back_middle = back_out.astype(jnp.float32) + back_middle_norm
     back_branch = back_middle.astype(jnp.bfloat16)
-    grad_out = jnp.einsum("tc,td->cd", gated, back_branch, preferred_element_type=jnp.float32)
-    back_gated = jnp.einsum("td,cd->tc", back_branch, out_full, preferred_element_type=jnp.float32)
+    grad_out = product_of("td,tc->dc", back_branch, gated)
+    back_gated = product_of("td,dc->tc", back_branch, out_full)
     back_projected_f, grad_conv = mixer_pull(back_gated)
     back_projected = back_projected_f.astype(jnp.bfloat16)
-    grad_in = jnp.einsum(
-        "td,ktc->kdc", normed_one, back_projected, preferred_element_type=jnp.float32
-    )
-    back_normed_one = lax.psum(
-        jnp.einsum(
-            "ktc,kdc->td", back_projected, in_full, preferred_element_type=jnp.float32
-        ).astype(jnp.bfloat16),
-        "tensor",
-    ).astype(jnp.float32)
+    grad_in = product_of("td,tc->dc", normed_one, back_projected)
+    red_mix = collect(jnp.concatenate([grad_in, grad_out], axis=1))
+    back_normed_one = tensor_sum(product_of("tc,dc->td", back_projected, in_full))
     back_tokens_norm, grad_gain_one = norm_one_pull(back_normed_one)
     back_tokens = back_middle + back_tokens_norm
-    grad_gains = jnp.stack([grad_gain_one, grad_gain_two])
-    red_in, red_out, red_gate_up, red_down, red_gains = (
-        lax.psum_scatter(grad_in, "dp", scatter_dimension=1, tiled=True),
-        lax.psum_scatter(grad_out, "dp", scatter_dimension=1, tiled=True),
-        lax.psum_scatter(grad_gate_up, "dp", scatter_dimension=1, tiled=True),
-        lax.psum_scatter(grad_down, "dp", scatter_dimension=1, tiled=True),
-        lax.psum_scatter(grad_gains, "dp", scatter_dimension=1, tiled=True),
-    )
-    conv_total = lax.psum(grad_conv, "dp")
+    grad_gains = jnp.stack([grad_gain_one, grad_gain_two]).reshape(2, N_DP, -1).transpose(1, 0, 2)
+    grad_small = jnp.concatenate(
+        [
+            grad_gains.reshape(N_DP, -1),
+            jnp.broadcast_to(grad_conv.reshape(1, -1), (N_DP, grad_conv.size)),
+        ],
+        axis=1,
+    )
+    red_small = jnp.sum(lax.all_to_all(grad_small, "dp", 0, 0, tiled=True), axis=0)
+    red_gains = red_small[: norm_gains.size].reshape(norm_gains.shape)
+    conv_total = red_small[norm_gains.size :].reshape(conv_weight.shape)
+    red_in = red_mix[:, : 3 * channels].reshape(-1, 3, channels).transpose(1, 0, 2)
+    red_out = red_mix[:, 3 * channels :].T
+    red_gate_up = red_gate_up.reshape(-1, 2, units).transpose(1, 0, 2)
+    red_down = red_down.T
     rate_wide = 0.8 / D**0.5
     rate_down = 0.8 / FF**0.5
     in_new = adam_step(in_weight, red_in, in_first, in_second, rate_wide, 0.1)

time: 1570 us -> 405 us (0.26)
  waiting for transfers between devices: 1200 us -> 214 us
  blocking collectives: 242 us -> 0 us
  starting transfers between devices: 0.59 us -> 61.2 us
  other arithmetic: 29.9 us -> 48.7 us
    unnamed x12 -> x0, waiting for transfers between devices: 517 us -> none
    all_gather x3 -> x0, waiting for transfers between devices: 307 us -> none  [the longest x1 157 us: shards(): lax.all_gather(gate_up_weight.astype(jnp.bfloat16), 'dp', axis=1, tiled=T...]
    reduce_scatter x2 -> x0, waiting for transfers between devices: 236 us -> none  [the longest x1 170 us: shards(): lax.psum_scatter(grad_down, 'dp', scatter_dimension=1, tiled=True)]
    all_gather x2 -> x0, blocking collectives: 160 us -> none  [the longest x1 81.5 us: shards(): lax.all_gather(norm_gains.astype(jnp.bfloat16), 'dp', axis=1, tiled=True)]
    psum x3 -> x0, waiting for transfers between devices: 143 us -> none  [the longest x1 56.3 us: shards(): lax.psum(jnp.dot(gated, out_full, preferred_element_type=jnp.float32), 't...]
    ppermute x0 -> x12, waiting for transfers between devices: none -> 131 us  [the longest x4 126 us: tensor_sum(): far = lax.ppermute(pair, 'tensor', HIGH_PAIRS)]
    all_to_all x0 -> x8, waiting for transfers between devices: none -> 83.2 us  [the longest x3 43.9 us: spread(): lax.all_to_all(copies, 'dp', 0, 0, tiled=True).reshape(-1, block.shape[1])]
    psum x1 -> x0, blocking collectives: 81.9 us -> none  [shards(): conv_total = lax.psum(grad_conv, 'dp')]
  transfers between devices with their start and end apart: 10 -> 20, of which waited for: 9 -> 12; matrix products, arithmetic and copies ran while one was open for 4% -> 23% of each run, Pallas kernels for 0% -> 0%
where the time goes in v1:
time: 405 us; the launch traced here: 402 us
  waiting for transfers between devices  214 us (53%)
  starting transfers between devices  61.2 us (15%)
  other arithmetic  48.7 us (12%)
  matrix products  46.4 us (11%)
  local copies, waits for them, and re-layouts  29.9 us (7%)
    ppermute x4, waiting for transfers between devices, tensor_sum(): far = lax.ppermute(pair, 'tensor', HIGH_PAIRS)  126 us
    dot_general x12, matrix products, product_of(): return jnp.einsum(spec, left, right, preferred_element_type=jnp.float32)  46.4 us
    all_to_all x3, waiting for transfers between devices, spread(): lax.all_to_all(copies, 'dp', 0, 0, tiled=True).reshape(-1, block.shape[1])  43.9 us
    all_to_all x3, waiting for transfers between devices, collect(): parts = lax.all_to_all(parts, 'dp', 0, 0, tiled=True)  27.2 us
    all_to_all x3, starting transfers between devices, spread(): lax.all_to_all(copies, 'dp', 0, 0, tiled=True).reshape(-1, block.shape[1])  18.8 us
    all_to_all x3, starting transfers between devices, collect(): parts = lax.all_to_all(parts, 'dp', 0, 0, tiled=True)  17.1 us
    all_to_all x1, starting transfers between devices, shards(): lax.all_to_all(jnp.broadcast_to(norm_gains[None], (N_DP,) + norm_gains.sh...  8.76 us
    unnamed x180, local copies, waits for them, and re-layouts  8.61 us
  transfers between devices with their start and end apart: 20, of which 12 were waited for; matrix products, arithmetic and copies ran while one was open for 23% of the time, Pallas kernels for 0%

profile of v1, /device:TPU:0, one launch (start us, length us, event | category | flops | bytes accessed | tf_op | source)
XLA Modules:
  0.0 402.4 jit_solution(3202939413527709855)
XLA Ops:
  2.0 8.8 %all-to-all-start = ((bf16[32,2,32]{2,1,0:T(2,128)(2,1)}), bf16[32,2,32]{2,1,0:T(2,128)(2,1)S(1)}, u32[]{:S(2)}, u32[]{:S(2)}) async-start(bf16[32,2,32]{2,1,0:T(2,128)(2,1)} %broadcast_in_dim.67), calls=%async_computation | async-start | bytes 32768 | tf_op jit(solution)/shard_map/all_to_all | solution.py:91
  12.4 6.5 %all-to-all-done = bf16[32,2,32]{2,1,0:T(2,128)(2,1)S(1)} async-done(((bf16[32,2,32]{2,1,0:T(2,128)(2,1)}), bf16[32,2,32]{2,1,0:T(2,128)(2,1)S(1)}, u32[]{:S(2)}, u32[]{:S(2)}) %all-to-all-start) | async-done | bytes 4128 | tf_op jit(solution)/shard_map/all_to_all | solution.py:91
  20.5 4.1 %all-to-all-start.1 = ((bf16[32,32,1024]{2,1,0:T(8,128)(2,1)}), bf16[32,32,1024]{2,1,0:T(8,128)(2,1)S(1)}, u32[]{:S(2)}, u32[]{:S(2)}) async-start(bf16[32,32,1024]{2,1,0:T(8,128)(2,1)} %broadcast_in_dim.68), calls=%async_computation.1 | async-start | bytes 4194304 | tf_op jit(solution)/shard_map/all_to_all | solution.py:41
  27.3 23.7 %all-to-all-done.1 = bf16[32,32,1024]{2,1,0:T(8,128)(2,1)S(1)} async-done(((bf16[32,32,1024]{2,1,0:T(8,128)(2,1)}), bf16[32,32,1024]{2,1,0:T(8,128)(2,1)S(1)}, u32[]{:S(2)}, u32[]{:S(2)}) %all-to-all-start.1) | async-done | bytes 2097184 | tf_op jit(solution)/shard_map/all_to_all | solution.py:41
  53.9 6.1 %all-to-all-start.2 = ((bf16[32,32,2304]{2,1,0:T(8,128)(2,1)}), bf16[32,32,2304]{2,1,0:T(8,128)(2,1)}, u32[]{:S(2)}, u32[]{:S(2)}) async-start(bf16[32,32,2304]{2,1,0:T(8,128)(2,1)} %broadcast_in_dim.72), calls=%async_computation.2 | async-start | bytes 9437184 | tf_op jit(solution)/shard_map/all_to_all | solution.py:41
  77.2 48.2 %collective-permute-done.1 = bf16[256,1024]{1,0:T(8,128)(2,1)S(1)} collective-permute-done((bf16[256,1024]{1,0:T(8,128)(2,1)S(1)}, bf16[256,1024]{1,0:T(8,128)(2,1)S(1)}, u32[]{:S(2)}, u32[]{:S(2)}) %collective-permute-start.1) | collective-permute-done | bytes 524320 | tf_op jit(solution)/shard_map/ppermute | solution.py:57
  128.7 8.5 %all-to-all-start.3 = ((bf16[32,32,1152]{2,1,0:T(8,128)(2,1)}), bf16[32,32,1152]{2,1,0:T(8,128)(2,1)}, u32[]{:S(2)}, u32[]{:S(2)}) async-start(bf16[32,32,1152]{2,1,0:T(8,128)(2,1)} %broadcast_in_dim.73), calls=%async_computation.3 | async-start | bytes 4718592 | tf_op jit(solution)/shard_map/all_to_all | solution.py:41
  142.1 7.2 %fusion.24 = f32[512,2304]{1,0:T(8,128)} fusion(bf16[1024,2304]{1,0:T(8,128)(2,1)} %bitcast.20, f32[1024]{0:T(1024)S(1)} %copy-done.51, f32[512]{0:T(512)S(1)} %fusion.61, bf16[1,512,1024]{2,1,0:T(8,128)(2,1)S(1)} %copy-done, f32[1,256,1024]{2,1,0:T(8,128)S(1)} %bitcast.178, f32[1,256,1024]{2,1,0:T(8,128)S(1)} %bitcast.176), kind=kOutput, calls=%fused_computation.53 | convolution fusion | flops 2419064832 | bytes 12589056 | tf_op jit(solution)/shard_map/td,df->tf/dot_general | solution.py:126
  149.3 20.2 %all-to-all-done.3 = bf16[32,32,1152]{2,1,0:T(8,128)(2,1)} async-done(((bf16[32,32,1152]{2,1,0:T(8,128)(2,1)}), bf16[32,32,1152]{2,1,0:T(8,128)(2,1)}, u32[]{:S(2)}, u32[]{:S(2)}) %all-to-all-start.3) | async-done | bytes 2359328 | tf_op jit(solution)/shard_map/all_to_all | solution.py:41
  169.4 5.5 %fusion.44 = (f32[512,1152]{1,0:T(8,128)S(1)}, f32[512,1152]{1,0:T(8,128)S(1)}, bf16[512,1152]{1,0:T(8,128)(2,1)S(1)}) fusion(f32[512,2304]{1,0:T(8,128)} %fusion.24, bf16[1024,1152]{1,0:T(8,128)(2,1)} %bitcast.22, bf16[1,512,1024]{2,1,0:T(8,128)(2,1)} %param.22), kind=kOutput, calls=%fused_computation.104 | convolution fusion | flops 1216217088 | bytes 14024704 | tf_op jit(solution)/shard_map/td,df->tf/dot_general | solution.py:126
  174.9 6.2 %fusion.38 = f32[512,1024]{1,0:T(8,128)S(1)} fusion(bf16[1024,2304]{1,0:T(8,128)(2,1)} %bitcast.20, f32[512,1152]{1,0:T(8,128)S(1)} %get-tuple-element.93, f32[512,1152]{1,0:T(8,128)S(1)} %get-tuple-element.92), kind=kOutput, calls=%fused_computation.97 | convolution fusion | flops 2418278400 | bytes 11534336 | tf_op jit(solution)/shard_map/tf,df->td/dot_general | solution.py:126
  184.9 15.0 %collective-permute-done.7 = bf16[256,1024]{1,0:T(8,128)(2,1)S(1)} collective-permute-done((bf16[256,1024]{1,0:T(8,128)(2,1)S(1)}, bf16[256,1024]{1,0:T(8,128)(2,1)S(1)}, u32[]{:S(2)}, u32[]{:S(2)}) %collective-permute-start.7) | collective-permute-done | bytes 524320 | tf_op jit(solution)/shard_map/ppermute | solution.py:57
  209.4 6.4 %all-to-all-start.6 = ((bf16[32,32,1152]{2,1,0:T(8,128)(2,1)}), bf16[32,32,1152]{2,1,0:T(8,128)(2,1)}, u32[]{:S(2)}, u32[]{:S(2)}) async-start(bf16[32,32,1152]{2,1,0:T(8,128)(2,1)} %bitcast.195), calls=%async_computation.6 | async-start | bytes 4718592 | tf_op jit(solution)/shard_map/all_to_all | solution.py:46
  215.9 7.5 %convolution_convert_fusion = bf16[1024,2304]{1,0:T(8,128)(2,1)} fusion(f32[512]{0:T(512)} %copy-done.57, f32[1024]{0:T(1024)} %mul.504, f32[512,1152]{1,0:T(8,128)} %copy-done.89, f32[512,1152]{1,0:T(8,128)} %copy-done.88, bf16[1,512,1024]{2,1,0:T(8,128)(2,1)S(1)} %copy-done, f32[256,1024]{1,0:T(8,128)S(1)} %get-tuple-element.104, ...), kind=kOutput, calls=%fused_computation.1 | convolution fusion | flops 2423783424 | bytes 12589056 | tf_op jit(solution)/shard_map/td,tf->df/dot_general | solution.py:126
  235.0 13.4 %all-to-all-done.6 = bf16[32,32,1152]{2,1,0:T(8,128)(2,1)} async-done(((bf16[32,32,1152]{2,1,0:T(8,128)(2,1)}), bf16[32,32,1152]{2,1,0:T(8,128)(2,1)}, u32[]{:S(2)}, u32[]{:S(2)}) %all-to-all-start.6) | async-done | bytes 2359328 | tf_op jit(solution)/shard_map/all_to_all | solution.py:46
  248.4 5.8 %all-to-all-start.5 = ((bf16[32,32,2304]{2,1,0:T(8,128)(2,1)}), bf16[32,32,2304]{2,1,0:T(8,128)(2,1)}, u32[]{:S(2)}, u32[]{:S(2)}) async-start(bf16[32,32,2304]{2,1,0:T(8,128)(2,1)} %bitcast.189), calls=%async_computation.5 | async-start | bytes 9437184 | tf_op jit(solution)/shard_map/all_to_all | solution.py:46
  261.5 55.5 %collective-permute-done.4 = bf16[256,1024]{1,0:T(8,128)(2,1)S(1)} collective-permute-done((bf16[256,1024]{1,0:T(8,128)(2,1)S(1)}, bf16[256,1024]{1,0:T(8,128)(2,1)S(1)}, u32[]{:S(2)}, u32[]{:S(2)}) %collective-permute-start.4) | collective-permute-done | bytes 524320 | tf_op jit(solution)/shard_map/ppermute | solution.py:57
  321.1 7.1 %collective-permute-done.10 = bf16[256,1024]{1,0:T(8,128)(2,1)S(1)} collective-permute-done((bf16[256,1024]{1,0:T(8,128)(2,1)S(1)}, bf16[256,1024]{1,0:T(8,128)(2,1)S(1)}, u32[]{:S(2)}, u32[]{:S(2)}) %collective-permute-start.10) | collective-permute-done | bytes 524320 | tf_op jit(solution)/shard_map/ppermute | solution.py:57
  347.0 3.8 convolution_convert_fusion.2
  350.8 7.3 %all-to-all-start.7 = ((f32[32,1,832]{2,1,0:T(1,128)}), f32[32,1,832]{2,1,0:T(1,128)S(1)}, u32[]{:S(2)}, u32[]{:S(2)}) async-start(f32[32,1,832]{2,1,0:T(1,128)} %all_to_all.34), calls=%async_computation.7 | async-start | bytes 229376 | tf_op jit(solution)/shard_map/all_to_all | solution.py:170
  361.3 5.5 %all-to-all-done.7 = f32[32,1,832]{2,1,0:T(1,128)S(1)} async-done(((f32[32,1,832]{2,1,0:T(1,128)}), f32[32,1,832]{2,1,0:T(1,128)S(1)}, u32[]{:S(2)}, u32[]{:S(2)}) %all-to-all-start.7) | async-done | bytes 106528 | tf_op jit(solution)/shard_map/all_to_all | solution.py:170
  366.8 4.9 %all-to-all-start.4 = ((bf16[32,32,1024]{2,1,0:T(8,128)(2,1)}), bf16[32,32,1024]{2,1,0:T(8,128)(2,1)}, u32[]{:S(2)}, u32[]{:S(2)}) async-start(bf16[32,32,1024]{2,1,0:T(8,128)(2,1)} %pad_maximum_fusion.2), calls=%async_computation.4 | async-start | bytes 4194304 | tf_op jit(solution)/shard_map/all_to_all | solution.py:46
  377.4 4.8 %fusion.14 = (f32[1,512,1024]{2,1,0:T(8,128)}, f32[1,512,1024]{2,1,0:T(8,128)}) fusion(bf16[1,512,1024]{2,1,0:T(8,128)(2,1)S(1)} %copy-done, f32[1,256,1024]{2,1,0:T(8,128)S(1)} %bitcast.185, f32[1,256,1024]{2,1,0:T(8,128)S(1)} %bitcast.184, f32[1,256,1024]{2,1,0:T(8,128)S(1)} %bitcast.187, f32[1,256,1024]{2,1,0:T(8,128)S(1)} %bitcast.186, ...), kind=kLoop, calls=%fused_computation.29 | loop fusion | flops 10485760 | bytes 14696448 | tf_op jit(solution)/shard_map/add | solution.py:161
  385.1 13.8 %all-to-all-done.4 = bf16[32,32,1024]{2,1,0:T(8,128)(2,1)} async-done(((bf16[32,32,1024]{2,1,0:T(8,128)(2,1)}), bf16[32,32,1024]{2,1,0:T(8,128)(2,1)}, u32[]{:S(2)}, u32[]{:S(2)}) %all-to-all-start.4) | async-done | bytes 2097184 | tf_op jit(solution)/shard_map/all_to_all | solution.py:46
  (292 shorter events, 104.7 us)
Async XLA Ops:
  2.0 17.0 %all-to-all-start = ((bf16[32,2,32]{2,1,0:T(2,128)(2,1)}), bf16[32,2,32]{2,1,0:T(2,128)(2,1)S(1)}, u32[]{:S(2)}, u32[]{:S(2)}) async-start(bf16[32,2,32]{2,1,0:T(2,128)(2,1)} %broadcast_in_dim.67), calls=%async_computation | async-start | bytes 32768 | tf_op jit(solution)/shard_map/all_to_all | solution.py:91
  20.5 30.5 %all-to-all-start.1 = ((bf16[32,32,1024]{2,1,0:T(8,128)(2,1)}), bf16[32,32,1024]{2,1,0:T(8,128)(2,1)S(1)}, u32[]{:S(2)}, u32[]{:S(2)}) async-start(bf16[32,32,1024]{2,1,0:T(8,128)(2,1)} %broadcast_in_dim.68), calls=%async_computation.1 | async-start | bytes 4194304 | tf_op jit(solution)/shard_map/all_to_all | solution.py:41
  53.9 72.4 %all-to-all-start.2 = ((bf16[32,32,2304]{2,1,0:T(8,128)(2,1)}), bf16[32,32,2304]{2,1,0:T(8,128)(2,1)}, u32[]{:S(2)}, u32[]{:S(2)}) async-start(bf16[32,32,2304]{2,1,0:T(8,128)(2,1)} %broadcast_in_dim.72), calls=%async_computation.2 | async-start | bytes 9437184 | tf_op jit(solution)/shard_map/all_to_all | solution.py:41
  69.1 2.8 collective-permute-start
  69.1 56.6 %copy-start.41 = (f32[1152,32]{0,1:T(8,128)S(1)}, f32[1152,32]{0,1:T(8,128)}, u32[]{:S(2)}) copy-start(f32[1152,32]{0,1:T(8,128)} %param.27) | copy-start | bytes 442372
  73.5 55.2 %copy-start.21 = (bf16[256,1024]{1,0:T(8,128)(2,1)}, bf16[256,1024]{1,0:T(8,128)(2,1)S(1)}, u32[]{:S(2)}) copy-start(bf16[256,1024]{1,0:T(8,128)(2,1)S(1)} %add_convert_fusion.5) | copy-start | bytes 1572868
  73.6 51.8 %collective-permute-start.1 = (bf16[256,1024]{1,0:T(8,128)(2,1)S(1)}, bf16[256,1024]{1,0:T(8,128)(2,1)S(1)}, u32[]{:S(2)}, u32[]{:S(2)}) collective-permute-start(bf16[256,1024]{1,0:T(8,128)(2,1)S(1)} %add_convert_fusion.5), channel_id=1, source_target_pairs={{0,2},{2,0},{1,3},{3,1},{4,6},{6,4},{5,7},{7,5},{8,10},{10,8},{9,1... | collective-permute-start | bytes 1572872 | tf_op jit(solution)/shard_map/ppermute | solution.py:57
  125.6 13.1 %collective-permute-start.2 = (f32[256,1024]{1,0:T(8,128)S(1)}, f32[256,1024]{1,0:T(8,128)}, u32[]{:S(2)}, u32[]{:S(2)}) collective-permute-start(f32[256,1024]{1,0:T(8,128)S(1)} %convert_add_fusion.4), channel_id=1, source_target_pairs={{0,1},{1,0},{2,3},{3,2},{4,5},{5,4},{6,7},{7,6},{8,9},{9,8},{10,11... | collective-permute-start | bytes 3145736 | tf_op jit(solution)/shard_map/ppermute | solution.py:59
  128.7 40.7 %all-to-all-start.3 = ((bf16[32,32,1152]{2,1,0:T(8,128)(2,1)}), bf16[32,32,1152]{2,1,0:T(8,128)(2,1)}, u32[]{:S(2)}, u32[]{:S(2)}) async-start(bf16[32,32,1152]{2,1,0:T(8,128)(2,1)} %broadcast_in_dim.73), calls=%async_computation.3 | async-start | bytes 4718592 | tf_op jit(solution)/shard_map/all_to_all | solution.py:41
  181.3 2.7 collective-permute-start.6
  184.2 15.7 %collective-permute-start.7 = (bf16[256,1024]{1,0:T(8,128)(2,1)S(1)}, bf16[256,1024]{1,0:T(8,128)(2,1)S(1)}, u32[]{:S(2)}, u32[]{:S(2)}) collective-permute-start(bf16[256,1024]{1,0:T(8,128)(2,1)S(1)} %add_convert_fusion.3), channel_id=1, source_target_pairs={{0,2},{2,0},{1,3},{3,1},{4,6},{6,4},{5,7},{7,5},{8,10},{10,8},{9,1... | collective-permute-start | bytes 1572872 | tf_op jit(solution)/shard_map/ppermute | solution.py:57
  201.1 22.2 %collective-permute-start.8 = (f32[256,1024]{1,0:T(8,128)}, f32[256,1024]{1,0:T(8,128)}, u32[]{:S(2)}, u32[]{:S(2)}) collective-permute-start(f32[256,1024]{1,0:T(8,128)} %convert_add_fusion.2), channel_id=1, source_target_pairs={{0,1},{1,0},{2,3},{3,2},{4,5},{5,4},{6,7},{7,6},{8,9},{9,8},{10,11... | collective-permute-start | bytes 3145736 | tf_op jit(solution)/shard_map/ppermute | solution.py:59
  205.4 50.3 %collective-permute-start.3 = (f32[256,1024]{1,0:T(8,128)}, f32[256,1024]{1,0:T(8,128)}, u32[]{:S(2)}, u32[]{:S(2)}) collective-permute-start(f32[256,1024]{1,0:T(8,128)} %constant_dynamic-slice_fusion.2), channel_id=1, source_target_pairs={{0,1},{1,0},{2,3},{3,2},{4,5},{5,4},{6,7},{7,6},{8,9},{9,8},{10,11... | collective-permute-start | bytes 3145736 | tf_op jit(solution)/shard_map/ppermute | solution.py:55
  209.4 39.0 %all-to-all-start.6 = ((bf16[32,32,1152]{2,1,0:T(8,128)(2,1)}), bf16[32,32,1152]{2,1,0:T(8,128)(2,1)}, u32[]{:S(2)}, u32[]{:S(2)}) async-start(bf16[32,32,1152]{2,1,0:T(8,128)(2,1)} %bitcast.195), calls=%async_computation.6 | async-start | bytes 4718592 | tf_op jit(solution)/shard_map/all_to_all | solution.py:46
  248.4 102.3 %all-to-all-start.5 = ((bf16[32,32,2304]{2,1,0:T(8,128)(2,1)}), bf16[32,32,2304]{2,1,0:T(8,128)(2,1)}, u32[]{:S(2)}, u32[]{:S(2)}) async-start(bf16[32,32,2304]{2,1,0:T(8,128)(2,1)} %bitcast.189), calls=%async_computation.5 | async-start | bytes 9437184 | tf_op jit(solution)/shard_map/all_to_all | solution.py:46
  255.7 2.8 collective-permute-start.9
  257.5 61.5 %copy-start.17 = (bf16[256,1024]{1,0:T(8,128)(2,1)}, bf16[256,1024]{1,0:T(8,128)(2,1)S(1)}, u32[]{:S(2)}) copy-start(bf16[256,1024]{1,0:T(8,128)(2,1)S(1)} %add_convert_fusion.4) | copy-start | bytes 1572868
  257.5 59.5 %collective-permute-start.4 = (bf16[256,1024]{1,0:T(8,128)(2,1)S(1)}, bf16[256,1024]{1,0:T(8,128)(2,1)S(1)}, u32[]{:S(2)}, u32[]{:S(2)}) collective-permute-start(bf16[256,1024]{1,0:T(8,128)(2,1)S(1)} %add_convert_fusion.4), channel_id=1, source_target_pairs={{0,2},{2,0},{1,3},{3,1},{4,6},{6,4},{5,7},{7,5},{8,10},{10,8},{9,1... | collective-permute-start | bytes 1572872 | tf_op jit(solution)/shard_map/ppermute | solution.py:57
  258.6 69.5 %copy-start.19 = (bf16[256,1024]{1,0:T(8,128)(2,1)}, bf16[256,1024]{1,0:T(8,128)(2,1)S(1)}, u32[]{:S(2)}) copy-start(bf16[256,1024]{1,0:T(8,128)(2,1)S(1)} %add_convert_fusion.2) | copy-start | bytes 1572868
  258.6 69.5 %collective-permute-start.10 = (bf16[256,1024]{1,0:T(8,128)(2,1)S(1)}, bf16[256,1024]{1,0:T(8,128)(2,1)S(1)}, u32[]{:S(2)}, u32[]{:S(2)}) collective-permute-start(bf16[256,1024]{1,0:T(8,128)(2,1)S(1)} %add_convert_fusion.2), channel_id=1, source_target_pairs={{0,2},{2,0},{1,3},{3,1},{4,6},{6,4},{5,7},{7,5},{8,10},{10,8},{9,1... | collective-permute-start | bytes 1572872 | tf_op jit(solution)/shard_map/ppermute | solution.py:57
  319.0 17.7 %collective-permute-start.5 = (f32[256,1024]{1,0:T(8,128)}, f32[256,1024]{1,0:T(8,128)}, u32[]{:S(2)}, u32[]{:S(2)}) collective-permute-start(f32[256,1024]{1,0:T(8,128)} %convert_add_fusion.3), channel_id=1, source_target_pairs={{0,1},{1,0},{2,3},{3,2},{4,5},{5,4},{6,7},{7,6},{8,9},{9,8},{10,11... | collective-permute-start | bytes 3145736 | tf_op jit(solution)/shard_map/ppermute | solution.py:59
  329.3 10.4 %collective-permute-start.11 = (f32[256,1024]{1,0:T(8,128)}, f32[256,1024]{1,0:T(8,128)}, u32[]{:S(2)}, u32[]{:S(2)}) collective-permute-start(f32[256,1024]{1,0:T(8,128)} %convert_add_fusion.1), channel_id=1, source_target_pairs={{0,1},{1,0},{2,3},{3,2},{4,5},{5,4},{6,7},{7,6},{8,9},{9,8},{10,11... | collective-permute-start | bytes 3145736 | tf_op jit(solution)/shard_map/ppermute | solution.py:59
  350.8 16.0 %all-to-all-start.7 = ((f32[32,1,832]{2,1,0:T(1,128)}), f32[32,1,832]{2,1,0:T(1,128)S(1)}, u32[]{:S(2)}, u32[]{:S(2)}) async-start(f32[32,1,832]{2,1,0:T(1,128)} %all_to_all.34), calls=%async_computation.7 | async-start | bytes 229376 | tf_op jit(solution)/shard_map/all_to_all | solution.py:170
  366.8 32.1 %all-to-all-start.4 = ((bf16[32,32,1024]{2,1,0:T(8,128)(2,1)}), bf16[32,32,1024]{2,1,0:T(8,128)(2,1)}, u32[]{:S(2)}, u32[]{:S(2)}) async-start(bf16[32,32,1024]{2,1,0:T(8,128)(2,1)} %pad_maximum_fusion.2), calls=%async_computation.4 | async-start | bytes 4194304 | tf_op jit(solution)/shard_map/all_to_all | solution.py:46
  (86 other events, 454.4 us)

commit v2 on v0

v2 whole, which is shorter than its diff:
```python
import jax
import jax.numpy as jnp
from jax import lax
from jax.experimental import pallas as pl
from jax.experimental.pallas import tpu as pltpu
from jax.sharding import PartitionSpec as P

D = 1024
FF = 4608
ADAM_STEP = 10
NX, NZ, NY = 4, 2, 4
N_DP = NX * NZ * NY
NEAR_PAIRS = [(d, d ^ NY) for d in range(N_DP)]
PLANES = [[(x * NZ + z) * NY + y for x in range(NX) for y in range(NY)] for z in range(NZ)]
CORE_PAIRS = [(0, 1), (1, 0), (2, 3), (3, 2)]
HIGH_PAIRS = [(0, 2), (2, 0), (1, 3), (3, 1)]


epsilon_norm = 1e-05
epsilon_adam = 1e-08
beta_one = 0.9
beta_two = 0.95


def rms_gain(values, gain_row):
    return (
        values
        * lax.rsqrt(jnp.mean(values * values, axis=-1, keepdims=True) + epsilon_norm)
        * gain_row
    )


def adam_step(master, gradient, first, second, step_rate, decay_rate):
    first_new = beta_one * first + (1.0 - beta_one) * gradient
    second_new = beta_two * second + (1.0 - beta_two) * gradient * gradient
    first_hat = first_new / (1.0 - beta_one**ADAM_STEP)
    second_hat = second_new / (1.0 - beta_two**ADAM_STEP)
    master_new = master - step_rate * (
        first_hat / (jnp.sqrt(second_hat) + epsilon_adam) + decay_rate * master
    )
    return (master_new, first_new, second_new)


def swap_core(value):
    return lax.ppermute(value, "tensor", CORE_PAIRS)


def swap_high(value):
    return lax.ppermute(value, "tensor", HIGH_PAIRS)


def swap_near(value):
    return lax.ppermute(value, "dp", NEAR_PAIRS)


def low(value):
    return value.astype(jnp.bfloat16)


def wide(value):
    return value.astype(jnp.float32)


def product_of(spec, left, right):
    return jnp.einsum(spec, left, right, preferred_element_type=jnp.float32)


def halves(value, core):
    half = value.shape[0] // 2
    return (
        lax.dynamic_slice_in_dim(value, core * half, half, 0),
        lax.dynamic_slice_in_dim(value, (1 - core) * half, half, 0),
    )


def joined(own, other, core):
    first = core == 0
    return jnp.concatenate([jnp.where(first, own, other), jnp.where(first, other, own)], axis=0)


def across_high(value):
    value = low(value)
    return wide(value) + wide(swap_high(value))


def sum_four(part, core):
    own, other = halves(part, core)
    return across_high(own + swap_core(other))


def sum_depth(pair):
    half = pair.shape[0] // 2
    return across_high(pair[:half] + wide(swap_near(low(pair[half:]))))


def to_planes(grad):
    columns = grad.shape[1]
    blocks = grad.reshape(NX, NZ, NY, -1, columns).transpose(0, 2, 1, 3, 4)
    return blocks.reshape(NX * NY, NZ, -1, columns)


def exchange(blocks):
    return lax.all_to_all(blocks, "dp", 0, 0, tiled=True, axis_index_groups=PLANES)


def in_order(mine, theirs, near):
    first = near == 0
    return jnp.where(first, mine, theirs), jnp.where(first, theirs, mine)


VMEM_BYTES = 40 * 1024 * 1024


def dot_rows(left, right):
    return lax.dot_general(left, right, (((1,), (1,)), ((), ())), preferred_element_type=jnp.float32)


def dot_columns(left, right):
    return lax.dot_general(left, right, (((0,), (0,)), ((), ())), preferred_element_type=jnp.float32)


def dot_plain(left, right):
    return jnp.dot(left, right, preferred_element_type=jnp.float32)


def hidden_kernel(
    normed_ref, back_ref, weights_ref, gate_ref, up_ref, hidden_ref, keep_ref, give_ref, held
):
    step = pl.program_id(0)
    rows = weights_ref.shape[3]

    @pl.when(step == 0)
    def _():
        for x in range(NX):
            for z in range(NZ):
                for y in range(NY):
                    start = ((x * NZ + z) * NY + y) * rows
                    for k in range(3):
                        held[k, start : start + rows, :] = weights_ref[x * NY + y, z, k]

    normed = normed_ref[...]
    gate = dot_plain(normed, held[0])
    up = dot_plain(normed, held[1])
    back = dot_plain(back_ref[...], held[2])
    share = jax.nn.sigmoid(gate)
    smooth = gate * share
    hidden_ref[...] = low(smooth * up)
    back_up = low(back * smooth)
    back_gate = low(back * up * (share + smooth * (1.0 - share)))
    gate_ref[...] = back_gate
    up_ref[...] = back_up
    part = dot_rows(back_gate, held[0]) + dot_rows(back_up, held[1])

    @pl.when(step < 2)
    def _():
        give_ref[...] = part

    @pl.when(step >= 2)
    def _():
        keep_ref[...] = part


def hidden_pass(normed, back, weights):
    tokens, width = normed.shape
    units = weights.shape[-1]
    block = tokens // 4
    turned = lambda i: ((i + 2) % 4, 0)
    narrow = jax.ShapeDtypeStruct((tokens, units), jnp.bfloat16)
    half = jax.ShapeDtypeStruct((tokens // 2, width), jnp.float32)
    return pl.pallas_call(
        hidden_kernel,
        grid=(4,),
        in_specs=[
            pl.BlockSpec((block, width), turned),
            pl.BlockSpec((block, width), turned),
            pl.BlockSpec(weights.shape, lambda i: (0, 0, 0, 0, 0)),
        ],
        out_specs=[
            pl.BlockSpec((block, units), turned),
            pl.BlockSpec((block, units), turned),
            pl.BlockSpec((block, units), turned),
            pl.BlockSpec((block, width), lambda i: (jnp.maximum(i - 2, 0), 0)),
            pl.BlockSpec((block, width), lambda i: (jnp.minimum(i, 1), 0)),
        ],
        out_shape=[narrow, narrow, narrow, half, half],
        scratch_shapes=[pltpu.VMEM((3, width, units), jnp.bfloat16)],
        compiler_params=pltpu.CompilerParams(vmem_limit_bytes=VMEM_BYTES),
        cost_estimate=pl.CostEstimate(
            flops=10 * tokens * width * units,
            bytes_accessed=16 * tokens * width,
            transcendentals=tokens * units,
        ),
        name="hidden_pass",
    )(normed, back, weights)


def grads_kernel(
    normed_ref, back_ref, gate_ref, up_ref, hidden_ref, down_ref, grads_ref, keep_ref, give_ref
):
    rows, units = down_ref.shape[3:]
    normed, back, hidden = normed_ref[...], back_ref[...], hidden_ref[...]
    for k, (left, right) in enumerate(
        ((normed, gate_ref[...]), (normed, up_ref[...]), (back, hidden))
    ):
        grad = low(dot_columns(left, right))
        for z in range(NZ):
            part = grad[z * NY * rows : (z + 1) * NY * rows]
            grads_ref[:, z, k] = part.reshape(NY, rows, units)
    down = jnp.concatenate(
        [down_ref[:, z, 0].reshape(NY * rows, units) for z in range(NZ)], axis=0
    )
    half = hidden.shape[0] // 2
    keep_ref[...] = dot_rows(hidden[:half], down)
    give_ref[...] = dot_rows(hidden[half:], down)


def grads_pass(normed, back, gate, up, hidden, weights):
    tokens, width = normed.shape
    units = weights.shape[-1]
    block = width // NX
    column = lambda i: (0, i)
    whole = lambda i: (0, 0)
    half = jax.ShapeDtypeStruct((tokens // 2, width), jnp.float32)
    return pl.pallas_call(
        grads_kernel,
        grid=(NX,),
        in_specs=[
            pl.BlockSpec((tokens, block), column),
            pl.BlockSpec((tokens, block), column),
            pl.BlockSpec((tokens, units), whole),
            pl.BlockSpec((tokens, units), whole),
            pl.BlockSpec((tokens, units), whole),
            pl.BlockSpec((NY, NZ, 1) + weights.shape[3:], lambda i: (i, 0, 2, 0, 0)),
        ],
        out_specs=[
            pl.BlockSpec((NY,) + weights.shape[1:], lambda i: (i, 0, 0, 0, 0)),
            pl.BlockSpec((tokens // 2, block), column),
            pl.BlockSpec((tokens // 2, block), column),
        ],
        out_shape=[jax.ShapeDtypeStruct(weights.shape, jnp.bfloat16), half, half],
        compiler_params=pltpu.CompilerParams(vmem_limit_bytes=VMEM_BYTES),
        cost_estimate=pl.CostEstimate(
            flops=8 * tokens * width * units,
            bytes_accessed=14 * tokens * width,
            transcendentals=0,
        ),
        name="grads_pass",
    )(normed, back, gate, up, hidden, weights)


def pieces(value):
    high = lax.reduce_precision(value, 8, 7)
    rest = value - high
    middle = lax.reduce_precision(rest, 8, 7)
    return [low(high), low(middle), low(rest - middle)]


def shards(
    tokens_in,
    cotangent,
    segment_ids,
    in_weight,
    out_weight,
    gate_up_weight,
    down_weight,
    conv_weight,
    norm_gains,
    in_first,
    in_second,
    out_first,
    out_second,
    gate_up_first,
    gate_up_second,
    down_first,
    down_second,
    conv_first,
    conv_second,
    gains_first,
    gains_second,
):
    rows, length, width = tokens_in.shape
    count = rows * length
    taps_n, channels = conv_weight.shape
    units = gate_up_weight.shape[2]
    own_rows = gate_up_weight.shape[1]
    part_units = units // NZ
    core = lax.axis_index("tensor") % 2
    near = (lax.axis_index("dp") // NY) % NZ

    mix_cols = 4 * channels
    low_mix = jnp.concatenate(
        [
            in_weight[0],
            in_weight[1],
            in_weight[2],
            out_weight.T,
            jnp.pad(norm_gains.T, ((0, 0), (0, 126))),
        ],
        axis=1,
    )
    low_mix = low(low_mix)
    low_ffn = low(jnp.concatenate([gate_up_weight, down_weight.T[None]], axis=0))
    keep = lax.dynamic_slice_in_dim(low_ffn, near * part_units, part_units, 2)
    give = lax.dynamic_slice_in_dim(low_ffn, (1 - near) * part_units, part_units, 2)
    take = swap_near(give)
    low_ffn = jnp.stack(in_order(keep, take, near), axis=0)
    ffn_copies = jnp.broadcast_to(low_ffn[None], (NX * NY,) + low_ffn.shape)
    back_out = cotangent.reshape(count, width)
    back_own, back_other = halves(back_out, core)
    back_near = swap_near(back_own)
    back_four = jnp.concatenate([back_own, back_near, back_other, swap_core(back_near)], axis=0)

    low_mix = jnp.stack(in_order(low_mix, swap_near(low_mix), near), axis=0)
    mix_full = exchange(jnp.broadcast_to(low_mix[None], (NX * NY,) + low_mix.shape))
    mix_full, ffn_copies, back_four = lax.optimization_barrier((mix_full, ffn_copies, back_four))
    ffn_full = exchange(ffn_copies)
    mix_full = mix_full.reshape(NX, NY, NZ, own_rows, -1).transpose(0, 2, 1, 3, 4).reshape(width, -1)
    in_full = mix_full[:, : 3 * channels]
    out_full = mix_full[:, 3 * channels : mix_cols]
    gains_value = wide(mix_full[:, mix_cols : mix_cols + 2]).T


    flat = wide(tokens_in.reshape(count, width))
    flat_half = halves(flat, core)[0]
    seg_flat = segment_ids.reshape(count)
    place = lax.iota(jnp.int32, count) % length
    mask_one = ((place >= 1) & (seg_flat == jnp.roll(seg_flat, 1)))[:, None]
    mask_two = ((place >= 2) & (seg_flat == jnp.roll(seg_flat, 2)))[:, None]

    def mixer_local(projected, taps):
        product = projected[:, :channels] * projected[:, 2 * channels :]
        conv_sum = taps[0] * product + taps[1] * jnp.where(
            mask_one, jnp.roll(product, 1, axis=0), 0.0
        )
        conv_sum = conv_sum + taps[2] * jnp.where(mask_two, jnp.roll(product, 2, axis=0), 0.0)
        return projected[:, channels : 2 * channels] * conv_sum

    normed_one = low(rms_gain(flat, gains_value[0]))
    projected = product_of("td,dc->tc", normed_one, in_full)
    gated_f, mixer_pull = jax.vjp(mixer_local, projected, conv_weight)
    gated = low(gated_f)
    middle = flat_half + sum_four(product_of("tc,dc->td", gated, out_full), core)
    normed_two_f, norm_two_pull = jax.vjp(rms_gain, middle, gains_value[1])
    normed_two = low(normed_two_f)
    normed_two = jnp.concatenate([normed_two, swap_near(normed_two)], axis=0)
    normed_two = jnp.concatenate([normed_two, swap_core(normed_two)], axis=0)

    back_gate, back_up, hidden, back_keep, back_give = hidden_pass(
        normed_two, back_four, ffn_full
    )
    back_pair = back_keep + swap_core(back_give)
    back_pair, back_gate, back_up, hidden = lax.optimization_barrier(
        (back_pair, back_gate, back_up, hidden)
    )
    back_normed_two = sum_depth(back_pair)
    grad_ffn, ffn_keep, ffn_give = grads_pass(
        normed_two, back_four, back_gate, back_up, hidden, ffn_full
    )
    grad_ffn = exchange(grad_ffn)

    ffn_keep, ffn_give, back_normed_two = lax.optimization_barrier(
        (ffn_keep, ffn_give, back_normed_two)
    )
    result = middle + sum_depth(ffn_keep + swap_core(ffn_give))
    result = joined(result, swap_core(result), core)

    back_middle_norm, grad_gain_two = norm_two_pull(back_normed_two)
    back_middle = wide(back_own) + back_middle_norm
    back_branch = low(back_middle)
    back_branch = joined(back_branch, swap_core(back_branch), core)
    grad_out = product_of("td,tc->dc", back_branch, gated)
    back_gated = product_of("td,dc->tc", back_branch, out_full)
    back_projected_f, grad_conv = mixer_pull(back_gated)
    back_projected = low(back_projected_f)
    grad_in = product_of("td,tc->dc", normed_one, back_projected)
    back_normed_one = product_of("tc,dc->td", back_projected, in_full)
    grad_gain_one = jnp.sum(back_normed_one * rms_gain(flat, 1.0), axis=0)
    grad_gains = jnp.stack([grad_gain_one, 0.5 * grad_gain_two])
    grad_gains = grad_gains.reshape(2, N_DP, own_rows).transpose(1, 0, 2).reshape(N_DP, -1)
    grad_conv = jnp.broadcast_to(grad_conv.reshape(1, -1), (N_DP, grad_conv.size))
    small_size = grad_gains.shape[1] + grad_conv.shape[1]
    small = jnp.concatenate([grad_gains, grad_conv], axis=1)
    small = jnp.pad(small, ((0, 0), (0, 1024 - small_size))).reshape(N_DP, 8, 128)
    small = jnp.concatenate(pieces(small) + [jnp.zeros((N_DP, own_rows - 24, 128), jnp.bfloat16)], axis=1)
    grad_mix = jnp.concatenate([low(grad_in), low(grad_out), small.reshape(width, 128)], axis=1)
    grad_mix = to_planes(grad_mix)
    grad_ffn, grad_mix = lax.optimization_barrier((grad_ffn, grad_mix))
    red_mix = jnp.sum(wide(exchange(grad_mix)), axis=0)
    keep = lax.dynamic_index_in_dim(red_mix, near, 0, keepdims=False)
    red_mix = keep + swap_near(lax.dynamic_index_in_dim(red_mix, 1 - near, 0, keepdims=False))
    grad_ffn = jnp.sum(wide(grad_ffn), axis=0)
    keep = lax.dynamic_index_in_dim(grad_ffn, near, 0, keepdims=False)
    take = swap_near(lax.dynamic_index_in_dim(grad_ffn, 1 - near, 0, keepdims=False))
    red_ffn = jnp.concatenate(in_order(keep, take, near), axis=2)
    back_normed_one = sum_four(back_normed_one, core)
    back_tokens_norm = jax.vjp(rms_gain, flat_half, gains_value[0])[1](back_normed_one)[0]
    back_tokens = back_middle + back_tokens_norm
    back_tokens = joined(back_tokens, swap_core(back_tokens), core)

    red_small = jnp.sum(red_mix[:24, mix_cols:].reshape(3, 1024), axis=0)
    red_gains = red_small[: norm_gains.size].reshape(norm_gains.shape)
    twin_gains = swap_core(red_gains)
    high_gains = swap_high(red_gains) + swap_high(twin_gains)
    red_gains = (red_gains + twin_gains) + high_gains
    conv_total = red_small[norm_gains.size : small_size].reshape(conv_weight.shape)
    red_in = red_mix[:, : 3 * channels].reshape(-1, 3, channels).transpose(1, 0, 2)
    red_out = red_mix[:, 3 * channels : mix_cols].T
    red_gate_up = red_ffn[:2]
    red_down = red_ffn[2].T
    rate_wide = 0.8 / D**0.5
    rate_down = 0.8 / FF**0.5
    in_new = adam_step(in_weight, red_in, in_first, in_second, rate_wide, 0.1)
    out_new = adam_step(out_weight, red_out, out_first, out_second, rate_wide, 0.1)
    gate_up_new = adam_step(
        gate_up_weight, red_gate_up, gate_up_first, gate_up_second, rate_wide, 0.1
    )
    down_new = adam_step(down_weight, red_down, down_first, down_second, rate_down, 0.1)
    conv_new = adam_step(conv_weight, conv_total, conv_first, conv_second, 1.0, 0.0)
    gains_new = adam_step(norm_gains, red_gains, gains_first, gains_second, 0.3, 0.0)
    return (
        result.reshape(rows, length, width),
        back_tokens.reshape(rows, length, width),
        in_new[0],
        in_new[1],
        in_new[2],
        out_new[0],
        out_new[1],
        out_new[2],
        gate_up_new[0],
        gate_up_new[1],
        gate_up_new[2],
        down_new[0],
        down_new[1],
        down_new[2],
        conv_new[0],
        conv_new[1],
        conv_new[2],
        gains_new[0],
        gains_new[1],
        gains_new[2],
    )


def solution(mesh):
    in_specs = (
        P("dp", None, None),
        P("dp", None, None),
        P("dp", None),
        P(None, "dp", "tensor"),
        P("tensor", "dp"),
        P(None, "dp", "tensor"),
        P("tensor", "dp"),
        P(None, "tensor"),
        P(None, "dp"),
        P(None, "dp", "tensor"),
        P(None, "dp", "tensor"),
        P("tensor", "dp"),
        P("tensor", "dp"),
        P(None, "dp", "tensor"),
        P(None, "dp", "tensor"),
        P("tensor", "dp"),
        P("tensor", "dp"),
        P(None, "tensor"),
        P(None, "tensor"),
        P(None, "dp"),
        P(None, "dp"),
    )
    out_specs = (
        P("dp", None, None),
        P("dp", None, None),
        P(None, "dp", "tensor"),
        P(None, "dp", "tensor"),
        P(None, "dp", "tensor"),
        P("tensor", "dp"),
        P("tensor", "dp"),
        P("tensor", "dp"),
        P(None, "dp", "tensor"),
        P(None, "dp", "tensor"),
        P(None, "dp", "tensor"),
        P("tensor", "dp"),
        P("tensor", "dp"),
        P("tensor", "dp"),
        P(None, "tensor"),
        P(None, "tensor"),
        P(None, "tensor"),
        P(None, "dp"),
        P(None, "dp"),
        P(None, "dp"),
    )
    return jax.shard_map(shards, mesh=mesh, in_specs=in_specs, out_specs=out_specs, check_vma=False)
```

time: 1570 us -> 294 us (0.19)
  waiting for transfers between devices: 1200 us -> 139 us
  blocking collectives: 242 us -> 0 us
  starting transfers between devices: 0.59 us -> 63.5 us
  matrix products: 48.1 us -> 10.4 us
  Pallas kernels: 0 us -> 21.4 us
    unnamed x12 -> x0, waiting for transfers between devices: 517 us -> none
    all_gather x3 -> x0, waiting for transfers between devices: 307 us -> none  [the longest x1 157 us: shards(): lax.all_gather(gate_up_weight.astype(jnp.bfloat16), 'dp', axis=1, tiled=T...]
    reduce_scatter x2 -> x0, waiting for transfers between devices: 236 us -> none  [the longest x1 170 us: shards(): lax.psum_scatter(grad_down, 'dp', scatter_dimension=1, tiled=True)]
    all_gather x2 -> x0, blocking collectives: 160 us -> none  [the longest x1 81.5 us: shards(): lax.all_gather(norm_gains.astype(jnp.bfloat16), 'dp', axis=1, tiled=True)]
    psum x3 -> x0, waiting for transfers between devices: 143 us -> none  [the longest x1 56.3 us: shards(): lax.psum(jnp.dot(gated, out_full, preferred_element_type=jnp.float32), 't...]
    ppermute x0 -> x24, waiting for transfers between devices: none -> 88.1 us  [the longest x8 54.8 us: swap_near(): return lax.ppermute(value, 'dp', NEAR_PAIRS)]
    psum x1 -> x0, blocking collectives: 81.9 us -> none  [shards(): conv_total = lax.psum(grad_conv, 'dp')]
    all_to_all x0 -> x4, waiting for transfers between devices: none -> 50.7 us  [exchange(): lax.all_to_all(blocks, 'dp', 0, 0, tiled=True, axis_index_groups=PLANES)]
  transfers between devices with their start and end apart: 10 -> 28, of which waited for: 9 -> 19; matrix products, arithmetic and copies ran while one was open for 4% -> 15% of each run, Pallas kernels for 0% -> 3%
where the time goes in v2:
time: 294 us; the launch traced here: 293 us
  waiting for transfers between devices  139 us (47%)
  starting transfers between devices  63.5 us (22%)
  other arithmetic  36.1 us (12%)
  Pallas kernels  21.4 us (7%)
  local copies, waits for them, and re-layouts  21.3 us (7%)
  matrix products  10.4 us (4%)
    ppermute x8, waiting for transfers between devices, swap_near(): return lax.ppermute(value, 'dp', NEAR_PAIRS)  54.8 us
    all_to_all x4, waiting for transfers between devices, exchange(): lax.all_to_all(blocks, 'dp', 0, 0, tiled=True, axis_index_groups=PLANES)  50.7 us
    all_to_all x4, starting transfers between devices, exchange(): lax.all_to_all(blocks, 'dp', 0, 0, tiled=True, axis_index_groups=PLANES)  35.2 us
    ppermute x6, waiting for transfers between devices, swap_high(): return lax.ppermute(value, 'tensor', HIGH_PAIRS)  26.1 us
    ppermute x6, starting transfers between devices, swap_high(): return lax.ppermute(value, 'tensor', HIGH_PAIRS)  15.9 us
    pallas_call x1, Pallas kernels, hidden_pass(): pl.pallas_call(hidden_kernel, grid=(4,), in_specs=[pl.BlockSpec((block, w...  11.9 us
    ppermute x8, starting transfers between devices, swap_near(): return lax.ppermute(value, 'dp', NEAR_PAIRS)  11.4 us
    dot_general x6, matrix products, product_of(): return jnp.einsum(spec, left, right, preferred_element_type=jnp.float32)  10.4 us
  transfers between devices with their start and end apart: 28, of which 19 were waited for; matrix products, arithmetic and copies ran while one was open for 15% of the time, Pallas kernels for 3%

profile of v2, /device:TPU:0, one launch (start us, length us, event | category | flops | bytes accessed | tf_op | source)
XLA Modules:
  0.0 293.3 jit_solution(12531095142343291167)
XLA Ops:
  9.3 7.3 %all-to-all-start = ((bf16[16,2,32,1152]{3,2,1,0:T(8,128)(2,1)}), bf16[16,2,32,1152]{3,2,1,0:T(8,128)(2,1)}, u32[]{:S(2)}, u32[]{:S(2)}) async-start(bf16[16,2,32,1152]{3,2,1,0:T(8,128)(2,1)} %broadcast_in_dim.62), calls=%async_computation | async-start | bytes 4718592 | tf_op jit(solution)/shard_map/all_to_all | solution.py:103
  20.8 10.5 %collective-permute-done.2 = bf16[256,1024]{1,0:T(8,128)(2,1)S(1)} collective-permute-done((bf16[256,1024]{1,0:T(8,128)(2,1)S(1)}, bf16[256,1024]{1,0:T(8,128)(2,1)S(1)}, u32[]{:S(2)}, u32[]{:S(2)}) %collective-permute-start.2) | collective-permute-done | bytes 524320 | tf_op jit(solution)/shard_map/ppermute | solution.py:53
  35.5 12.9 %all-to-all-done = bf16[16,2,32,1152]{3,2,1,0:T(8,128)(2,1)} async-done(((bf16[16,2,32,1152]{3,2,1,0:T(8,128)(2,1)}), bf16[16,2,32,1152]{3,2,1,0:T(8,128)(2,1)}, u32[]{:S(2)}, u32[]{:S(2)}) %all-to-all-start) | async-done | bytes 2359328 | tf_op jit(solution)/shard_map/all_to_all | solution.py:103
  58.8 4.5 %all-to-all-start.1 = ((bf16[16,2,3,32,576]{4,3,2,1,0:T(8,128)(2,1)}), bf16[16,2,3,32,576]{4,3,2,1,0:T(8,128)(2,1)}, u32[]{:S(2)}, u32[]{:S(2)}) async-start(bf16[16,2,3,32,576]{4,3,2,1,0:T(8,128)(2,1)} %broadcast_in_dim.64), calls=%async_computation.1 | async-start | bytes 7864320 | tf_op jit(solution)/shard_map/all_to_all | solution.py:103
  65.1 3.8 %collective-permute-start.5 = (bf16[256,1024]{1,0:T(8,128)(2,1)S(1)}, bf16[256,1024]{1,0:T(8,128)(2,1)S(1)}, u32[]{:S(2)}, u32[]{:S(2)}) collective-permute-start(bf16[256,1024]{1,0:T(8,128)(2,1)S(1)} %add_convert_fusion.3), channel_id=1, source_target_pairs={{0,2},{2,0},{1,3},{3,1},{4,6},{6,4},{5,7},{7,5},{8,10},{10,8},{9,1... | collective-permute-start | bytes 1572872 | tf_op jit(solution)/shard_map/ppermute | solution.py:49
  69.1 12.3 %collective-permute-done.5 = bf16[256,1024]{1,0:T(8,128)(2,1)S(1)} collective-permute-done((bf16[256,1024]{1,0:T(8,128)(2,1)S(1)}, bf16[256,1024]{1,0:T(8,128)(2,1)S(1)}, u32[]{:S(2)}, u32[]{:S(2)}) %collective-permute-start.5) | collective-permute-done | bytes 524320 | tf_op jit(solution)/shard_map/ppermute | solution.py:49
  83.3 12.6 %collective-permute-done.6 = bf16[256,1024]{1,0:T(8,128)(2,1)S(1)} collective-permute-done((bf16[256,1024]{1,0:T(8,128)(2,1)S(1)}, bf16[256,1024]{1,0:T(8,128)(2,1)S(1)}, u32[]{:S(2)}, u32[]{:S(2)}) %collective-permute-start.6) | collective-permute-done | bytes 524320 | tf_op jit(solution)/shard_map/ppermute | solution.py:53
  100.2 16.4 %all-to-all-done.1.weights_ref.down_ref = bf16[16,2,3,32,576]{4,3,2,1,0:T(8,128)(2,1)} async-done(((bf16[16,2,3,32,576]{4,3,2,1,0:T(8,128)(2,1)}), bf16[16,2,3,32,576]{4,3,2,1,0:T(8,128)(2,1)}, u32[]{:S(2)}, u32[]{:S(2)}) %all-to-all-start.1) | async-done | bytes 3538976 | tf_op jit(solution)/shard_map/all_to_all | solution.py:103
  118.2 11.9 %hidden_pass.1 = (bf16[1024,576]{1,0:T(8,128)(2,1)S(1)}, bf16[1024,576]{1,0:T(8,128)(2,1)S(1)}, bf16[1024,576]{1,0:T(8,128)(2,1)S(1)}, f32[512,1024]{1,0:T(8,128)S(1)}, f32[512,1024]{1,0:T(8,128)S(1)}) custom-call(bf16[1024,1024]{1,0:T(8,128)(2,1)S(1)} %copy-done.2, bf16[1024,1024]{1,0:T(8,128)(2,1)S(1)} %pad_maximum_fusion.back_ref, ...), custom_call_target="tpu_custom_call" | custom-call | flops 6039797760 | bytes 16777216 | tf_op jit(solution)/shard_map/hidden_pass/pallas_call | solution.py:170
  130.2 4.1 %collective-permute-done.8 = f32[512,1024]{1,0:T(8,128)S(1)} collective-permute-done((f32[512,1024]{1,0:T(8,128)S(1)}, f32[512,1024]{1,0:T(8,128)S(1)}, u32[]{:S(2)}, u32[]{:S(2)}) %collective-permute-start.8) | collective-permute-done | bytes 2097184 | tf_op jit(solution)/shard_map/ppermute | solution.py:45
  136.8 12.2 %collective-permute-done.9 = bf16[256,1024]{1,0:T(8,128)(2,1)S(1)} collective-permute-done((bf16[256,1024]{1,0:T(8,128)(2,1)S(1)}, bf16[256,1024]{1,0:T(8,128)(2,1)S(1)}, u32[]{:S(2)}, u32[]{:S(2)}) %collective-permute-start.9) | collective-permute-done | bytes 524320 | tf_op jit(solution)/shard_map/ppermute | solution.py:53
  149.2 4.0 %collective-permute-start.10 = (bf16[256,1024]{1,0:T(8,128)(2,1)S(1)}, bf16[256,1024]{1,0:T(8,128)(2,1)S(1)}, u32[]{:S(2)}, u32[]{:S(2)}) collective-permute-start(bf16[256,1024]{1,0:T(8,128)(2,1)S(1)} %add_convert_fusion.2), channel_id=1, source_target_pairs={{0,2},{2,0},{1,3},{3,1},{4,6},{6,4},{5,7},{7,5},{8,10},{10,8},{9,1... | collective-permute-start | bytes 1572872 | tf_op jit(solution)/shard_map/ppermute | solution.py:49
  153.1 9.5 %grads_pass.1 = (bf16[16,2,3,32,576]{4,3,2,1,0:T(8,128)(2,1)}, f32[512,1024]{1,0:T(8,128)S(1)}, f32[512,1024]{1,0:T(8,128)S(1)}) custom-call(bf16[1024,1024]{1,0:T(8,128)(2,1)S(1)} %copy-done.2, bf16[1024,1024]{1,0:T(8,128)(2,1)S(1)} %copy-done.1, bf16[1024,576]{1,0:T(8,128)(2,1)S(1)} %get-tuple-element.48.gate_ref, ...), custom_call_target="tpu_custom_call" | custom-call | flops 4831838208 | bytes 14680064 | tf_op jit(solution)/shard_map/grads_pass/pallas_call | solution.py:224
  166.3 11.1 %all-to-all-start.2 = ((bf16[16,2,3,32,576]{4,3,2,1,0:T(8,128)(2,1)}), bf16[16,2,3,32,576]{4,3,2,1,0:T(8,128)(2,1)}, u32[]{:S(2)}, u32[]{:S(2)}) async-start(bf16[16,2,3,32,576]{4,3,2,1,0:T(8,128)(2,1)} %get-tuple-element.57), calls=%async_computation.2 | async-start | bytes 7864320 | tf_op jit(solution)/shard_map/all_to_all | solution.py:103
  185.5 4.5 %multiply_reduce_fusion = (f32[1024]{0:T(1024)S(1)}, f32[512,1024]{1,0:T(8,128)}) fusion(bf16[1,512,1024]{2,1,0:T(8,128)(2,1)} %param.21, f32[512]{0:T(512)S(1)} %copy-done.64, bf16[1024,1152]{1,0:T(8,128)(2,1)} %bitcast.145, f32[512,256]{1,0:T(8,128)} %slice_multiply_fusion, f32[512,256]{1,0:T(8,128)} %get-tuple-element.128, f32[512,256]{1,0:T(8,128)} %get-tuple-element.146), kind=kOutput, calls=%fused_computation.10 | convolution fusion | flops 808582144 | bytes 6297600 | tf_op jit(solution)/shard_map/tc,dc->td/dot_general | solution.py:65
  197.5 3.3 %collective-permute-start.17 = (bf16[256,1024]{1,0:T(8,128)(2,1)S(1)}, bf16[256,1024]{1,0:T(8,128)(2,1)S(1)}, u32[]{:S(2)}, u32[]{:S(2)}) collective-permute-start(bf16[256,1024]{1,0:T(8,128)(2,1)S(1)} %add_convert_fusion.1), channel_id=1, source_target_pairs={{0,2},{2,0},{1,3},{3,1},{4,6},{6,4},{5,7},{7,5},{8,10},{10,8},{9,1... | collective-permute-start | bytes 1572872 | tf_op jit(solution)/shard_map/ppermute | solution.py:49
  206.2 7.7 %collective-permute-done.17 = bf16[256,1024]{1,0:T(8,128)(2,1)S(1)} collective-permute-done((bf16[256,1024]{1,0:T(8,128)(2,1)S(1)}, bf16[256,1024]{1,0:T(8,128)(2,1)S(1)}, u32[]{:S(2)}, u32[]{:S(2)}) %collective-permute-start.17) | collective-permute-done | bytes 524320 | tf_op jit(solution)/shard_map/ppermute | solution.py:49
  214.3 10.8 %collective-permute-done.12 = bf16[256,1024]{1,0:T(8,128)(2,1)S(1)} collective-permute-done((bf16[256,1024]{1,0:T(8,128)(2,1)S(1)}, bf16[256,1024]{1,0:T(8,128)(2,1)S(1)}, u32[]{:S(2)}, u32[]{:S(2)}) %collective-permute-start.12) | collective-permute-done | bytes 524320 | tf_op jit(solution)/shard_map/ppermute | solution.py:53
  227.2 2.9 all-to-all-done.2
  230.1 12.3 %all-to-all-start.3 = ((bf16[16,2,32,1152]{3,2,1,0:T(8,128)(2,1)}), bf16[16,2,32,1152]{3,2,1,0:T(8,128)(2,1)}, u32[]{:S(2)}, u32[]{:S(2)}) async-start(bf16[16,2,32,1152]{3,2,1,0:T(8,128)(2,1)} %bitcast.136), calls=%async_computation.3 | async-start | bytes 4718592 | tf_op jit(solution)/shard_map/all_to_all | solution.py:103
  249.2 3.5 %collective-permute-done.20 = f32[3,32,576]{2,1,0:T(8,128)S(1)} collective-permute-done((f32[3,32,576]{2,1,0:T(8,128)S(1)}, f32[3,32,576]{2,1,0:T(8,128)S(1)}, u32[]{:S(2)}, u32[]{:S(2)}) %collective-permute-start.20) | collective-permute-done | bytes 221216 | tf_op jit(solution)/shard_map/ppermute | solution.py:53
  256.9 18.4 %all-to-all-done.3 = bf16[16,2,32,1152]{3,2,1,0:T(8,128)(2,1)} async-done(((bf16[16,2,32,1152]{3,2,1,0:T(8,128)(2,1)}), bf16[16,2,32,1152]{3,2,1,0:T(8,128)(2,1)}, u32[]{:S(2)}, u32[]{:S(2)}) %all-to-all-start.3) | async-done | bytes 2359328 | tf_op jit(solution)/shard_map/all_to_all | solution.py:103
  282.8 3.3 %collective-permute-start.22 = (f32[2,32]{1,0:T(2,128)S(1)}, f32[2,32]{1,0:T(2,128)S(1)}, u32[]{:S(2)}, u32[]{:S(2)}) collective-permute-start(f32[2,32]{1,0:T(2,128)S(1)} %reshape.254), channel_id=1, source_target_pairs={{0,2},{2,0},{1,3},{3,1},{4,6},{6,4},{5,7},{7,5},{8,10},{10,8},{9,1... | collective-permute-start | bytes 776 | tf_op jit(solution)/shard_map/ppermute | solution.py:49
  288.6 4.2 %collective-permute-done.23 = f32[2,32]{1,0:T(2,128)S(1)} collective-permute-done((f32[2,32]{1,0:T(2,128)S(1)}, f32[2,32]{1,0:T(2,128)S(1)}, u32[]{:S(2)}, u32[]{:S(2)}) %collective-permute-start.23) | collective-permute-done | bytes 288 | tf_op jit(solution)/shard_map/ppermute | solution.py:49
  (283 shorter events, 87.4 us)
Async XLA Ops:
  3.2 4.4 %collective-permute-start = (bf16[32,1152]{1,0:T(8,128)(2,1)S(1)}, bf16[32,1152]{1,0:T(8,128)(2,1)S(1)}, u32[]{:S(2)}, u32[]{:S(2)}) collective-permute-start(bf16[32,1152]{1,0:T(8,128)(2,1)S(1)} %constant_dynamic-update-slice_fusion), channel_id=1, source_target_pairs={{0,16},{4,20},{8,24},{12,28},{16,0},{20,4},{24,8},{28,12},{32,48},... | collective-permute-start | bytes 221192 | tf_op jit(solution)/shard_map/ppermute | solution.py:53
  9.3 39.1 %all-to-all-start = ((bf16[16,2,32,1152]{3,2,1,0:T(8,128)(2,1)}), bf16[16,2,32,1152]{3,2,1,0:T(8,128)(2,1)}, u32[]{:S(2)}, u32[]{:S(2)}) async-start(bf16[16,2,32,1152]{3,2,1,0:T(8,128)(2,1)} %broadcast_in_dim.62), calls=%async_computation | async-start | bytes 4718592 | tf_op jit(solution)/shard_map/all_to_all | solution.py:103
  17.5 13.7 %collective-permute-start.2 = (bf16[256,1024]{1,0:T(8,128)(2,1)S(1)}, bf16[256,1024]{1,0:T(8,128)(2,1)S(1)}, u32[]{:S(2)}, u32[]{:S(2)}) collective-permute-start(bf16[256,1024]{1,0:T(8,128)(2,1)S(1)} %get-tuple-element.143), channel_id=1, source_target_pairs={{0,16},{4,20},{8,24},{12,28},{16,0},{20,4},{24,8},{28,12},{32,48},... | collective-permute-start | bytes 1572872 | tf_op jit(solution)/shard_map/ppermute | solution.py:53
  19.6 12.9 %collective-permute-start.1 = (bf16[3,32,576]{2,1,0:T(8,128)(2,1)S(1)}, bf16[3,32,576]{2,1,0:T(8,128)(2,1)S(1)}, u32[]{:S(2)}, u32[]{:S(2)}) collective-permute-start(bf16[3,32,576]{2,1,0:T(8,128)(2,1)S(1)} %fusion.19), channel_id=1, source_target_pairs={{0,16},{4,20},{8,24},{12,28},{16,0},{20,4},{24,8},{28,12},{32,48},... | collective-permute-start | bytes 331784 | tf_op jit(solution)/shard_map/ppermute | solution.py:53
  58.8 4.5 %collective-permute-start.4 = (f32[256,1024]{1,0:T(8,128)}, f32[256,1024]{1,0:T(8,128)}, u32[]{:S(2)}, u32[]{:S(2)}) collective-permute-start(f32[256,1024]{1,0:T(8,128)} %constant_dynamic-slice_fusion.1), channel_id=1, source_target_pairs={{0,1},{1,0},{2,3},{3,2},{4,5},{5,4},{6,7},{7,6},{8,9},{9,8},{10,11... | collective-permute-start | bytes 3145736 | tf_op jit(solution)/shard_map/ppermute | solution.py:45
  58.8 57.7 %all-to-all-start.1 = ((bf16[16,2,3,32,576]{4,3,2,1,0:T(8,128)(2,1)}), bf16[16,2,3,32,576]{4,3,2,1,0:T(8,128)(2,1)}, u32[]{:S(2)}, u32[]{:S(2)}) async-start(bf16[16,2,3,32,576]{4,3,2,1,0:T(8,128)(2,1)} %broadcast_in_dim.64), calls=%async_computation.1 | async-start | bytes 7864320 | tf_op jit(solution)/shard_map/all_to_all | solution.py:103
  65.1 16.4 %collective-permute-start.5 = (bf16[256,1024]{1,0:T(8,128)(2,1)S(1)}, bf16[256,1024]{1,0:T(8,128)(2,1)S(1)}, u32[]{:S(2)}, u32[]{:S(2)}) collective-permute-start(bf16[256,1024]{1,0:T(8,128)(2,1)S(1)} %add_convert_fusion.3), channel_id=1, source_target_pairs={{0,2},{2,0},{1,3},{3,1},{4,6},{6,4},{5,7},{7,5},{8,10},{10,8},{9,1... | collective-permute-start | bytes 1572872 | tf_op jit(solution)/shard_map/ppermute | solution.py:49
  81.9 13.9 %collective-permute-start.6 = (bf16[256,1024]{1,0:T(8,128)(2,1)S(1)}, bf16[256,1024]{1,0:T(8,128)(2,1)S(1)}, u32[]{:S(2)}, u32[]{:S(2)}) collective-permute-start(bf16[256,1024]{1,0:T(8,128)(2,1)S(1)} %multiply_convert_fusion.1), channel_id=1, source_target_pairs={{0,16},{4,20},{8,24},{12,28},{16,0},{20,4},{24,8},{28,12},{32,48},... | collective-permute-start | bytes 1572872 | tf_op jit(solution)/shard_map/ppermute | solution.py:53
  130.1 4.2 %collective-permute-start.8 = (f32[512,1024]{1,0:T(8,128)S(1)}, f32[512,1024]{1,0:T(8,128)S(1)}, u32[]{:S(2)}, u32[]{:S(2)}) collective-permute-start(f32[512,1024]{1,0:T(8,128)S(1)} %get-tuple-element.44), channel_id=1, source_target_pairs={{0,1},{1,0},{2,3},{3,2},{4,5},{5,4},{6,7},{7,6},{8,9},{9,8},{10,11... | collective-permute-start | bytes 6291464 | tf_op jit(solution)/shard_map/ppermute | solution.py:45
  135.0 14.0 %collective-permute-start.9 = (bf16[256,1024]{1,0:T(8,128)(2,1)S(1)}, bf16[256,1024]{1,0:T(8,128)(2,1)S(1)}, u32[]{:S(2)}, u32[]{:S(2)}) collective-permute-start(bf16[256,1024]{1,0:T(8,128)(2,1)S(1)} %slice.234), channel_id=1, source_target_pairs={{0,16},{4,20},{8,24},{12,28},{16,0},{20,4},{24,8},{28,12},{32,48},... | collective-permute-start | bytes 1572872 | tf_op jit(solution)/shard_map/ppermute | solution.py:53
  149.2 15.4 %collective-permute-start.10 = (bf16[256,1024]{1,0:T(8,128)(2,1)S(1)}, bf16[256,1024]{1,0:T(8,128)(2,1)S(1)}, u32[]{:S(2)}, u32[]{:S(2)}) collective-permute-start(bf16[256,1024]{1,0:T(8,128)(2,1)S(1)} %add_convert_fusion.2), channel_id=1, source_target_pairs={{0,2},{2,0},{1,3},{3,1},{4,6},{6,4},{5,7},{7,5},{8,10},{10,8},{9,1... | collective-permute-start | bytes 1572872 | tf_op jit(solution)/shard_map/ppermute | solution.py:49
  166.2 12.1 %collective-permute-start.15 = (bf16[256,1024]{1,0:T(8,128)(2,1)}, bf16[256,1024]{1,0:T(8,128)(2,1)}, u32[]{:S(2)}, u32[]{:S(2)}) collective-permute-start(bf16[256,1024]{1,0:T(8,128)(2,1)} %fusion.41), channel_id=1, source_target_pairs={{0,1},{1,0},{2,3},{3,2},{4,5},{5,4},{6,7},{7,6},{8,9},{9,8},{10,11... | collective-permute-start | bytes 1572872 | tf_op jit(solution)/shard_map/ppermute | solution.py:45
  166.3 63.8 %all-to-all-start.2 = ((bf16[16,2,3,32,576]{4,3,2,1,0:T(8,128)(2,1)}), bf16[16,2,3,32,576]{4,3,2,1,0:T(8,128)(2,1)}, u32[]{:S(2)}, u32[]{:S(2)}) async-start(bf16[16,2,3,32,576]{4,3,2,1,0:T(8,128)(2,1)} %get-tuple-element.57), calls=%async_computation.2 | async-start | bytes 7864320 | tf_op jit(solution)/shard_map/all_to_all | solution.py:103
  178.1 22.7 %collective-permute-start.11 = (f32[512,1024]{1,0:T(8,128)}, f32[512,1024]{1,0:T(8,128)}, u32[]{:S(2)}, u32[]{:S(2)}) collective-permute-start(f32[512,1024]{1,0:T(8,128)} %copy-done.3), channel_id=1, source_target_pairs={{0,1},{1,0},{2,3},{3,2},{4,5},{5,4},{6,7},{7,6},{8,9},{9,8},{10,11... | collective-permute-start | bytes 6291464 | tf_op jit(solution)/shard_map/ppermute | solution.py:45
  197.5 16.3 %collective-permute-start.17 = (bf16[256,1024]{1,0:T(8,128)(2,1)S(1)}, bf16[256,1024]{1,0:T(8,128)(2,1)S(1)}, u32[]{:S(2)}, u32[]{:S(2)}) collective-permute-start(bf16[256,1024]{1,0:T(8,128)(2,1)S(1)} %add_convert_fusion.1), channel_id=1, source_target_pairs={{0,2},{2,0},{1,3},{3,1},{4,6},{6,4},{5,7},{7,5},{8,10},{10,8},{9,1... | collective-permute-start | bytes 1572872 | tf_op jit(solution)/shard_map/ppermute | solution.py:49
  202.9 22.2 %collective-permute-start.12 = (bf16[256,1024]{1,0:T(8,128)(2,1)S(1)}, bf16[256,1024]{1,0:T(8,128)(2,1)S(1)}, u32[]{:S(2)}, u32[]{:S(2)}) collective-permute-start(bf16[256,1024]{1,0:T(8,128)(2,1)S(1)} %slice.233), channel_id=1, source_target_pairs={{0,16},{4,20},{8,24},{12,28},{16,0},{20,4},{24,8},{28,12},{32,48},... | collective-permute-start | bytes 1572872 | tf_op jit(solution)/shard_map/ppermute | solution.py:53
  226.0 21.0 %collective-permute-start.13 = (bf16[256,1024]{1,0:T(8,128)(2,1)}, bf16[256,1024]{1,0:T(8,128)(2,1)}, u32[]{:S(2)}, u32[]{:S(2)}) collective-permute-start(bf16[256,1024]{1,0:T(8,128)(2,1)} %fusion.7), channel_id=1, source_target_pairs={{0,2},{2,0},{1,3},{3,1},{4,6},{6,4},{5,7},{7,5},{8,10},{10,8},{9,1... | collective-permute-start | bytes 1572872 | tf_op jit(solution)/shard_map/ppermute | solution.py:49
  230.1 45.2 %all-to-all-start.3 = ((bf16[16,2,32,1152]{3,2,1,0:T(8,128)(2,1)}), bf16[16,2,32,1152]{3,2,1,0:T(8,128)(2,1)}, u32[]{:S(2)}, u32[]{:S(2)}) async-start(bf16[16,2,32,1152]{3,2,1,0:T(8,128)(2,1)} %bitcast.136), calls=%async_computation.3 | async-start | bytes 4718592 | tf_op jit(solution)/shard_map/all_to_all | solution.py:103
  245.4 7.3 %collective-permute-start.20 = (f32[3,32,576]{2,1,0:T(8,128)S(1)}, f32[3,32,576]{2,1,0:T(8,128)S(1)}, u32[]{:S(2)}, u32[]{:S(2)}) collective-permute-start(f32[3,32,576]{2,1,0:T(8,128)S(1)} %dynamic-slice_bitcast_fusion.2), channel_id=1, source_target_pairs={{0,16},{4,20},{8,24},{12,28},{16,0},{20,4},{24,8},{28,12},{32,48},... | collective-permute-start | bytes 663560 | tf_op jit(solution)/shard_map/ppermute | solution.py:53
  249.1 5.8 %collective-permute-start.18 = (f32[256,1024]{1,0:T(8,128)S(1)}, f32[256,1024]{1,0:T(8,128)S(1)}, u32[]{:S(2)}, u32[]{:S(2)}) collective-permute-start(f32[256,1024]{1,0:T(8,128)S(1)} %get-tuple-element.138), channel_id=1, source_target_pairs={{0,1},{1,0},{2,3},{3,2},{4,5},{5,4},{6,7},{7,6},{8,9},{9,8},{10,11... | collective-permute-start | bytes 3145736 | tf_op jit(solution)/shard_map/ppermute | solution.py:45
  277.4 5.2 %collective-permute-start.19 = (f32[32,1152]{1,0:T(8,128)S(1)}, f32[32,1152]{1,0:T(8,128)S(1)}, u32[]{:S(2)}, u32[]{:S(2)}) collective-permute-start(f32[32,1152]{1,0:T(8,128)S(1)} %dynamic-slice_bitcast_fusion.3), channel_id=1, source_target_pairs={{0,16},{4,20},{8,24},{12,28},{16,0},{20,4},{24,8},{28,12},{32,48},... | collective-permute-start | bytes 442376 | tf_op jit(solution)/shard_map/ppermute | solution.py:53
  282.8 4.9 %collective-permute-start.21 = (f32[2,32]{1,0:T(2,128)S(1)}, f32[2,32]{1,0:T(2,128)S(1)}, u32[]{:S(2)}, u32[]{:S(2)}) collective-permute-start(f32[2,32]{1,0:T(2,128)S(1)} %reshape.254), channel_id=1, source_target_pairs={{0,1},{1,0},{2,3},{3,2},{4,5},{5,4},{6,7},{7,6},{8,9},{9,8},{10,11... | collective-permute-start | bytes 776 | tf_op jit(solution)/shard_map/ppermute | solution.py:45
  282.8 5.8 %collective-permute-start.22 = (f32[2,32]{1,0:T(2,128)S(1)}, f32[2,32]{1,0:T(2,128)S(1)}, u32[]{:S(2)}, u32[]{:S(2)}) collective-permute-start(f32[2,32]{1,0:T(2,128)S(1)} %reshape.254), channel_id=1, source_target_pairs={{0,2},{2,0},{1,3},{3,1},{4,6},{6,4},{5,7},{7,5},{8,10},{10,8},{9,1... | collective-permute-start | bytes 776 | tf_op jit(solution)/shard_map/ppermute | solution.py:49
  287.6 5.1 %collective-permute-start.23 = (f32[2,32]{1,0:T(2,128)S(1)}, f32[2,32]{1,0:T(2,128)S(1)}, u32[]{:S(2)}, u32[]{:S(2)}) collective-permute-start(f32[2,32]{1,0:T(2,128)S(1)} %collective-permute-done.21), channel_id=1, source_target_pairs={{0,2},{2,0},{1,3},{3,1},{4,6},{6,4},{5,7},{7,5},{8,10},{10,8},{9,1... | collective-permute-start | bytes 776 | tf_op jit(solution)/shard_map/ppermute | solution.py:49
  (74 other events, 572.3 us)

commit v3 on v2

--- a/solution.py
+++ b/solution.py
@@ -106,6 +106,12 @@
 def in_order(mine, theirs, near):
     first = near == 0
     return jnp.where(first, mine, theirs), jnp.where(first, theirs, mine)
+
+
+def whole_units(grad, near):
+    keep = lax.dynamic_index_in_dim(grad, near, 0, keepdims=False)
+    take = swap_near(lax.dynamic_index_in_dim(grad, 1 - near, 0, keepdims=False))
+    return jnp.concatenate(in_order(keep, take, near), axis=-1)
 
 
 VMEM_BYTES = 40 * 1024 * 1024
@@ -195,19 +201,30 @@
 
 
 def grads_kernel(
-    normed_ref, back_ref, gate_ref, up_ref, hidden_ref, down_ref, grads_ref, keep_ref, give_ref
+    normed_ref,
+    back_ref,
+    gate_ref,
+    up_ref,
+    hidden_ref,
+    down_ref,
+    pair_grad_ref,
+    down_grad_ref,
+    keep_ref,
+    give_ref,
 ):
     rows, units = down_ref.shape[3:]
-    normed, back, hidden = normed_ref[...], back_ref[...], hidden_ref[...]
-    for k, (left, right) in enumerate(
-        ((normed, gate_ref[...]), (normed, up_ref[...]), (back, hidden))
-    ):
-        grad = low(dot_columns(left, right))
+    plane = NY * rows
+    normed, hidden = normed_ref[...], hidden_ref[...]
+    for k, right in enumerate((gate_ref[...], up_ref[...])):
+        grad = low(dot_columns(normed, right))
         for z in range(NZ):
-            part = grad[z * NY * rows : (z + 1) * NY * rows]
-            grads_ref[:, z, k] = part.reshape(NY, rows, units)
+            part = grad[z * plane : (z + 1) * plane]
+            pair_grad_ref[:, z, k] = part.reshape(NY, rows, units)
+    grad = low(dot_columns(back_ref[...], hidden))
+    for z in range(NZ):
+        down_grad_ref[:, z] = grad[z * plane : (z + 1) * plane].reshape(NY, rows, units)
     down = jnp.concatenate(
-        [down_ref[:, z, 0].reshape(NY * rows, units) for z in range(NZ)], axis=0
+        [down_ref[:, z, 0].reshape(plane, units) for z in range(NZ)], axis=0
     )
     half = hidden.shape[0] // 2
     keep_ref[...] = dot_rows(hidden[:half], down)
@@ -216,7 +233,7 @@
 
 def grads_pass(normed, back, gate, up, hidden, weights):
     tokens, width = normed.shape
-    units = weights.shape[-1]
+    rows, units = weights.shape[3:]
     block = width // NX
     column = lambda i: (0, i)
     whole = lambda i: (0, 0)
@@ -230,14 +247,20 @@
             pl.BlockSpec((tokens, units), whole),
             pl.BlockSpec((tokens, units), whole),
             pl.BlockSpec((tokens, units), whole),
-            pl.BlockSpec((NY, NZ, 1) + weights.shape[3:], lambda i: (i, 0, 2, 0, 0)),
+            pl.BlockSpec((NY, NZ, 1, rows, units), lambda i: (i, 0, 2, 0, 0)),
         ],
         out_specs=[
-            pl.BlockSpec((NY,) + weights.shape[1:], lambda i: (i, 0, 0, 0, 0)),
+            pl.BlockSpec((NY, NZ, 2, rows, units), lambda i: (i, 0, 0, 0, 0)),
+            pl.BlockSpec((NY, NZ, rows, units), lambda i: (i, 0, 0, 0)),
             pl.BlockSpec((tokens // 2, block), column),
             pl.BlockSpec((tokens // 2, block), column),
         ],
-        out_shape=[jax.ShapeDtypeStruct(weights.shape, jnp.bfloat16), half, half],
+        out_shape=[
+            jax.ShapeDtypeStruct((NX * NY, NZ, 2, rows, units), jnp.bfloat16),
+            jax.ShapeDtypeStruct((NX * NY, NZ, rows, units), jnp.bfloat16),
+            half,
+            half,
+        ],
         compiler_params=pltpu.CompilerParams(vmem_limit_bytes=VMEM_BYTES),
         cost_estimate=pl.CostEstimate(
             flops=8 * tokens * width * units,
@@ -343,21 +366,23 @@
     normed_two_f, norm_two_pull = jax.vjp(rms_gain, middle, gains_value[1])
     normed_two = low(normed_two_f)
     normed_two = jnp.concatenate([normed_two, swap_near(normed_two)], axis=0)
+    normed_two, ffn_full = lax.optimization_barrier((normed_two, ffn_full))
     normed_two = jnp.concatenate([normed_two, swap_core(normed_two)], axis=0)
 
     back_gate, back_up, hidden, back_keep, back_give = hidden_pass(
         normed_two, back_four, ffn_full
     )
+    grad_pair, grad_down, ffn_keep, ffn_give = grads_pass(
+        normed_two, back_four, back_gate, back_up, hidden, ffn_full
+    )
     back_pair = back_keep + swap_core(back_give)
-    back_pair, back_gate, back_up, hidden = lax.optimization_barrier(
-        (back_pair, back_gate, back_up, hidden)
-    )
+    back_pair, grad_down = lax.optimization_barrier((back_pair, grad_down))
     back_normed_two = sum_depth(back_pair)
-    grad_ffn, ffn_keep, ffn_give = grads_pass(
-        normed_two, back_four, back_gate, back_up, hidden, ffn_full
-    )
-    grad_ffn = exchange(grad_ffn)
-
+    grad_down = exchange(grad_down)
+    back_normed_two, grad_down, grad_pair = lax.optimization_barrier(
+        (back_normed_two, grad_down, grad_pair)
+    )
+    grad_pair = exchange(grad_pair)
     ffn_keep, ffn_give, back_normed_two = lax.optimization_barrier(
         (ffn_keep, ffn_give, back_normed_two)
     )
@@ -376,6 +401,8 @@
     back_normed_one = product_of("tc,dc->td", back_projected, in_full)
     grad_gain_one = jnp.sum(back_normed_one * rms_gain(flat, 1.0), axis=0)
     grad_gains = jnp.stack([grad_gain_one, 0.5 * grad_gain_two])
+    grad_gains = grad_gains + swap_core(grad_gains)
+    grad_gains = grad_gains + swap_high(grad_gains)
     grad_gains = grad_gains.reshape(2, N_DP, own_rows).transpose(1, 0, 2).reshape(N_DP, -1)
     grad_conv = jnp.broadcast_to(grad_conv.reshape(1, -1), (N_DP, grad_conv.size))
     small_size = grad_gains.shape[1] + grad_conv.shape[1]
@@ -384,14 +411,12 @@
     small = jnp.concatenate(pieces(small) + [jnp.zeros((N_DP, own_rows - 24, 128), jnp.bfloat16)], axis=1)
     grad_mix = jnp.concatenate([low(grad_in), low(grad_out), small.reshape(width, 128)], axis=1)
     grad_mix = to_planes(grad_mix)
-    grad_ffn, grad_mix = lax.optimization_barrier((grad_ffn, grad_mix))
+    grad_pair, grad_mix = lax.optimization_barrier((grad_pair, grad_mix))
     red_mix = jnp.sum(wide(exchange(grad_mix)), axis=0)
     keep = lax.dynamic_index_in_dim(red_mix, near, 0, keepdims=False)
     red_mix = keep + swap_near(lax.dynamic_index_in_dim(red_mix, 1 - near, 0, keepdims=False))
-    grad_ffn = jnp.sum(wide(grad_ffn), axis=0)
-    keep = lax.dynamic_index_in_dim(grad_ffn, near, 0, keepdims=False)
-    take = swap_near(lax.dynamic_index_in_dim(grad_ffn, 1 - near, 0, keepdims=False))
-    red_ffn = jnp.concatenate(in_order(keep, take, near), axis=2)
+    red_down = whole_units(jnp.sum(wide(grad_down), axis=0), near).T
+    red_gate_up = whole_units(jnp.sum(wide(grad_pair), axis=0), near)
     back_normed_one = sum_four(back_normed_one, core)
     back_tokens_norm = jax.vjp(rms_gain, flat_half, gains_value[0])[1](back_normed_one)[0]
     back_tokens = back_middle + back_tokens_norm
@@ -399,14 +424,9 @@
 
     red_small = jnp.sum(red_mix[:24, mix_cols:].reshape(3, 1024), axis=0)
     red_gains = red_small[: norm_gains.size].reshape(norm_gains.shape)
-    twin_gains = swap_core(red_gains)
-    high_gains = swap_high(red_gains) + swap_high(twin_gains)
-    red_gains = (red_gains + twin_gains) + high_gains
     conv_total = red_small[norm_gains.size : small_size].reshape(conv_weight.shape)
     red_in = red_mix[:, : 3 * channels].reshape(-1, 3, channels).transpose(1, 0, 2)
     red_out = red_mix[:, 3 * channels : mix_cols].T
-    red_gate_up = red_ffn[:2]
-    red_down = red_ffn[2].T
     rate_wide = 0.8 / D**0.5
     rate_down = 0.8 / FF**0.5
     in_new = adam_step(in_weight, red_in, in_first, in_second, rate_wide, 0.1)

time: 294 us -> 290 us (0.986)
  waiting for transfers between devices: 139 us -> 129 us
  other arithmetic: 36.1 us -> 42.9 us
  starting transfers between devices: 63.5 us -> 60.5 us
    ppermute x8 -> x9, waiting for transfers between devices: 54.8 us -> 43.9 us  [swap_near(): return lax.ppermute(value, 'dp', NEAR_PAIRS)]
    ppermute x6 -> x5, waiting for transfers between devices: 26.1 us -> 36 us  [swap_high(): return lax.ppermute(value, 'tensor', HIGH_PAIRS)]
    all_to_all x4 -> x5, waiting for transfers between devices: 50.7 us -> 44.6 us  [exchange(): lax.all_to_all(blocks, 'dp', 0, 0, tiled=True, axis_index_groups=PLANES)]
    all_to_all x4 -> x5, starting transfers between devices: 35.2 us -> 31.9 us  [exchange(): lax.all_to_all(blocks, 'dp', 0, 0, tiled=True, axis_index_groups=PLANES)]
    unnamed x146 -> x161, local copies, waits for them, and re-layouts: 5.78 us -> 8.46 us
    ppermute x8 -> x9, starting transfers between devices: 11.4 us -> 10.7 us  [swap_near(): return lax.ppermute(value, 'dp', NEAR_PAIRS)]
    ppermute x6 -> x5, starting transfers between devices: 15.9 us -> 16.2 us  [swap_high(): return lax.ppermute(value, 'tensor', HIGH_PAIRS)]
  transfers between devices with their start and end apart: 28 -> 29, of which waited for: 19 -> 18; matrix products, arithmetic and copies ran while one was open for 15% -> 16% of each run, Pallas kernels for 3% -> 3%
where the time goes in v3:
time: 290 us; the launch traced here: 289 us
  waiting for transfers between devices  129 us (44%)
  starting transfers between devices  60.5 us (21%)
  other arithmetic  42.9 us (15%)
  local copies, waits for them, and re-layouts  23.8 us (8%)
  Pallas kernels  21.5 us (7%)
  matrix products  9.34 us (3%)
    all_to_all x5, waiting for transfers between devices, exchange(): lax.all_to_all(blocks, 'dp', 0, 0, tiled=True, axis_index_groups=PLANES)  44.6 us
    ppermute x9, waiting for transfers between devices, swap_near(): return lax.ppermute(value, 'dp', NEAR_PAIRS)  43.9 us
    ppermute x5, waiting for transfers between devices, swap_high(): return lax.ppermute(value, 'tensor', HIGH_PAIRS)  36 us
    all_to_all x5, starting transfers between devices, exchange(): lax.all_to_all(blocks, 'dp', 0, 0, tiled=True, axis_index_groups=PLANES)  31.9 us
    ppermute x5, starting transfers between devices, swap_high(): return lax.ppermute(value, 'tensor', HIGH_PAIRS)  16.2 us
    pallas_call x1, Pallas kernels, hidden_pass(): pl.pallas_call(hidden_kernel, grid=(4,), in_specs=[pl.BlockSpec((block, w...  11.9 us
    ppermute x9, starting transfers between devices, swap_near(): return lax.ppermute(value, 'dp', NEAR_PAIRS)  10.7 us
    pallas_call x1, Pallas kernels, grads_pass(): pl.pallas_call(grads_kernel, grid=(NX,), in_specs=[pl.BlockSpec((tokens,...  9.53 us
  transfers between devices with their start and end apart: 29, of which 18 were waited for; matrix products, arithmetic and copies ran while one was open for 16% of the time, Pallas kernels for 3%

profile of v3, /device:TPU:0, one launch (start us, length us, event | category | flops | bytes accessed | tf_op | source)
XLA Modules:
  0.0 289.1 jit_solution(3269003632388980762)
XLA Ops:
  9.3 7.3 %all-to-all-start = ((bf16[16,2,32,1152]{3,2,1,0:T(8,128)(2,1)}), bf16[16,2,32,1152]{3,2,1,0:T(8,128)(2,1)}, u32[]{:S(2)}, u32[]{:S(2)}) async-start(bf16[16,2,32,1152]{3,2,1,0:T(8,128)(2,1)} %broadcast_in_dim.62), calls=%async_computation | async-start | bytes 4718592 | tf_op jit(solution)/shard_map/all_to_all | solution.py:103
  20.8 10.4 %collective-permute-done.2 = bf16[256,1024]{1,0:T(8,128)(2,1)S(1)} collective-permute-done((bf16[256,1024]{1,0:T(8,128)(2,1)S(1)}, bf16[256,1024]{1,0:T(8,128)(2,1)S(1)}, u32[]{:S(2)}, u32[]{:S(2)}) %collective-permute-start.2) | collective-permute-done | bytes 524320 | tf_op jit(solution)/shard_map/ppermute | solution.py:53
  35.5 12.9 %all-to-all-done = bf16[16,2,32,1152]{3,2,1,0:T(8,128)(2,1)} async-done(((bf16[16,2,32,1152]{3,2,1,0:T(8,128)(2,1)}), bf16[16,2,32,1152]{3,2,1,0:T(8,128)(2,1)}, u32[]{:S(2)}, u32[]{:S(2)}) %all-to-all-start) | async-done | bytes 2359328 | tf_op jit(solution)/shard_map/all_to_all | solution.py:103
  57.8 4.5 %all-to-all-start.1 = ((bf16[16,2,3,32,576]{4,3,2,1,0:T(8,128)(2,1)}), bf16[16,2,3,32,576]{4,3,2,1,0:T(8,128)(2,1)}, u32[]{:S(2)}, u32[]{:S(2)}) async-start(bf16[16,2,3,32,576]{4,3,2,1,0:T(8,128)(2,1)} %broadcast_in_dim.64), calls=%async_computation.1 | async-start | bytes 7864320 | tf_op jit(solution)/shard_map/all_to_all | solution.py:103
  63.9 2.6 collective-permute-done.4
  66.7 3.8 %collective-permute-start.5 = (bf16[256,1024]{1,0:T(8,128)(2,1)S(1)}, bf16[256,1024]{1,0:T(8,128)(2,1)S(1)}, u32[]{:S(2)}, u32[]{:S(2)}) collective-permute-start(bf16[256,1024]{1,0:T(8,128)(2,1)S(1)} %add_convert_fusion.3), channel_id=1, source_target_pairs={{0,2},{2,0},{1,3},{3,1},{4,6},{6,4},{5,7},{7,5},{8,10},{10,8},{9,1... | collective-permute-start | bytes 1572872 | tf_op jit(solution)/shard_map/ppermute | solution.py:49
  70.8 12.0 %collective-permute-done.5 = bf16[256,1024]{1,0:T(8,128)(2,1)S(1)} collective-permute-done((bf16[256,1024]{1,0:T(8,128)(2,1)S(1)}, bf16[256,1024]{1,0:T(8,128)(2,1)S(1)}, u32[]{:S(2)}, u32[]{:S(2)}) %collective-permute-start.5) | collective-permute-done | bytes 524320 | tf_op jit(solution)/shard_map/ppermute | solution.py:49
  84.6 12.3 %collective-permute-done.6 = bf16[256,1024]{1,0:T(8,128)(2,1)S(1)} collective-permute-done((bf16[256,1024]{1,0:T(8,128)(2,1)S(1)}, bf16[256,1024]{1,0:T(8,128)(2,1)S(1)}, u32[]{:S(2)}, u32[]{:S(2)}) %collective-permute-start.6) | collective-permute-done | bytes 524320 | tf_op jit(solution)/shard_map/ppermute | solution.py:53
  97.9 11.7 %all-to-all-done.1.weights_ref.down_ref = bf16[16,2,3,32,576]{4,3,2,1,0:T(8,128)(2,1)} async-done(((bf16[16,2,3,32,576]{4,3,2,1,0:T(8,128)(2,1)}), bf16[16,2,3,32,576]{4,3,2,1,0:T(8,128)(2,1)}, u32[]{:S(2)}, u32[]{:S(2)}) %all-to-all-start.1) | async-done | bytes 3538976 | tf_op jit(solution)/shard_map/all_to_all | solution.py:103
  112.6 11.9 %hidden_pass.1 = (bf16[1024,576]{1,0:T(8,128)(2,1)S(1)}, bf16[1024,576]{1,0:T(8,128)(2,1)S(1)}, bf16[1024,576]{1,0:T(8,128)(2,1)S(1)}, f32[512,1024]{1,0:T(8,128)S(1)}, f32[512,1024]{1,0:T(8,128)S(1)}) custom-call(bf16[1024,1024]{1,0:T(8,128)(2,1)S(1)} %constant_dynamic-update-slice_fusion.2.normed_ref, bf16[1024,1024]{1,0:T(8,128)(2,1)S(1)} %pad_maximum_fusion.back_ref, ...), custom_call_target="tpu_custom_call" | custom-call | flops 6039797760 | bytes 16777216 | tf_op jit(solution)/shard_map/hidden_pass/pallas_call | solution.py:176
  126.5 9.5 %grads_pass.1 = (bf16[16,2,2,32,576]{4,3,2,1,0:T(8,128)(2,1)}, bf16[16,2,32,576]{3,2,1,0:T(8,128)(2,1)}, f32[512,1024]{1,0:T(8,128)S(1)}, f32[512,1024]{1,0:T(8,128)S(1)}) custom-call(bf16[1024,1024]{1,0:T(8,128)(2,1)S(1)} %constant_dynamic-update-slice_fusion.2.normed_ref, bf16[1024,1024]{1,0:T(8,128)(2,1)S(1)} %copy-done.1, ...), custom_call_target="tpu_custom_call" | custom-call | flops 4831838208 | bytes 14680064 | tf_op jit(solution)/shard_map/grads_pass/pallas_call | solution.py:241
  141.3 6.4 %all-to-all-start.2 = ((bf16[16,2,32,576]{3,2,1,0:T(8,128)(2,1)}), bf16[16,2,32,576]{3,2,1,0:T(8,128)(2,1)}, u32[]{:S(2)}, u32[]{:S(2)}) async-start(bf16[16,2,32,576]{3,2,1,0:T(8,128)(2,1)} %get-tuple-element.58), calls=%async_computation.2 | async-start | bytes 2621440 | tf_op jit(solution)/shard_map/all_to_all | solution.py:103
  147.8 6.4 %collective-permute-done.9 = bf16[256,1024]{1,0:T(8,128)(2,1)} collective-permute-done((bf16[256,1024]{1,0:T(8,128)(2,1)}, bf16[256,1024]{1,0:T(8,128)(2,1)}, u32[]{:S(2)}, u32[]{:S(2)}) %collective-permute-start.9) | collective-permute-done | bytes 524320 | tf_op jit(solution)/shard_map/ppermute | solution.py:53
  156.5 3.7 %collective-permute-start.10 = (bf16[256,1024]{1,0:T(8,128)(2,1)}, bf16[256,1024]{1,0:T(8,128)(2,1)}, u32[]{:S(2)}, u32[]{:S(2)}) collective-permute-start(bf16[256,1024]{1,0:T(8,128)(2,1)} %add_convert_fusion.2), channel_id=1, source_target_pairs={{0,2},{2,0},{1,3},{3,1},{4,6},{6,4},{5,7},{7,5},{8,10},{10,8},{9,1... | collective-permute-start | bytes 1572872 | tf_op jit(solution)/shard_map/ppermute | solution.py:49
  160.8 11.3 %collective-permute-done.10 = bf16[256,1024]{1,0:T(8,128)(2,1)} collective-permute-done((bf16[256,1024]{1,0:T(8,128)(2,1)}, bf16[256,1024]{1,0:T(8,128)(2,1)}, u32[]{:S(2)}, u32[]{:S(2)}) %collective-permute-start.10) | collective-permute-done | bytes 524320 | tf_op jit(solution)/shard_map/ppermute | solution.py:49
  179.7 6.4 %all-to-all-start.3 = ((bf16[16,2,2,32,576]{4,3,2,1,0:T(8,128)(2,1)}), bf16[16,2,2,32,576]{4,3,2,1,0:T(8,128)(2,1)}, u32[]{:S(2)}, u32[]{:S(2)}) async-start(bf16[16,2,2,32,576]{4,3,2,1,0:T(8,128)(2,1)} %get-tuple-element.64), calls=%async_computation.3 | async-start | bytes 5242880 | tf_op jit(solution)/shard_map/all_to_all | solution.py:103
  200.3 3.7 %collective-permute-start.20 = (f32[2,1024]{1,0:T(2,128)S(1)}, f32[2,1024]{1,0:T(2,128)S(1)}, u32[]{:S(2)}, u32[]{:S(2)}) collective-permute-start(f32[2,1024]{1,0:T(2,128)S(1)} %fusion.39), channel_id=1, source_target_pairs={{0,2},{2,0},{1,3},{3,1},{4,6},{6,4},{5,7},{7,5},{8,10},{10,8},{9,1... | collective-permute-start | bytes 24584 | tf_op jit(solution)/shard_map/ppermute | solution.py:49
  207.6 3.6 %collective-permute-start.17 = (bf16[256,1024]{1,0:T(8,128)(2,1)S(1)}, bf16[256,1024]{1,0:T(8,128)(2,1)S(1)}, u32[]{:S(2)}, u32[]{:S(2)}) collective-permute-start(bf16[256,1024]{1,0:T(8,128)(2,1)S(1)} %add_convert_fusion.1), channel_id=1, source_target_pairs={{0,2},{2,0},{1,3},{3,1},{4,6},{6,4},{5,7},{7,5},{8,10},{10,8},{9,1... | collective-permute-start | bytes 1572872 | tf_op jit(solution)/shard_map/ppermute | solution.py:49
  216.0 8.0 %collective-permute-done.17 = bf16[256,1024]{1,0:T(8,128)(2,1)S(1)} collective-permute-done((bf16[256,1024]{1,0:T(8,128)(2,1)S(1)}, bf16[256,1024]{1,0:T(8,128)(2,1)S(1)}, u32[]{:S(2)}, u32[]{:S(2)}) %collective-permute-start.17) | collective-permute-done | bytes 524320 | tf_op jit(solution)/shard_map/ppermute | solution.py:49
  224.4 9.3 %collective-permute-done.12 = bf16[256,1024]{1,0:T(8,128)(2,1)S(1)} collective-permute-done((bf16[256,1024]{1,0:T(8,128)(2,1)S(1)}, bf16[256,1024]{1,0:T(8,128)(2,1)S(1)}, u32[]{:S(2)}, u32[]{:S(2)}) %collective-permute-start.12) | collective-permute-done | bytes 524320 | tf_op jit(solution)/shard_map/ppermute | solution.py:53
  240.3 7.2 %all-to-all-start.4 = ((bf16[16,2,32,1152]{3,2,1,0:T(8,128)(2,1)}), bf16[16,2,32,1152]{3,2,1,0:T(8,128)(2,1)}, u32[]{:S(2)}, u32[]{:S(2)}) async-start(bf16[16,2,32,1152]{3,2,1,0:T(8,128)(2,1)} %bitcast.146), calls=%async_computation.4 | async-start | bytes 4718592 | tf_op jit(solution)/shard_map/all_to_all | solution.py:103
  247.5 3.2 %collective-permute-done.13 = bf16[256,1024]{1,0:T(8,128)(2,1)} collective-permute-done((bf16[256,1024]{1,0:T(8,128)(2,1)}, bf16[256,1024]{1,0:T(8,128)(2,1)}, u32[]{:S(2)}, u32[]{:S(2)}) %collective-permute-start.13) | collective-permute-done | bytes 524320 | tf_op jit(solution)/shard_map/ppermute | solution.py:49
  258.9 20.0 %all-to-all-done.4 = bf16[16,2,32,1152]{3,2,1,0:T(8,128)(2,1)} async-done(((bf16[16,2,32,1152]{3,2,1,0:T(8,128)(2,1)}), bf16[16,2,32,1152]{3,2,1,0:T(8,128)(2,1)}, u32[]{:S(2)}, u32[]{:S(2)}) %all-to-all-start.4) | async-done | bytes 2359328 | tf_op jit(solution)/shard_map/all_to_all | solution.py:103
  283.6 2.6 collective-permute-done.21
  (305 shorter events, 96.4 us)
Async XLA Ops:
  3.2 4.4 %collective-permute-start = (bf16[32,1152]{1,0:T(8,128)(2,1)S(1)}, bf16[32,1152]{1,0:T(8,128)(2,1)S(1)}, u32[]{:S(2)}, u32[]{:S(2)}) collective-permute-start(bf16[32,1152]{1,0:T(8,128)(2,1)S(1)} %constant_dynamic-update-slice_fusion), channel_id=1, source_target_pairs={{0,16},{4,20},{8,24},{12,28},{16,0},{20,4},{24,8},{28,12},{32,48},... | collective-permute-start | bytes 221192 | tf_op jit(solution)/shard_map/ppermute | solution.py:53
  9.3 39.1 %all-to-all-start = ((bf16[16,2,32,1152]{3,2,1,0:T(8,128)(2,1)}), bf16[16,2,32,1152]{3,2,1,0:T(8,128)(2,1)}, u32[]{:S(2)}, u32[]{:S(2)}) async-start(bf16[16,2,32,1152]{3,2,1,0:T(8,128)(2,1)} %broadcast_in_dim.62), calls=%async_computation | async-start | bytes 4718592 | tf_op jit(solution)/shard_map/all_to_all | solution.py:103
  17.5 13.7 %collective-permute-start.2 = (bf16[256,1024]{1,0:T(8,128)(2,1)S(1)}, bf16[256,1024]{1,0:T(8,128)(2,1)S(1)}, u32[]{:S(2)}, u32[]{:S(2)}) collective-permute-start(bf16[256,1024]{1,0:T(8,128)(2,1)S(1)} %get-tuple-element.151), channel_id=1, source_target_pairs={{0,16},{4,20},{8,24},{12,28},{16,0},{20,4},{24,8},{28,12},{32,48},... | collective-permute-start | bytes 1572872 | tf_op jit(solution)/shard_map/ppermute | solution.py:53
  19.6 12.9 %collective-permute-start.1 = (bf16[3,32,576]{2,1,0:T(8,128)(2,1)S(1)}, bf16[3,32,576]{2,1,0:T(8,128)(2,1)S(1)}, u32[]{:S(2)}, u32[]{:S(2)}) collective-permute-start(bf16[3,32,576]{2,1,0:T(8,128)(2,1)S(1)} %fusion.17), channel_id=1, source_target_pairs={{0,16},{4,20},{8,24},{12,28},{16,0},{20,4},{24,8},{28,12},{32,48},... | collective-permute-start | bytes 331784 | tf_op jit(solution)/shard_map/ppermute | solution.py:53
  57.8 51.8 %all-to-all-start.1 = ((bf16[16,2,3,32,576]{4,3,2,1,0:T(8,128)(2,1)}), bf16[16,2,3,32,576]{4,3,2,1,0:T(8,128)(2,1)}, u32[]{:S(2)}, u32[]{:S(2)}) async-start(bf16[16,2,3,32,576]{4,3,2,1,0:T(8,128)(2,1)} %broadcast_in_dim.64), calls=%async_computation.1 | async-start | bytes 7864320 | tf_op jit(solution)/shard_map/all_to_all | solution.py:103
  66.7 16.0 %collective-permute-start.5 = (bf16[256,1024]{1,0:T(8,128)(2,1)S(1)}, bf16[256,1024]{1,0:T(8,128)(2,1)S(1)}, u32[]{:S(2)}, u32[]{:S(2)}) collective-permute-start(bf16[256,1024]{1,0:T(8,128)(2,1)S(1)} %add_convert_fusion.3), channel_id=1, source_target_pairs={{0,2},{2,0},{1,3},{3,1},{4,6},{6,4},{5,7},{7,5},{8,10},{10,8},{9,1... | collective-permute-start | bytes 1572872 | tf_op jit(solution)/shard_map/ppermute | solution.py:49
  83.2 13.6 %collective-permute-start.6 = (bf16[256,1024]{1,0:T(8,128)(2,1)S(1)}, bf16[256,1024]{1,0:T(8,128)(2,1)S(1)}, u32[]{:S(2)}, u32[]{:S(2)}) collective-permute-start(bf16[256,1024]{1,0:T(8,128)(2,1)S(1)} %multiply_convert_fusion.1), channel_id=1, source_target_pairs={{0,16},{4,20},{8,24},{12,28},{16,0},{20,4},{24,8},{28,12},{32,48},... | collective-permute-start | bytes 1572872 | tf_op jit(solution)/shard_map/ppermute | solution.py:53
  124.5 11.5 %collective-permute-start.8 = (f32[512,1024]{1,0:T(8,128)S(1)}, f32[512,1024]{1,0:T(8,128)S(1)}, u32[]{:S(2)}, u32[]{:S(2)}) collective-permute-start(f32[512,1024]{1,0:T(8,128)S(1)} %get-tuple-element.55), channel_id=1, source_target_pairs={{0,1},{1,0},{2,3},{3,2},{4,5},{5,4},{6,7},{7,6},{8,9},{9,8},{10,11... | collective-permute-start | bytes 6291464 | tf_op jit(solution)/shard_map/ppermute | solution.py:45
  139.6 14.5 %collective-permute-start.9 = (bf16[256,1024]{1,0:T(8,128)(2,1)}, bf16[256,1024]{1,0:T(8,128)(2,1)}, u32[]{:S(2)}, u32[]{:S(2)}) collective-permute-start(bf16[256,1024]{1,0:T(8,128)(2,1)} %slice.210), channel_id=1, source_target_pairs={{0,16},{4,20},{8,24},{12,28},{16,0},{20,4},{24,8},{28,12},{32,48},... | collective-permute-start | bytes 1572872 | tf_op jit(solution)/shard_map/ppermute | solution.py:53
  141.3 33.2 %all-to-all-start.2 = ((bf16[16,2,32,576]{3,2,1,0:T(8,128)(2,1)}), bf16[16,2,32,576]{3,2,1,0:T(8,128)(2,1)}, u32[]{:S(2)}, u32[]{:S(2)}) async-start(bf16[16,2,32,576]{3,2,1,0:T(8,128)(2,1)} %get-tuple-element.58), calls=%async_computation.2 | async-start | bytes 2621440 | tf_op jit(solution)/shard_map/all_to_all | solution.py:103
  156.5 15.6 %collective-permute-start.10 = (bf16[256,1024]{1,0:T(8,128)(2,1)}, bf16[256,1024]{1,0:T(8,128)(2,1)}, u32[]{:S(2)}, u32[]{:S(2)}) collective-permute-start(bf16[256,1024]{1,0:T(8,128)(2,1)} %add_convert_fusion.2), channel_id=1, source_target_pairs={{0,2},{2,0},{1,3},{3,1},{4,6},{6,4},{5,7},{7,5},{8,10},{10,8},{9,1... | collective-permute-start | bytes 1572872 | tf_op jit(solution)/shard_map/ppermute | solution.py:49
  177.7 10.3 %collective-permute-start.15 = (bf16[256,1024]{1,0:T(8,128)(2,1)}, bf16[256,1024]{1,0:T(8,128)(2,1)}, u32[]{:S(2)}, u32[]{:S(2)}) collective-permute-start(bf16[256,1024]{1,0:T(8,128)(2,1)} %fusion.40), channel_id=1, source_target_pairs={{0,1},{1,0},{2,3},{3,2},{4,5},{5,4},{6,7},{7,6},{8,9},{9,8},{10,11... | collective-permute-start | bytes 1572872 | tf_op jit(solution)/shard_map/ppermute | solution.py:45
  177.7 8.6 %collective-permute-start.23 = (f32[32,576]{1,0:T(8,128)S(1)}, f32[32,576]{1,0:T(8,128)}, u32[]{:S(2)}, u32[]{:S(2)}) collective-permute-start(f32[32,576]{1,0:T(8,128)S(1)} %dynamic-slice_bitcast_fusion.4), channel_id=1, source_target_pairs={{0,16},{4,20},{8,24},{12,28},{16,0},{20,4},{24,8},{28,12},{32,48},... | collective-permute-start | bytes 221192 | tf_op jit(solution)/shard_map/ppermute | solution.py:53
  179.7 57.1 %all-to-all-start.3 = ((bf16[16,2,2,32,576]{4,3,2,1,0:T(8,128)(2,1)}), bf16[16,2,2,32,576]{4,3,2,1,0:T(8,128)(2,1)}, u32[]{:S(2)}, u32[]{:S(2)}) async-start(bf16[16,2,2,32,576]{4,3,2,1,0:T(8,128)(2,1)} %get-tuple-element.64), calls=%async_computation.3 | async-start | bytes 5242880 | tf_op jit(solution)/shard_map/all_to_all | solution.py:103
  186.2 25.1 %collective-permute-start.11 = (f32[512,1024]{1,0:T(8,128)}, f32[512,1024]{1,0:T(8,128)}, u32[]{:S(2)}, u32[]{:S(2)}) collective-permute-start(f32[512,1024]{1,0:T(8,128)} %copy-done.2), channel_id=1, source_target_pairs={{0,1},{1,0},{2,3},{3,2},{4,5},{5,4},{6,7},{7,6},{8,9},{9,8},{10,11... | collective-permute-start | bytes 6291464 | tf_op jit(solution)/shard_map/ppermute | solution.py:45
  194.9 5.3 %collective-permute-start.19 = (f32[2,1024]{1,0:T(2,128)S(1)}, f32[2,1024]{1,0:T(2,128)S(1)}, u32[]{:S(2)}, u32[]{:S(2)}) collective-permute-start(f32[2,1024]{1,0:T(2,128)S(1)} %pad_maximum_fusion.9), channel_id=1, source_target_pairs={{0,1},{1,0},{2,3},{3,2},{4,5},{5,4},{6,7},{7,6},{8,9},{9,8},{10,11... | collective-permute-start | bytes 24584 | tf_op jit(solution)/shard_map/ppermute | solution.py:45
  200.1 5.8 %collective-permute-start.16 = (f32[256,1024]{1,0:T(8,128)}, f32[256,1024]{1,0:T(8,128)}, u32[]{:S(2)}, u32[]{:S(2)}) collective-permute-start(f32[256,1024]{1,0:T(8,128)} %constant_dynamic-slice_fusion), channel_id=1, source_target_pairs={{0,1},{1,0},{2,3},{3,2},{4,5},{5,4},{6,7},{7,6},{8,9},{9,8},{10,11... | collective-permute-start | bytes 3145736 | tf_op jit(solution)/shard_map/ppermute | solution.py:45
  200.3 5.3 %collective-permute-start.20 = (f32[2,1024]{1,0:T(2,128)S(1)}, f32[2,1024]{1,0:T(2,128)S(1)}, u32[]{:S(2)}, u32[]{:S(2)}) collective-permute-start(f32[2,1024]{1,0:T(2,128)S(1)} %fusion.39), channel_id=1, source_target_pairs={{0,2},{2,0},{1,3},{3,1},{4,6},{6,4},{5,7},{7,5},{8,10},{10,8},{9,1... | collective-permute-start | bytes 24584 | tf_op jit(solution)/shard_map/ppermute | solution.py:49
  207.6 16.4 %collective-permute-start.17 = (bf16[256,1024]{1,0:T(8,128)(2,1)S(1)}, bf16[256,1024]{1,0:T(8,128)(2,1)S(1)}, u32[]{:S(2)}, u32[]{:S(2)}) collective-permute-start(bf16[256,1024]{1,0:T(8,128)(2,1)S(1)} %add_convert_fusion.1), channel_id=1, source_target_pairs={{0,2},{2,0},{1,3},{3,1},{4,6},{6,4},{5,7},{7,5},{8,10},{10,8},{9,1... | collective-permute-start | bytes 1572872 | tf_op jit(solution)/shard_map/ppermute | solution.py:49
  213.4 20.2 %collective-permute-start.12 = (bf16[256,1024]{1,0:T(8,128)(2,1)S(1)}, bf16[256,1024]{1,0:T(8,128)(2,1)S(1)}, u32[]{:S(2)}, u32[]{:S(2)}) collective-permute-start(bf16[256,1024]{1,0:T(8,128)(2,1)S(1)} %slice.209), channel_id=1, source_target_pairs={{0,16},{4,20},{8,24},{12,28},{16,0},{20,4},{24,8},{28,12},{32,48},... | collective-permute-start | bytes 1572872 | tf_op jit(solution)/shard_map/ppermute | solution.py:53
  234.6 16.1 %collective-permute-start.13 = (bf16[256,1024]{1,0:T(8,128)(2,1)}, bf16[256,1024]{1,0:T(8,128)(2,1)}, u32[]{:S(2)}, u32[]{:S(2)}) collective-permute-start(bf16[256,1024]{1,0:T(8,128)(2,1)} %fusion.7), channel_id=1, source_target_pairs={{0,2},{2,0},{1,3},{3,1},{4,6},{6,4},{5,7},{7,5},{8,10},{10,8},{9,1... | collective-permute-start | bytes 1572872 | tf_op jit(solution)/shard_map/ppermute | solution.py:49
  239.6 15.3 %collective-permute-start.22 = (f32[2,32,576]{2,1,0:T(8,128)}, f32[2,32,576]{2,1,0:T(8,128)}, u32[]{:S(2)}, u32[]{:S(2)}) collective-permute-start(f32[2,32,576]{2,1,0:T(8,128)} %dynamic-slice_bitcast_fusion.2), channel_id=1, source_target_pairs={{0,16},{4,20},{8,24},{12,28},{16,0},{20,4},{24,8},{28,12},{32,48},... | collective-permute-start | bytes 442376 | tf_op jit(solution)/shard_map/ppermute | solution.py:53
  240.3 38.6 %all-to-all-start.4 = ((bf16[16,2,32,1152]{3,2,1,0:T(8,128)(2,1)}), bf16[16,2,32,1152]{3,2,1,0:T(8,128)(2,1)}, u32[]{:S(2)}, u32[]{:S(2)}) async-start(bf16[16,2,32,1152]{3,2,1,0:T(8,128)(2,1)} %bitcast.146), calls=%async_computation.4 | async-start | bytes 4718592 | tf_op jit(solution)/shard_map/all_to_all | solution.py:103
  281.0 5.2 %collective-permute-start.21 = (f32[32,1152]{1,0:T(8,128)S(1)}, f32[32,1152]{1,0:T(8,128)S(1)}, u32[]{:S(2)}, u32[]{:S(2)}) collective-permute-start(f32[32,1152]{1,0:T(8,128)S(1)} %dynamic-slice_bitcast_fusion.3), channel_id=1, source_target_pairs={{0,16},{4,20},{8,24},{12,28},{16,0},{20,4},{24,8},{28,12},{32,48},... | collective-permute-start | bytes 442376 | tf_op jit(solution)/shard_map/ppermute | solution.py:53
  (82 other events, 785.7 us)

commit v4 on v3

--- a/solution.py
+++ b/solution.py
@@ -86,11 +86,6 @@
 def sum_four(part, core):
     own, other = halves(part, core)
     return across_high(own + swap_core(other))
-
-
-def sum_depth(pair):
-    half = pair.shape[0] // 2
-    return across_high(pair[:half] + wide(swap_near(low(pair[half:]))))
 
 
 def to_planes(grad):
@@ -207,22 +202,19 @@
     up_ref,
     hidden_ref,
     down_ref,
-    pair_grad_ref,
-    down_grad_ref,
+    grads_ref,
     keep_ref,
     give_ref,
 ):
     rows, units = down_ref.shape[3:]
     plane = NY * rows
     normed, hidden = normed_ref[...], hidden_ref[...]
-    for k, right in enumerate((gate_ref[...], up_ref[...])):
-        grad = low(dot_columns(normed, right))
+    pairs = ((normed, gate_ref[...]), (normed, up_ref[...]), (back_ref[...], hidden))
+    for k, (left, right) in enumerate(pairs):
+        grad = low(dot_columns(left, right))
         for z in range(NZ):
             part = grad[z * plane : (z + 1) * plane]
-            pair_grad_ref[:, z, k] = part.reshape(NY, rows, units)
-    grad = low(dot_columns(back_ref[...], hidden))
-    for z in range(NZ):
-        down_grad_ref[:, z] = grad[z * plane : (z + 1) * plane].reshape(NY, rows, units)
+            grads_ref[:, z, k] = part.reshape(NY, rows, units)
     down = jnp.concatenate(
         [down_ref[:, z, 0].reshape(plane, units) for z in range(NZ)], axis=0
     )
@@ -250,14 +242,12 @@
             pl.BlockSpec((NY, NZ, 1, rows, units), lambda i: (i, 0, 2, 0, 0)),
         ],
         out_specs=[
-            pl.BlockSpec((NY, NZ, 2, rows, units), lambda i: (i, 0, 0, 0, 0)),
-            pl.BlockSpec((NY, NZ, rows, units), lambda i: (i, 0, 0, 0)),
+            pl.BlockSpec((NY, NZ, 3, rows, units), lambda i: (i, 0, 0, 0, 0)),
             pl.BlockSpec((tokens // 2, block), column),
             pl.BlockSpec((tokens // 2, block), column),
         ],
         out_shape=[
-            jax.ShapeDtypeStruct((NX * NY, NZ, 2, rows, units), jnp.bfloat16),
-            jax.ShapeDtypeStruct((NX * NY, NZ, rows, units), jnp.bfloat16),
+            jax.ShapeDtypeStruct(weights.shape, jnp.bfloat16),
             half,
             half,
         ],
@@ -269,6 +259,111 @@
         ),
         name="grads_pass",
     )(normed, back, gate, up, hidden, weights)
+
+
+def mixer_kernel(
+    branch_ref,
+    weights_ref,
+    projected_ref,
+    masks_ref,
+    taps_ref,
+    gated_ref,
+    scale_ref,
+    branch_part_ref,
+    weights_part_ref,
+    normed_ref,
+    tokens_ref,
+    grads_ref,
+    back_ref,
+    gain_ref,
+    conv_ref,
+    held,
+):
+    channels = gated_ref.shape[1]
+    rows = grads_ref.shape[2]
+
+    @pl.when(pl.program_id(0) == 0)
+    def _():
+        count = branch_ref.shape[0]
+        back = dot_plain(branch_ref[...], weights_ref[:, 3 * channels : 4 * channels])
+        b_part = projected_ref[:, :channels]
+        c_part = projected_ref[:, channels : 2 * channels]
+        x_part = projected_ref[:, 2 * channels :]
+        tap_zero, tap_one, tap_two = taps_ref[0:1], taps_ref[1:2], taps_ref[2:3]
+        one, two = masks_ref[:, 0:1] > 0.0, masks_ref[:, 1:2] > 0.0
+        product = b_part * x_part
+        first = jnp.where(one, pltpu.roll(product, 1, 0), 0.0)
+        second = jnp.where(two, pltpu.roll(product, 2, 0), 0.0)
+        conv_sum = tap_zero * product + tap_one * first + tap_two * second
+        grad = back * c_part
+        conv_ref[0:1] = jnp.sum(grad * product, axis=0, keepdims=True)
+        conv_ref[1:2] = jnp.sum(grad * first, axis=0, keepdims=True)
+        conv_ref[2:3] = jnp.sum(grad * second, axis=0, keepdims=True)
+        back_product = tap_zero * grad
+        back_product += tap_one * pltpu.roll(jnp.where(one, grad, 0.0), count - 1, 0)
+        back_product += tap_two * pltpu.roll(jnp.where(two, grad, 0.0), count - 2, 0)
+        held[:, :channels] = low(back_product * x_part)
+        held[:, channels : 2 * channels] = low(back * conv_sum)
+        held[:, 2 * channels :] = low(back_product * b_part)
+
+    back_projected = held[...]
+    plane = NY * rows
+    grad_in = low(dot_columns(normed_ref[...], back_projected))
+    grad_out = low(dot_columns(branch_part_ref[...], gated_ref[...]))
+    for z in range(NZ):
+        part = slice(z * plane, (z + 1) * plane)
+        grads_ref[:, z, :, : 3 * channels] = grad_in[part].reshape(NY, rows, 3 * channels)
+        grads_ref[:, z, :, 3 * channels :] = grad_out[part].reshape(NY, rows, channels)
+    back_normed = dot_rows(back_projected, weights_part_ref[:, : 3 * channels])
+    back_ref[...] = back_normed
+    unit = tokens_ref[...].astype(jnp.float32) * scale_ref[...]
+    gain_ref[...] = jnp.sum(back_normed * unit, axis=0, keepdims=True)
+
+
+def mixer_pass(branch, weights, projected, masks, taps, gated, scale, normed, tokens):
+    count, width = branch.shape
+    channels = gated.shape[1]
+    rows = width // N_DP
+    block = width // NX
+    whole = lambda i: (0, 0)
+    column = pl.BlockSpec((count, block), lambda i: (0, i))
+    return pl.pallas_call(
+        mixer_kernel,
+        grid=(NX,),
+        in_specs=[
+            pl.BlockSpec(branch.shape, whole),
+            pl.BlockSpec(weights.shape, whole),
+            pl.BlockSpec(projected.shape, whole),
+            pl.BlockSpec(masks.shape, whole),
+            pl.BlockSpec(taps.shape, whole),
+            pl.BlockSpec(gated.shape, whole),
+            pl.BlockSpec(scale.shape, whole),
+            column,
+            pl.BlockSpec((block, weights.shape[1]), lambda i: (i, 0)),
+            column,
+            column,
+        ],
+        out_specs=[
+            pl.BlockSpec((NY, NZ, rows, 4 * channels), lambda i: (i, 0, 0, 0)),
+            column,
+            pl.BlockSpec((1, block), lambda i: (0, i)),
+            pl.BlockSpec(taps.shape, whole),
+        ],
+        out_shape=[
+            jax.ShapeDtypeStruct((NX * NY, NZ, rows, 4 * channels), jnp.bfloat16),
+            jax.ShapeDtypeStruct((count, width), jnp.float32),
+            jax.ShapeDtypeStruct((1, width), jnp.float32),
+            jax.ShapeDtypeStruct(taps.shape, jnp.float32),
+        ],
+        scratch_shapes=[pltpu.VMEM((count, 3 * channels), jnp.bfloat16)],
+        compiler_params=pltpu.CompilerParams(vmem_limit_bytes=VMEM_BYTES),
+        cost_estimate=pl.CostEstimate(
+            flops=16 * count * width * channels,
+            bytes_accessed=20 * count * width,
+            transcendentals=0,
+        ),
+        name="mixer_pass",
+    )(branch, weights, projected, masks, taps, gated, scale, branch, weights, normed, tokens)
 
 
 def pieces(value):
@@ -333,22 +428,26 @@
     back_near = swap_near(back_own)
     back_four = jnp.concatenate([back_own, back_near, back_other, swap_core(back_near)], axis=0)
 
-    low_mix = jnp.stack(in_order(low_mix, swap_near(low_mix), near), axis=0)
-    mix_full = exchange(jnp.broadcast_to(low_mix[None], (NX * NY,) + low_mix.shape))
-    mix_full, ffn_copies, back_four = lax.optimization_barrier((mix_full, ffn_copies, back_four))
-    ffn_full = exchange(ffn_copies)
-    mix_full = mix_full.reshape(NX, NY, NZ, own_rows, -1).transpose(0, 2, 1, 3, 4).reshape(width, -1)
-    in_full = mix_full[:, : 3 * channels]
-    out_full = mix_full[:, 3 * channels : mix_cols]
-    gains_value = wide(mix_full[:, mix_cols : mix_cols + 2]).T
-
-
     flat = wide(tokens_in.reshape(count, width))
     flat_half = halves(flat, core)[0]
     seg_flat = segment_ids.reshape(count)
     place = lax.iota(jnp.int32, count) % length
     mask_one = ((place >= 1) & (seg_flat == jnp.roll(seg_flat, 1)))[:, None]
     mask_two = ((place >= 2) & (seg_flat == jnp.roll(seg_flat, 2)))[:, None]
+    masks = wide(jnp.concatenate([mask_one, mask_two], axis=1))
+    scale_one = lax.rsqrt(jnp.mean(flat * flat, axis=-1, keepdims=True) + epsilon_norm)
+
+    low_mix = jnp.stack(in_order(low_mix, swap_near(low_mix), near), axis=0)
+    mix_full = exchange(jnp.broadcast_to(low_mix[None], (NX * NY,) + low_mix.shape))
+    mix_full, ffn_copies, back_four, masks, scale_one = lax.optimization_barrier(
+        (mix_full, ffn_copies, back_four, masks, scale_one)
+    )
+    ffn_full = exchange(ffn_copies)
+    mix_full = mix_full.reshape(NX, NY, NZ, own_rows, -1).transpose(0, 2, 1, 3, 4).reshape(width, -1)
+    in_full = mix_full[:, : 3 * channels]
+    out_full = mix_full[:, 3 * channels : mix_cols]
+    gains_value = wide(mix_full[:, mix_cols : mix_cols + 2]).T
+
 
     def mixer_local(projected, taps):
         product = projected[:, :channels] * projected[:, 2 * channels :]
@@ -360,8 +459,7 @@
 
     normed_one = low(rms_gain(flat, gains_value[0]))
     projected = product_of("td,dc->tc", normed_one, in_full)
-    gated_f, mixer_pull = jax.vjp(mixer_local, projected, conv_weight)
-    gated = low(gated_f)
+    gated = low(mixer_local(projected, conv_weight))
     middle = flat_half + sum_four(product_of("tc,dc->td", gated, out_full), core)
     normed_two_f, norm_two_pull = jax.vjp(rms_gain, middle, gains_value[1])
     normed_two = low(normed_two_f)
@@ -372,61 +470,74 @@
     back_gate, back_up, hidden, back_keep, back_give = hidden_pass(
         normed_two, back_four, ffn_full
     )
-    grad_pair, grad_down, ffn_keep, ffn_give = grads_pass(
+    back_pair = back_keep + swap_core(back_give)
+    back_pair, back_gate, back_up, hidden = lax.optimization_barrier(
+        (back_pair, back_gate, back_up, hidden)
+    )
+    grad_ffn, ffn_keep, ffn_give = grads_pass(
         normed_two, back_four, back_gate, back_up, hidden, ffn_full
     )
-    back_pair = back_keep + swap_core(back_give)
-    back_pair, grad_down = lax.optimization_barrier((back_pair, grad_down))
-    back_normed_two = sum_depth(back_pair)
-    grad_down = exchange(grad_down)
-    back_normed_two, grad_down, grad_pair = lax.optimization_barrier(
-        (back_normed_two, grad_down, grad_pair)
-    )
-    grad_pair = exchange(grad_pair)
+    back_normed_two = back_pair[: count // 2] + wide(swap_near(low(back_pair[count // 2 :])))
+    back_normed_two, grad_ffn = lax.optimization_barrier((back_normed_two, grad_ffn))
+    back_normed_two = across_high(back_normed_two)
+    grad_ffn = exchange(grad_ffn)
+
     ffn_keep, ffn_give, back_normed_two = lax.optimization_barrier(
         (ffn_keep, ffn_give, back_normed_two)
     )
-    result = middle + sum_depth(ffn_keep + swap_core(ffn_give))
-    result = joined(result, swap_core(result), core)
+    ffn_pair = ffn_keep + swap_core(ffn_give)
+    ffn_half = ffn_pair[: count // 2] + wide(swap_near(low(ffn_pair[count // 2 :])))
 
     back_middle_norm, grad_gain_two = norm_two_pull(back_normed_two)
     back_middle = wide(back_own) + back_middle_norm
     back_branch = low(back_middle)
     back_branch = joined(back_branch, swap_core(back_branch), core)
-    grad_out = product_of("td,tc->dc", back_branch, gated)
-    back_gated = product_of("td,dc->tc", back_branch, out_full)
-    back_projected_f, grad_conv = mixer_pull(back_gated)
-    back_projected = low(back_projected_f)
-    grad_in = product_of("td,tc->dc", normed_one, back_projected)
-    back_normed_one = product_of("tc,dc->td", back_projected, in_full)
-    grad_gain_one = jnp.sum(back_normed_one * rms_gain(flat, 1.0), axis=0)
-    grad_gains = jnp.stack([grad_gain_one, 0.5 * grad_gain_two])
-    grad_gains = grad_gains + swap_core(grad_gains)
-    grad_gains = grad_gains + swap_high(grad_gains)
+    grad_mix, back_normed_one, grad_gain_one, grad_conv = mixer_pass(
+        back_branch,
+        mix_full,
+        projected,
+        masks,
+        conv_weight,
+        gated,
+        scale_one,
+        normed_one,
+        tokens_in.reshape(count, width),
+    )
+    grad_gains = jnp.concatenate([grad_gain_one, 0.5 * grad_gain_two[None]], axis=0)
     grad_gains = grad_gains.reshape(2, N_DP, own_rows).transpose(1, 0, 2).reshape(N_DP, -1)
     grad_conv = jnp.broadcast_to(grad_conv.reshape(1, -1), (N_DP, grad_conv.size))
     small_size = grad_gains.shape[1] + grad_conv.shape[1]
     small = jnp.concatenate([grad_gains, grad_conv], axis=1)
     small = jnp.pad(small, ((0, 0), (0, 1024 - small_size))).reshape(N_DP, 8, 128)
-    small = jnp.concatenate(pieces(small) + [jnp.zeros((N_DP, own_rows - 24, 128), jnp.bfloat16)], axis=1)
-    grad_mix = jnp.concatenate([low(grad_in), low(grad_out), small.reshape(width, 128)], axis=1)
-    grad_mix = to_planes(grad_mix)
-    grad_pair, grad_mix = lax.optimization_barrier((grad_pair, grad_mix))
+    small = jnp.concatenate(
+        pieces(small) + [jnp.zeros((N_DP, own_rows - 24, 128), jnp.bfloat16)], axis=1
+    )
+    grad_mix = jnp.concatenate([grad_mix, to_planes(small.reshape(width, 128))], axis=3)
+    own, other = halves(back_normed_one, core)
+    back_normed_one = own + swap_core(other)
+    grad_ffn, grad_mix, back_normed_one = lax.optimization_barrier(
+        (grad_ffn, grad_mix, back_normed_one)
+    )
     red_mix = jnp.sum(wide(exchange(grad_mix)), axis=0)
     keep = lax.dynamic_index_in_dim(red_mix, near, 0, keepdims=False)
     red_mix = keep + swap_near(lax.dynamic_index_in_dim(red_mix, 1 - near, 0, keepdims=False))
-    red_down = whole_units(jnp.sum(wide(grad_down), axis=0), near).T
-    red_gate_up = whole_units(jnp.sum(wide(grad_pair), axis=0), near)
-    back_normed_one = sum_four(back_normed_one, core)
+    back_normed_one = across_high(back_normed_one)
+    grad_ffn, back_normed_one = lax.optimization_barrier((grad_ffn, back_normed_one))
+    red_ffn = whole_units(jnp.sum(wide(grad_ffn), axis=0), near)
+    result = middle + across_high(ffn_half)
+    result = joined(result, swap_core(result), core)
     back_tokens_norm = jax.vjp(rms_gain, flat_half, gains_value[0])[1](back_normed_one)[0]
     back_tokens = back_middle + back_tokens_norm
     back_tokens = joined(back_tokens, swap_core(back_tokens), core)
 
     red_small = jnp.sum(red_mix[:24, mix_cols:].reshape(3, 1024), axis=0)
     red_gains = red_small[: norm_gains.size].reshape(norm_gains.shape)
+    red_gains = jnp.sum(lax.all_gather(red_gains, "tensor"), axis=0)
     conv_total = red_small[norm_gains.size : small_size].reshape(conv_weight.shape)
     red_in = red_mix[:, : 3 * channels].reshape(-1, 3, channels).transpose(1, 0, 2)
     red_out = red_mix[:, 3 * channels : mix_cols].T
+    red_gate_up = red_ffn[:2]
+    red_down = red_ffn[2].T
     rate_wide = 0.8 / D**0.5
     rate_down = 0.8 / FF**0.5
     in_new = adam_step(in_weight, red_in, in_first, in_second, rate_wide, 0.1)

time: 290 us -> 270 us (0.931)
  starting transfers between devices: 60.5 us -> 41.8 us
  waiting for transfers between devices: 129 us -> 116 us
  blocking collectives: 0 us -> 6.56 us
  matrix products: 9.34 us -> 2.79 us
  Pallas kernels: 21.5 us -> 26.2 us
  other arithmetic: 42.9 us -> 46.2 us
    ppermute x9 -> x8, waiting for transfers between devices: 43.9 us -> 20.3 us  [swap_near(): return lax.ppermute(value, 'dp', NEAR_PAIRS)]
    all_to_all x5 -> x4, waiting for transfers between devices: 44.6 us -> 59.9 us  [exchange(): lax.all_to_all(blocks, 'dp', 0, 0, tiled=True, axis_index_groups=PLANES)]
    ppermute x5 -> x4, waiting for transfers between devices: 36 us -> 26.6 us  [swap_high(): return lax.ppermute(value, 'tensor', HIGH_PAIRS)]
    all_to_all x5 -> x4, starting transfers between devices: 31.9 us -> 23.7 us  [exchange(): lax.all_to_all(blocks, 'dp', 0, 0, tiled=True, axis_index_groups=PLANES)]
    all_gather x0 -> x1, blocking collectives: none -> 6.56 us  [shards(): red_gains = jnp.sum(lax.all_gather(red_gains, 'tensor'), axis=0)]
    dot_general x6 -> x2, matrix products: 9.34 us -> 2.79 us  [product_of(): return jnp.einsum(spec, left, right, preferred_element_type=jnp.float32)]
    ppermute x5 -> x4, starting transfers between devices: 16.2 us -> 10.8 us  [swap_high(): return lax.ppermute(value, 'tensor', HIGH_PAIRS)]
    ppermute x9 -> x8, starting transfers between devices: 10.7 us -> 5.79 us  [swap_near(): return lax.ppermute(value, 'dp', NEAR_PAIRS)]
  transfers between devices with their start and end apart: 29 -> 25, of which waited for: 18 -> 16; matrix products, arithmetic and copies ran while one was open for 16% -> 19% of each run, Pallas kernels for 3% -> 5%
where the time goes in v4:
time: 270 us; the launch traced here: 268 us
  waiting for transfers between devices  116 us (43%)
  other arithmetic  46.2 us (17%)
  starting transfers between devices  41.8 us (15%)
  local copies, waits for them, and re-layouts  26.7 us (10%)
  Pallas kernels  26.2 us (10%)
  blocking collectives  6.56 us (2%)
  matrix products  2.79 us (1%)
    all_to_all x4, waiting for transfers between devices, exchange(): lax.all_to_all(blocks, 'dp', 0, 0, tiled=True, axis_index_groups=PLANES)  59.9 us
    ppermute x4, waiting for transfers between devices, swap_high(): return lax.ppermute(value, 'tensor', HIGH_PAIRS)  26.6 us
    all_to_all x4, starting transfers between devices, exchange(): lax.all_to_all(blocks, 'dp', 0, 0, tiled=True, axis_index_groups=PLANES)  23.7 us
    ppermute x8, waiting for transfers between devices, swap_near(): return lax.ppermute(value, 'dp', NEAR_PAIRS)  20.3 us
    pallas_call x1, Pallas kernels, hidden_pass(): pl.pallas_call(hidden_kernel, grid=(4,), in_specs=[pl.BlockSpec((block, w...  12 us
    ppermute x4, starting transfers between devices, swap_high(): return lax.ppermute(value, 'tensor', HIGH_PAIRS)  10.8 us
    pallas_call x1, Pallas kernels, grads_pass(): pl.pallas_call(grads_kernel, grid=(NX,), in_specs=[pl.BlockSpec((tokens,...  9.83 us
    unnamed x117, local copies, waits for them, and re-layouts  9.7 us
  transfers between devices with their start and end apart: 25, of which 16 were waited for; matrix products, arithmetic and copies ran while one was open for 19% of the time, Pallas kernels for 5%

profile of v4, /device:TPU:0, one launch (start us, length us, event | category | flops | bytes accessed | tf_op | source)
XLA Modules:
  0.0 267.6 jit_solution(14657077773910758529)
XLA Ops:
  13.2 7.2 %all-to-all-start = ((bf16[16,2,32,1152]{3,2,1,0:T(8,128)(2,1)}), bf16[16,2,32,1152]{3,2,1,0:T(8,128)(2,1)S(1)}, u32[]{:S(2)}, u32[]{:S(2)}) async-start(bf16[16,2,32,1152]{3,2,1,0:T(8,128)(2,1)} %broadcast_in_dim.57), calls=%async_computation | async-start | bytes 4718592 | tf_op jit(solution)/shard_map/all_to_all | solution.py:98
  29.8 3.0 %pad_maximum_fusion.1.back_ref = bf16[1024,1024]{1,0:T(8,128)(2,1)} fusion(bf16[256,1024]{1,0:T(8,128)(2,1)} %collective-permute-done.3, bf16[256,1024]{1,0:T(8,128)(2,1)} %get-tuple-element.160, bf16[256,1024]{1,0:T(8,128)(2,1)} %collective-permute-done.2, bf16[256,1024]{1,0:T(8,128)(2,1)} %get-tuple-element.161), kind=kLoop, calls=%fused_computation.3 | loop fusion | flops 8388608 | bytes 4194304 | tf_op jit(solution)/shard_map/concatenate | solution.py:429
  32.8 19.7 %all-to-all-done = bf16[16,2,32,1152]{3,2,1,0:T(8,128)(2,1)S(1)} async-done(((bf16[16,2,32,1152]{3,2,1,0:T(8,128)(2,1)}), bf16[16,2,32,1152]{3,2,1,0:T(8,128)(2,1)S(1)}, u32[]{:S(2)}, u32[]{:S(2)}) %all-to-all-start) | async-done | bytes 2359328 | tf_op jit(solution)/shard_map/all_to_all | solution.py:98
  52.4 3.7 %broadcast_in_dim.59 = bf16[16,2,3,32,576]{4,3,2,1,0:T(8,128)(2,1)} broadcast(bf16[2,3,32,576]{3,2,1,0:T(8,128)(2,1)} %pad_maximum_fusion.4), dimensions={1,2,3,4} | broadcast | bytes 3760128 | tf_op jit(solution)/shard_map/broadcast_in_dim | solution.py:425
  63.6 4.5 %all-to-all-start.1 = ((bf16[16,2,3,32,576]{4,3,2,1,0:T(8,128)(2,1)}), bf16[16,2,3,32,576]{4,3,2,1,0:T(8,128)(2,1)}, u32[]{:S(2)}, u32[]{:S(2)}) async-start(bf16[16,2,3,32,576]{4,3,2,1,0:T(8,128)(2,1)} %broadcast_in_dim.59), calls=%async_computation.1 | async-start | bytes 7864320 | tf_op jit(solution)/shard_map/all_to_all | solution.py:98
  72.5 3.7 %collective-permute-start.5 = (bf16[256,1024]{1,0:T(8,128)(2,1)S(1)}, bf16[256,1024]{1,0:T(8,128)(2,1)S(1)}, u32[]{:S(2)}, u32[]{:S(2)}) collective-permute-start(bf16[256,1024]{1,0:T(8,128)(2,1)S(1)} %add_convert_fusion), channel_id=1, source_target_pairs={{0,2},{2,0},{1,3},{3,1},{4,6},{6,4},{5,7},{7,5},{8,10},{10,8},{9,1... | collective-permute-start | bytes 1572872 | tf_op jit(solution)/shard_map/ppermute | solution.py:49
  76.5 12.0 %collective-permute-done.5 = bf16[256,1024]{1,0:T(8,128)(2,1)S(1)} collective-permute-done((bf16[256,1024]{1,0:T(8,128)(2,1)S(1)}, bf16[256,1024]{1,0:T(8,128)(2,1)S(1)}, u32[]{:S(2)}, u32[]{:S(2)}) %collective-permute-start.5) | collective-permute-done | bytes 524320 | tf_op jit(solution)/shard_map/ppermute | solution.py:49
  90.2 13.3 %collective-permute-done.6 = bf16[256,1024]{1,0:T(8,128)(2,1)S(1)} collective-permute-done((bf16[256,1024]{1,0:T(8,128)(2,1)S(1)}, bf16[256,1024]{1,0:T(8,128)(2,1)S(1)}, u32[]{:S(2)}, u32[]{:S(2)}) %collective-permute-start.6) | collective-permute-done | bytes 524320 | tf_op jit(solution)/shard_map/ppermute | solution.py:53
  104.6 10.6 %all-to-all-done.1.weights_ref.down_ref = bf16[16,2,3,32,576]{4,3,2,1,0:T(8,128)(2,1)} async-done(((bf16[16,2,3,32,576]{4,3,2,1,0:T(8,128)(2,1)}), bf16[16,2,3,32,576]{4,3,2,1,0:T(8,128)(2,1)}, u32[]{:S(2)}, u32[]{:S(2)}) %all-to-all-start.1) | async-done | bytes 3538976 | tf_op jit(solution)/shard_map/all_to_all | solution.py:98
  118.2 12.0 %hidden_pass.1 = (bf16[1024,576]{1,0:T(8,128)(2,1)S(1)}, bf16[1024,576]{1,0:T(8,128)(2,1)S(1)}, bf16[1024,576]{1,0:T(8,128)(2,1)S(1)}, f32[512,1024]{1,0:T(8,128)S(1)}, f32[512,1024]{1,0:T(8,128)S(1)}) custom-call(bf16[1024,1024]{1,0:T(8,128)(2,1)S(1)} %constant_dynamic-update-slice_fusion.2.normed_ref, bf16[1024,1024]{1,0:T(8,128)(2,1)S(1)} %copy-done.11, ...), custom_call_target="tpu_custom_call" | custom-call | flops 6039797760 | bytes 16777216 | tf_op jit(solution)/shard_map/hidden_pass/pallas_call | solution.py:171
  130.4 4.0 %collective-permute-done.8 = f32[512,1024]{1,0:T(8,128)S(1)} collective-permute-done((f32[512,1024]{1,0:T(8,128)S(1)}, f32[512,1024]{1,0:T(8,128)S(1)}, u32[]{:S(2)}, u32[]{:S(2)}) %collective-permute-start.8) | collective-permute-done | bytes 2097184 | tf_op jit(solution)/shard_map/ppermute | solution.py:45
  136.0 9.8 %grads_pass.1 = (bf16[16,2,3,32,576]{4,3,2,1,0:T(8,128)(2,1)}, f32[512,1024]{1,0:T(8,128)S(1)}, f32[512,1024]{1,0:T(8,128)}) custom-call(bf16[1024,1024]{1,0:T(8,128)(2,1)S(1)} %constant_dynamic-update-slice_fusion.2.normed_ref, bf16[1024,1024]{1,0:T(8,128)(2,1)S(1)} %copy-done.11, bf16[1024,576]{1,0:T(8,128)(2,1)S(1)} %get-tuple-element.63.gate_ref, ...), custom_call_target="tpu_custom_call" | custom-call | flops 4831838208 | bytes 14680064 | tf_op jit(solution)/shard_map/grads_pass/pallas_call | solution.py:233
  150.2 3.6 %collective-permute-start.10 = (bf16[256,1024]{1,0:T(8,128)(2,1)}, bf16[256,1024]{1,0:T(8,128)(2,1)}, u32[]{:S(2)}, u32[]{:S(2)}) collective-permute-start(bf16[256,1024]{1,0:T(8,128)(2,1)} %convert_add_fusion.2), channel_id=1, source_target_pairs={{0,2},{2,0},{1,3},{3,1},{4,6},{6,4},{5,7},{7,5},{8,10},{10,8},{9,1... | collective-permute-start | bytes 1572872 | tf_op jit(solution)/shard_map/ppermute | solution.py:49
  153.8 6.5 %all-to-all-start.2 = ((bf16[16,2,3,32,576]{4,3,2,1,0:T(8,128)(2,1)}), bf16[16,2,3,32,576]{4,3,2,1,0:T(8,128)(2,1)}, u32[]{:S(2)}, u32[]{:S(2)}) async-start(bf16[16,2,3,32,576]{4,3,2,1,0:T(8,128)(2,1)} %get-tuple-element.74), calls=%async_computation.2 | async-start | bytes 7864320 | tf_op jit(solution)/shard_map/all_to_all | solution.py:98
  160.3 5.2 %collective-permute-done.10 = bf16[256,1024]{1,0:T(8,128)(2,1)} collective-permute-done((bf16[256,1024]{1,0:T(8,128)(2,1)}, bf16[256,1024]{1,0:T(8,128)(2,1)}, u32[]{:S(2)}, u32[]{:S(2)}) %collective-permute-start.10) | collective-permute-done | bytes 524320 | tf_op jit(solution)/shard_map/ppermute | solution.py:49
  173.4 4.4 %mixer_pass.1 = (bf16[16,2,32,1024]{3,2,1,0:T(8,128)(2,1)S(1)}, f32[512,1024]{1,0:T(8,128)S(1)}, f32[1,1024]{1,0:T(1,128)S(1)}, f32[3,256]{1,0:T(4,128)S(1)}) custom-call(bf16[512,1024]{1,0:T(8,128)(2,1)S(1)} %pad_maximum_fusion.3.branch_ref.branch_part_ref, bf16[1024,1152]{1,0:T(8,128)(2,1)S(1)} %bitcast.126, f32[512,768]{1,0:T(8,128)S(1)} %copy-done.2, ...), custom_call_target="tpu_custom_call" | custom-call | flops 2147483648 | bytes 10485760 | tf_op jit(solution)/shard_map/mixer_pass/pallas_call | solution.py:330
  189.9 22.3 %all-to-all-done.2 = bf16[16,2,3,32,576]{4,3,2,1,0:T(8,128)(2,1)} async-done(((bf16[16,2,3,32,576]{4,3,2,1,0:T(8,128)(2,1)}), bf16[16,2,3,32,576]{4,3,2,1,0:T(8,128)(2,1)}, u32[]{:S(2)}, u32[]{:S(2)}) %all-to-all-start.2) | async-done | bytes 3538976 | tf_op jit(solution)/shard_map/all_to_all | solution.py:98
  214.2 3.5 %collective-permute-start.13 = (bf16[256,1024]{1,0:T(8,128)(2,1)}, bf16[256,1024]{1,0:T(8,128)(2,1)}, u32[]{:S(2)}, u32[]{:S(2)}) collective-permute-start(bf16[256,1024]{1,0:T(8,128)(2,1)} %fusion.4), channel_id=1, source_target_pairs={{0,2},{2,0},{1,3},{3,1},{4,6},{6,4},{5,7},{7,5},{8,10},{10,8},{9,1... | collective-permute-start | bytes 1572872 | tf_op jit(solution)/shard_map/ppermute | solution.py:49
  217.8 5.5 %all-to-all-start.3 = ((bf16[16,2,32,1152]{3,2,1,0:T(8,128)(2,1)}), bf16[16,2,32,1152]{3,2,1,0:T(8,128)(2,1)S(1)}, u32[]{:S(2)}, u32[]{:S(2)}) async-start(bf16[16,2,32,1152]{3,2,1,0:T(8,128)(2,1)} %pad_maximum_fusion), calls=%async_computation.3 | async-start | bytes 4718592 | tf_op jit(solution)/shard_map/all_to_all | solution.py:98
  223.3 5.4 %collective-permute-done.17 = bf16[256,1024]{1,0:T(8,128)(2,1)} collective-permute-done((bf16[256,1024]{1,0:T(8,128)(2,1)S(1)}, bf16[256,1024]{1,0:T(8,128)(2,1)}, u32[]{:S(2)}, u32[]{:S(2)}) %collective-permute-start.17) | collective-permute-done | bytes 524320 | tf_op jit(solution)/shard_map/ppermute | solution.py:49
  230.1 2.9 %convert_reduce_fusion = f32[2,3,32,576]{3,2,1,0:T(8,128)S(1)} fusion(bf16[16,2,3,32,576]{4,3,2,1,0:T(8,128)(2,1)} %all-to-all-done.2), kind=kLoop, calls=%fused_computation | loop fusion | flops 3428352 | bytes 3981312 | tf_op jit(solution)/shard_map/reduce_sum | solution.py:526
  233.4 4.1 %collective-permute-done.13 = bf16[256,1024]{1,0:T(8,128)(2,1)} collective-permute-done((bf16[256,1024]{1,0:T(8,128)(2,1)}, bf16[256,1024]{1,0:T(8,128)(2,1)}, u32[]{:S(2)}, u32[]{:S(2)}) %collective-permute-start.13) | collective-permute-done | bytes 524320 | tf_op jit(solution)/shard_map/ppermute | solution.py:49
  245.3 7.3 %all-to-all-done.3 = bf16[16,2,32,1152]{3,2,1,0:T(8,128)(2,1)S(1)} async-done(((bf16[16,2,32,1152]{3,2,1,0:T(8,128)(2,1)}), bf16[16,2,32,1152]{3,2,1,0:T(8,128)(2,1)S(1)}, u32[]{:S(2)}, u32[]{:S(2)}) %all-to-all-start.3) | async-done | bytes 2359328 | tf_op jit(solution)/shard_map/all_to_all | solution.py:98
  258.4 6.6 %all_gather.3 = f32[4,2,32]{2,1,0:T(2,128)S(1)} all-gather(f32[1,2,32]{2,1,0:T(2,128)S(1)} %all_gather_reshape.3), channel_id=1, replica_groups=mesh['dp'=32,'tensor'=4] {'tensor'}, dimensions={0}, use_global_device_ids=true | all-gather | bytes 1280 | tf_op jit(solution)/shard_map/all_gather | solution.py:535
  (252 shorter events, 85.1 us)
Async XLA Ops:
  3.3 8.2 %collective-permute-start = (bf16[32,1152]{1,0:T(8,128)(2,1)S(1)}, bf16[32,1152]{1,0:T(8,128)(2,1)S(1)}, u32[]{:S(2)}, u32[]{:S(2)}) collective-permute-start(bf16[32,1152]{1,0:T(8,128)(2,1)S(1)} %constant_dynamic-update-slice_fusion), channel_id=1, source_target_pairs={{0,16},{4,20},{8,24},{12,28},{16,0},{20,4},{24,8},{28,12},{32,48},... | collective-permute-start | bytes 221192 | tf_op jit(solution)/shard_map/ppermute | solution.py:53
  8.1 19.8 %collective-permute-start.1 = (bf16[3,32,576]{2,1,0:T(8,128)(2,1)}, bf16[3,32,576]{2,1,0:T(8,128)(2,1)}, u32[]{:S(2)}, u32[]{:S(2)}) collective-permute-start(bf16[3,32,576]{2,1,0:T(8,128)(2,1)} %fusion.17), channel_id=1, source_target_pairs={{0,16},{4,20},{8,24},{12,28},{16,0},{20,4},{24,8},{28,12},{32,48},... | collective-permute-start | bytes 331784 | tf_op jit(solution)/shard_map/ppermute | solution.py:53
  9.3 15.2 %collective-permute-start.2 = (bf16[256,1024]{1,0:T(8,128)(2,1)}, bf16[256,1024]{1,0:T(8,128)(2,1)}, u32[]{:S(2)}, u32[]{:S(2)}) collective-permute-start(bf16[256,1024]{1,0:T(8,128)(2,1)} %get-tuple-element.161), channel_id=1, source_target_pairs={{0,16},{4,20},{8,24},{12,28},{16,0},{20,4},{24,8},{28,12},{32,48},... | collective-permute-start | bytes 1572872 | tf_op jit(solution)/shard_map/ppermute | solution.py:53
  13.2 39.2 %all-to-all-start = ((bf16[16,2,32,1152]{3,2,1,0:T(8,128)(2,1)}), bf16[16,2,32,1152]{3,2,1,0:T(8,128)(2,1)S(1)}, u32[]{:S(2)}, u32[]{:S(2)}) async-start(bf16[16,2,32,1152]{3,2,1,0:T(8,128)(2,1)} %broadcast_in_dim.57), calls=%async_computation | async-start | bytes 4718592 | tf_op jit(solution)/shard_map/all_to_all | solution.py:98
  24.5 5.3 %collective-permute-start.3 = (bf16[256,1024]{1,0:T(8,128)(2,1)}, bf16[256,1024]{1,0:T(8,128)(2,1)}, u32[]{:S(2)}, u32[]{:S(2)}) collective-permute-start(bf16[256,1024]{1,0:T(8,128)(2,1)} %collective-permute-done.2), channel_id=1, source_target_pairs={{0,1},{1,0},{2,3},{3,2},{4,5},{5,4},{6,7},{7,6},{8,9},{9,8},{10,11... | collective-permute-start | bytes 1572872 | tf_op jit(solution)/shard_map/ppermute | solution.py:45
  63.6 51.6 %all-to-all-start.1 = ((bf16[16,2,3,32,576]{4,3,2,1,0:T(8,128)(2,1)}), bf16[16,2,3,32,576]{4,3,2,1,0:T(8,128)(2,1)}, u32[]{:S(2)}, u32[]{:S(2)}) async-start(bf16[16,2,3,32,576]{4,3,2,1,0:T(8,128)(2,1)} %broadcast_in_dim.59), calls=%async_computation.1 | async-start | bytes 7864320 | tf_op jit(solution)/shard_map/all_to_all | solution.py:98
  69.7 2.7 %collective-permute-start.4 = (f32[256,1024]{1,0:T(8,128)S(1)}, f32[256,1024]{1,0:T(8,128)S(1)}, u32[]{:S(2)}, u32[]{:S(2)}) collective-permute-start(f32[256,1024]{1,0:T(8,128)S(1)} %constant_dynamic-slice_fusion.1), channel_id=1, source_target_pairs={{0,1},{1,0},{2,3},{3,2},{4,5},{5,4},{6,7},{7,6},{8,9},{9,8},{10,11... | collective-permute-start | bytes 3145736 | tf_op jit(solution)/shard_map/ppermute | solution.py:45
  72.5 15.9 %collective-permute-start.5 = (bf16[256,1024]{1,0:T(8,128)(2,1)S(1)}, bf16[256,1024]{1,0:T(8,128)(2,1)S(1)}, u32[]{:S(2)}, u32[]{:S(2)}) collective-permute-start(bf16[256,1024]{1,0:T(8,128)(2,1)S(1)} %add_convert_fusion), channel_id=1, source_target_pairs={{0,2},{2,0},{1,3},{3,1},{4,6},{6,4},{5,7},{7,5},{8,10},{10,8},{9,1... | collective-permute-start | bytes 1572872 | tf_op jit(solution)/shard_map/ppermute | solution.py:49
  89.9 13.6 %collective-permute-start.6 = (bf16[256,1024]{1,0:T(8,128)(2,1)S(1)}, bf16[256,1024]{1,0:T(8,128)(2,1)S(1)}, u32[]{:S(2)}, u32[]{:S(2)}) collective-permute-start(bf16[256,1024]{1,0:T(8,128)(2,1)S(1)} %multiply_convert_fusion.1), channel_id=1, source_target_pairs={{0,16},{4,20},{8,24},{12,28},{16,0},{20,4},{24,8},{28,12},{32,48},... | collective-permute-start | bytes 1572872 | tf_op jit(solution)/shard_map/ppermute | solution.py:53
  115.2 2.9 %collective-permute-start.7 = (bf16[512,1024]{1,0:T(8,128)(2,1)}, bf16[512,1024]{1,0:T(8,128)(2,1)S(1)}, u32[]{:S(2)}, u32[]{:S(2)}) collective-permute-start(bf16[512,1024]{1,0:T(8,128)(2,1)} %pad_maximum_fusion.2), channel_id=1, source_target_pairs={{0,1},{1,0},{2,3},{3,2},{4,5},{5,4},{6,7},{7,6},{8,9},{9,8},{10,11... | collective-permute-start | bytes 3145736 | tf_op jit(solution)/shard_map/ppermute | solution.py:45
  130.2 4.2 %collective-permute-start.8 = (f32[512,1024]{1,0:T(8,128)S(1)}, f32[512,1024]{1,0:T(8,128)S(1)}, u32[]{:S(2)}, u32[]{:S(2)}) collective-permute-start(f32[512,1024]{1,0:T(8,128)S(1)} %get-tuple-element.59), channel_id=1, source_target_pairs={{0,1},{1,0},{2,3},{3,2},{4,5},{5,4},{6,7},{7,6},{8,9},{9,8},{10,11... | collective-permute-start | bytes 6291464 | tf_op jit(solution)/shard_map/ppermute | solution.py:45
  135.0 14.2 %collective-permute-start.9 = (bf16[256,1024]{1,0:T(8,128)(2,1)S(1)}, bf16[256,1024]{1,0:T(8,128)(2,1)S(1)}, u32[]{:S(2)}, u32[]{:S(2)}) collective-permute-start(bf16[256,1024]{1,0:T(8,128)(2,1)S(1)} %slice.232), channel_id=1, source_target_pairs={{0,16},{4,20},{8,24},{12,28},{16,0},{20,4},{24,8},{28,12},{32,48},... | collective-permute-start | bytes 1572872 | tf_op jit(solution)/shard_map/ppermute | solution.py:53
  150.2 15.3 %collective-permute-start.10 = (bf16[256,1024]{1,0:T(8,128)(2,1)}, bf16[256,1024]{1,0:T(8,128)(2,1)}, u32[]{:S(2)}, u32[]{:S(2)}) collective-permute-start(bf16[256,1024]{1,0:T(8,128)(2,1)} %convert_add_fusion.2), channel_id=1, source_target_pairs={{0,2},{2,0},{1,3},{3,1},{4,6},{6,4},{5,7},{7,5},{8,10},{10,8},{9,1... | collective-permute-start | bytes 1572872 | tf_op jit(solution)/shard_map/ppermute | solution.py:49
  153.8 58.4 %all-to-all-start.2 = ((bf16[16,2,3,32,576]{4,3,2,1,0:T(8,128)(2,1)}), bf16[16,2,3,32,576]{4,3,2,1,0:T(8,128)(2,1)}, u32[]{:S(2)}, u32[]{:S(2)}) async-start(bf16[16,2,3,32,576]{4,3,2,1,0:T(8,128)(2,1)} %get-tuple-element.74), calls=%async_computation.2 | async-start | bytes 7864320 | tf_op jit(solution)/shard_map/all_to_all | solution.py:98
  169.4 14.3 %collective-permute-start.11 = (f32[512,1024]{1,0:T(8,128)}, f32[512,1024]{1,0:T(8,128)}, u32[]{:S(2)}, u32[]{:S(2)}) collective-permute-start(f32[512,1024]{1,0:T(8,128)} %get-tuple-element.72), channel_id=1, source_target_pairs={{0,1},{1,0},{2,3},{3,2},{4,5},{5,4},{6,7},{7,6},{8,9},{9,8},{10,11... | collective-permute-start | bytes 6291464 | tf_op jit(solution)/shard_map/ppermute | solution.py:45
  183.3 5.9 %collective-permute-start.16 = (f32[256,1024]{1,0:T(8,128)S(1)}, f32[256,1024]{1,0:T(8,128)S(1)}, u32[]{:S(2)}, u32[]{:S(2)}) collective-permute-start(f32[256,1024]{1,0:T(8,128)S(1)} %constant_dynamic-slice_fusion), channel_id=1, source_target_pairs={{0,1},{1,0},{2,3},{3,2},{4,5},{5,4},{6,7},{7,6},{8,9},{9,8},{10,11... | collective-permute-start | bytes 3145736 | tf_op jit(solution)/shard_map/ppermute | solution.py:45
  186.9 25.3 %collective-permute-start.12 = (bf16[256,1024]{1,0:T(8,128)(2,1)}, bf16[256,1024]{1,0:T(8,128)(2,1)}, u32[]{:S(2)}, u32[]{:S(2)}) collective-permute-start(bf16[256,1024]{1,0:T(8,128)(2,1)} %slice.231), channel_id=1, source_target_pairs={{0,16},{4,20},{8,24},{12,28},{16,0},{20,4},{24,8},{28,12},{32,48},... | collective-permute-start | bytes 1572872 | tf_op jit(solution)/shard_map/ppermute | solution.py:53
  212.2 16.5 %collective-permute-start.17 = (bf16[256,1024]{1,0:T(8,128)(2,1)S(1)}, bf16[256,1024]{1,0:T(8,128)(2,1)}, u32[]{:S(2)}, u32[]{:S(2)}) collective-permute-start(bf16[256,1024]{1,0:T(8,128)(2,1)S(1)} %dynamic-slice_add_fusion), channel_id=1, source_target_pairs={{0,2},{2,0},{1,3},{3,1},{4,6},{6,4},{5,7},{7,5},{8,10},{10,8},{9,1... | collective-permute-start | bytes 1572872 | tf_op jit(solution)/shard_map/ppermute | solution.py:49
  214.2 23.3 %collective-permute-start.13 = (bf16[256,1024]{1,0:T(8,128)(2,1)}, bf16[256,1024]{1,0:T(8,128)(2,1)}, u32[]{:S(2)}, u32[]{:S(2)}) collective-permute-start(bf16[256,1024]{1,0:T(8,128)(2,1)} %fusion.4), channel_id=1, source_target_pairs={{0,2},{2,0},{1,3},{3,1},{4,6},{6,4},{5,7},{7,5},{8,10},{10,8},{9,1... | collective-permute-start | bytes 1572872 | tf_op jit(solution)/shard_map/ppermute | solution.py:49
  217.8 34.8 %all-to-all-start.3 = ((bf16[16,2,32,1152]{3,2,1,0:T(8,128)(2,1)}), bf16[16,2,32,1152]{3,2,1,0:T(8,128)(2,1)S(1)}, u32[]{:S(2)}, u32[]{:S(2)}) async-start(bf16[16,2,32,1152]{3,2,1,0:T(8,128)(2,1)} %pad_maximum_fusion), calls=%async_computation.3 | async-start | bytes 4718592 | tf_op jit(solution)/shard_map/all_to_all | solution.py:98
  233.0 7.2 %collective-permute-start.20 = (f32[3,32,576]{2,1,0:T(8,128)S(1)}, f32[3,32,576]{2,1,0:T(8,128)S(1)}, u32[]{:S(2)}, u32[]{:S(2)}) collective-permute-start(f32[3,32,576]{2,1,0:T(8,128)S(1)} %dynamic-slice_bitcast_fusion.2), channel_id=1, source_target_pairs={{0,16},{4,20},{8,24},{12,28},{16,0},{20,4},{24,8},{28,12},{32,48},... | collective-permute-start | bytes 663560 | tf_op jit(solution)/shard_map/ppermute | solution.py:53
  239.7 2.7 %collective-permute-start.14 = (f32[256,1024]{1,0:T(8,128)S(1)}, f32[256,1024]{1,0:T(8,128)S(1)}, u32[]{:S(2)}, u32[]{:S(2)}) collective-permute-start(f32[256,1024]{1,0:T(8,128)S(1)} %get-tuple-element.157), channel_id=1, source_target_pairs={{0,1},{1,0},{2,3},{3,2},{4,5},{5,4},{6,7},{7,6},{8,9},{9,8},{10,11... | collective-permute-start | bytes 3145736 | tf_op jit(solution)/shard_map/ppermute | solution.py:45
  239.8 4.3 %collective-permute-start.18 = (f32[256,1024]{1,0:T(8,128)S(1)}, f32[256,1024]{1,0:T(8,128)S(1)}, u32[]{:S(2)}, u32[]{:S(2)}) collective-permute-start(f32[256,1024]{1,0:T(8,128)S(1)} %get-tuple-element.156), channel_id=1, source_target_pairs={{0,1},{1,0},{2,3},{3,2},{4,5},{5,4},{6,7},{7,6},{8,9},{9,8},{10,11... | collective-permute-start | bytes 3145736 | tf_op jit(solution)/shard_map/ppermute | solution.py:45
  252.9 5.2 %collective-permute-start.19 = (f32[32,1152]{1,0:T(8,128)S(1)}, f32[32,1152]{1,0:T(8,128)S(1)}, u32[]{:S(2)}, u32[]{:S(2)}) collective-permute-start(f32[32,1152]{1,0:T(8,128)S(1)} %dynamic-slice_bitcast_fusion.3), channel_id=1, source_target_pairs={{0,16},{4,20},{8,24},{12,28},{16,0},{20,4},{24,8},{28,12},{32,48},... | collective-permute-start | bytes 442376 | tf_op jit(solution)/shard_map/ppermute | solution.py:53
  (56 other events, 321.1 us)

commit v5 on v4

--- a/solution.py
+++ b/solution.py
@@ -107,6 +107,25 @@
     keep = lax.dynamic_index_in_dim(grad, near, 0, keepdims=False)
     take = swap_near(lax.dynamic_index_in_dim(grad, 1 - near, 0, keepdims=False))
     return jnp.concatenate(in_order(keep, take, near), axis=-1)
+
+
+def spread_kernel(block_ref, copies_ref):
+    copies_ref[0] = block_ref[...]
+
+
+def spread_pass(block):
+    return pl.pallas_call(
+        spread_kernel,
+        grid=(NX * NY,),
+        in_specs=[pl.BlockSpec(block.shape, lambda i: (0,) * block.ndim)],
+        out_specs=pl.BlockSpec((1,) + block.shape, lambda i: (i,) + (0,) * block.ndim),
+        out_shape=jax.ShapeDtypeStruct((NX * NY,) + block.shape, block.dtype),
+        compiler_params=pltpu.CompilerParams(vmem_limit_bytes=VMEM_BYTES),
+        cost_estimate=pl.CostEstimate(
+            flops=0, bytes_accessed=2 * NX * NY * block.size, transcendentals=0
+        ),
+        name="spread_pass",
+    )(block)
 
 
 VMEM_BYTES = 40 * 1024 * 1024
@@ -417,12 +436,18 @@
         axis=1,
     )
     low_mix = low(low_mix)
-    low_ffn = low(jnp.concatenate([gate_up_weight, down_weight.T[None]], axis=0))
+    low_mix = jnp.stack(in_order(low_mix, swap_near(low_mix), near), axis=0)
+    low_mix, gate_up_early, down_early, cotangent, tokens_in, segment_ids = (
+        lax.optimization_barrier(
+            (low_mix, gate_up_weight, down_weight, cotangent, tokens_in, segment_ids)
+        )
+    )
+    low_ffn = low(jnp.concatenate([gate_up_early, down_early.T[None]], axis=0))
     keep = lax.dynamic_slice_in_dim(low_ffn, near * part_units, part_units, 2)
     give = lax.dynamic_slice_in_dim(low_ffn, (1 - near) * part_units, part_units, 2)
     take = swap_near(give)
     low_ffn = jnp.stack(in_order(keep, take, near), axis=0)
-    ffn_copies = jnp.broadcast_to(low_ffn[None], (NX * NY,) + low_ffn.shape)
+    ffn_copies = spread_pass(low_ffn)
     back_out = cotangent.reshape(count, width)
     back_own, back_other = halves(back_out, core)
     back_near = swap_near(back_own)
@@ -437,7 +462,6 @@
     masks = wide(jnp.concatenate([mask_one, mask_two], axis=1))
     scale_one = lax.rsqrt(jnp.mean(flat * flat, axis=-1, keepdims=True) + epsilon_norm)
 
-    low_mix = jnp.stack(in_order(low_mix, swap_near(low_mix), near), axis=0)
     mix_full = exchange(jnp.broadcast_to(low_mix[None], (NX * NY,) + low_mix.shape))
     mix_full, ffn_copies, back_four, masks, scale_one = lax.optimization_barrier(
         (mix_full, ffn_copies, back_four, masks, scale_one)
@@ -522,7 +546,9 @@
     keep = lax.dynamic_index_in_dim(red_mix, near, 0, keepdims=False)
     red_mix = keep + swap_near(lax.dynamic_index_in_dim(red_mix, 1 - near, 0, keepdims=False))
     back_normed_one = across_high(back_normed_one)
-    grad_ffn, back_normed_one = lax.optimization_barrier((grad_ffn, back_normed_one))
+    grad_ffn, back_normed_one, ffn_half = lax.optimization_barrier(
+        (grad_ffn, back_normed_one, ffn_half)
+    )
     red_ffn = whole_units(jnp.sum(wide(grad_ffn), axis=0), near)
     result = middle + across_high(ffn_half)
     result = joined(result, swap_core(result), core)

time: 270 us -> 277 us (1.026)
  waiting for transfers between devices: 116 us -> 105 us
  starting transfers between devices: 41.8 us -> 52.3 us
  local copies, waits for them, and re-layouts: 26.7 us -> 33 us
    all_to_all x4, starting transfers between devices: 23.7 us -> 34.5 us  [exchange(): lax.all_to_all(blocks, 'dp', 0, 0, tiled=True, axis_index_groups=PLANES)]
    all_to_all x4, waiting for transfers between devices: 59.9 us -> 50 us  [exchange(): lax.all_to_all(blocks, 'dp', 0, 0, tiled=True, axis_index_groups=PLANES)]
    unnamed x117 -> x119, local copies, waits for them, and re-layouts: 9.7 us -> 14.1 us
    broadcast_in_dim x1 -> x0, local copies, waits for them, and re-layouts: 3.67 us -> none  [shards(): ffn_copies = jnp.broadcast_to(low_ffn[None], (NX * NY,) + low_ffn.shape)]
    ppermute x4, waiting for transfers between devices: 26.6 us -> 23.2 us  [swap_high(): return lax.ppermute(value, 'tensor', HIGH_PAIRS)]
    ppermute x8, waiting for transfers between devices: 20.3 us -> 23.7 us  [swap_near(): return lax.ppermute(value, 'dp', NEAR_PAIRS)]
  transfers between devices with their start and end apart: 25 -> 25, of which waited for: 16 -> 15; matrix products, arithmetic and copies ran while one was open for 19% -> 20% of each run, Pallas kernels for 5% -> 5%
where the time goes in v5:
time: 277 us; the launch traced here: 275 us
  waiting for transfers between devices  105 us (38%)
  starting transfers between devices  52.3 us (19%)
  other arithmetic  46.6 us (17%)
  local copies, waits for them, and re-layouts  33 us (12%)
  Pallas kernels  26.5 us (10%)
  blocking collectives  6.56 us (2%)
  matrix products  2.79 us (1%)
    all_to_all x4, waiting for transfers between devices, exchange(): lax.all_to_all(blocks, 'dp', 0, 0, tiled=True, axis_index_groups=PLANES)  50 us
    all_to_all x4, starting transfers between devices, exchange(): lax.all_to_all(blocks, 'dp', 0, 0, tiled=True, axis_index_groups=PLANES)  34.5 us
    ppermute x8, waiting for transfers between devices, swap_near(): return lax.ppermute(value, 'dp', NEAR_PAIRS)  23.7 us
    ppermute x4, waiting for transfers between devices, swap_high(): return lax.ppermute(value, 'tensor', HIGH_PAIRS)  23.2 us
    unnamed x119, local copies, waits for them, and re-layouts  14.1 us
    pallas_call x1, Pallas kernels, hidden_pass(): pl.pallas_call(hidden_kernel, grid=(4,), in_specs=[pl.BlockSpec((block, w...  11.9 us
    pallas_call x1, Pallas kernels, grads_pass(): pl.pallas_call(grads_kernel, grid=(NX,), in_specs=[pl.BlockSpec((tokens,...  9.66 us
    ppermute x9, waiting for transfers between devices, swap_core(): return lax.ppermute(value, 'tensor', CORE_PAIRS)  8.52 us
  transfers between devices with their start and end apart: 25, of which 15 were waited for; matrix products, arithmetic and copies ran while one was open for 20% of the time, Pallas kernels for 5%

profile of v5, /device:TPU:0, one launch (start us, length us, event | category | flops | bytes accessed | tf_op | source)
XLA Modules:
  0.0 274.8 jit_solution(3330199138571817952)
XLA Ops:
  9.3 7.1 %all-to-all-start = ((bf16[16,2,32,1152]{3,2,1,0:T(8,128)(2,1)}), bf16[16,2,32,1152]{3,2,1,0:T(8,128)(2,1)S(1)}, u32[]{:S(2)}, u32[]{:S(2)}) async-start(bf16[16,2,32,1152]{3,2,1,0:T(8,128)(2,1)} %broadcast_in_dim.51), calls=%async_computation | async-start | bytes 4718592 | tf_op jit(solution)/shard_map/all_to_all | solution.py:98
  21.7 2.3 dynamic-slice_bitcast_fusion
  31.0 5.3 %collective-permute-done.2 = bf16[256,1024]{1,0:T(8,128)(2,1)} collective-permute-done((bf16[256,1024]{1,0:T(8,128)(2,1)}, bf16[256,1024]{1,0:T(8,128)(2,1)}, u32[]{:S(2)}, u32[]{:S(2)}) %collective-permute-start.2) | collective-permute-done | bytes 524320 | tf_op jit(solution)/shard_map/ppermute | solution.py:53
  45.4 2.8 %pad_maximum_fusion.1.back_ref = bf16[1024,1024]{1,0:T(8,128)(2,1)} fusion(bf16[256,1024]{1,0:T(8,128)(2,1)} %collective-permute-done.3, bf16[256,1024]{1,0:T(8,128)(2,1)S(1)} %copy-done.30, bf16[256,1024]{1,0:T(8,128)(2,1)} %collective-permute-done.2, bf16[256,1024]{1,0:T(8,128)(2,1)} %get-tuple-element.175), kind=kLoop, calls=%fused_computation.3 | loop fusion | flops 8388608 | bytes 4194304 | tf_op jit(solution)/shard_map/concatenate | solution.py:454
  57.2 7.2 %all-to-all-start.1 = ((bf16[16,2,3,32,576]{4,3,2,1,0:T(8,128)(2,1)}), bf16[16,2,3,32,576]{4,3,2,1,0:T(8,128)(2,1)}, u32[]{:S(2)}, u32[]{:S(2)}) async-start(bf16[16,2,3,32,576]{4,3,2,1,0:T(8,128)(2,1)} %copy-done.1), calls=%async_computation.1 | async-start | bytes 7864320 | tf_op jit(solution)/shard_map/all_to_all | solution.py:98
  66.2 2.4 collective-permute-done.4
  68.8 4.0 %collective-permute-start.5 = (bf16[256,1024]{1,0:T(8,128)(2,1)S(1)}, bf16[256,1024]{1,0:T(8,128)(2,1)S(1)}, u32[]{:S(2)}, u32[]{:S(2)}) collective-permute-start(bf16[256,1024]{1,0:T(8,128)(2,1)S(1)} %add_convert_fusion), channel_id=1, source_target_pairs={{0,2},{2,0},{1,3},{3,1},{4,6},{6,4},{5,7},{7,5},{8,10},{10,8},{9,1... | collective-permute-start | bytes 1572872 | tf_op jit(solution)/shard_map/ppermute | solution.py:49
  73.0 12.0 %collective-permute-done.5 = bf16[256,1024]{1,0:T(8,128)(2,1)S(1)} collective-permute-done((bf16[256,1024]{1,0:T(8,128)(2,1)S(1)}, bf16[256,1024]{1,0:T(8,128)(2,1)S(1)}, u32[]{:S(2)}, u32[]{:S(2)}) %collective-permute-start.5) | collective-permute-done | bytes 524320 | tf_op jit(solution)/shard_map/ppermute | solution.py:49
  87.3 12.9 %collective-permute-done.6 = bf16[256,1024]{1,0:T(8,128)(2,1)S(1)} collective-permute-done((bf16[256,1024]{1,0:T(8,128)(2,1)S(1)}, bf16[256,1024]{1,0:T(8,128)(2,1)S(1)}, u32[]{:S(2)}, u32[]{:S(2)}) %collective-permute-start.6) | collective-permute-done | bytes 524320 | tf_op jit(solution)/shard_map/ppermute | solution.py:53
  101.3 15.9 %all-to-all-done.1.weights_ref.down_ref = bf16[16,2,3,32,576]{4,3,2,1,0:T(8,128)(2,1)} async-done(((bf16[16,2,3,32,576]{4,3,2,1,0:T(8,128)(2,1)}), bf16[16,2,3,32,576]{4,3,2,1,0:T(8,128)(2,1)}, u32[]{:S(2)}, u32[]{:S(2)}) %all-to-all-start.1) | async-done | bytes 3538976 | tf_op jit(solution)/shard_map/all_to_all | solution.py:98
  120.1 11.9 %hidden_pass.1 = (bf16[1024,576]{1,0:T(8,128)(2,1)S(1)}, bf16[1024,576]{1,0:T(8,128)(2,1)S(1)}, bf16[1024,576]{1,0:T(8,128)(2,1)S(1)}, f32[512,1024]{1,0:T(8,128)S(1)}, f32[512,1024]{1,0:T(8,128)S(1)}) custom-call(bf16[1024,1024]{1,0:T(8,128)(2,1)S(1)} %constant_dynamic-update-slice_fusion.2.normed_ref, bf16[1024,1024]{1,0:T(8,128)(2,1)S(1)} %copy-done.12, ...), custom_call_target="tpu_custom_call" | custom-call | flops 6039797760 | bytes 16777216 | tf_op jit(solution)/shard_map/hidden_pass/pallas_call | solution.py:190
  132.3 4.0 %collective-permute-done.8 = f32[512,1024]{1,0:T(8,128)S(1)} collective-permute-done((f32[512,1024]{1,0:T(8,128)S(1)}, f32[512,1024]{1,0:T(8,128)S(1)}, u32[]{:S(2)}, u32[]{:S(2)}) %collective-permute-start.8) | collective-permute-done | bytes 2097184 | tf_op jit(solution)/shard_map/ppermute | solution.py:45
  138.5 9.7 %grads_pass.1 = (bf16[16,2,3,32,576]{4,3,2,1,0:T(8,128)(2,1)}, f32[512,1024]{1,0:T(8,128)S(1)}, f32[512,1024]{1,0:T(8,128)}) custom-call(bf16[1024,1024]{1,0:T(8,128)(2,1)S(1)} %constant_dynamic-update-slice_fusion.2.normed_ref, bf16[1024,1024]{1,0:T(8,128)(2,1)S(1)} %copy-done.12, bf16[1024,576]{1,0:T(8,128)(2,1)S(1)} %get-tuple-element.77.gate_ref, ...), custom_call_target="tpu_custom_call" | custom-call | flops 4831838208 | bytes 14680064 | tf_op jit(solution)/shard_map/grads_pass/pallas_call | solution.py:252
  152.1 3.9 %collective-permute-start.10 = (bf16[256,1024]{1,0:T(8,128)(2,1)}, bf16[256,1024]{1,0:T(8,128)(2,1)}, u32[]{:S(2)}, u32[]{:S(2)}) collective-permute-start(bf16[256,1024]{1,0:T(8,128)(2,1)} %convert_add_fusion.2), channel_id=1, source_target_pairs={{0,2},{2,0},{1,3},{3,1},{4,6},{6,4},{5,7},{7,5},{8,10},{10,8},{9,1... | collective-permute-start | bytes 1572872 | tf_op jit(solution)/shard_map/ppermute | solution.py:49
  156.0 12.3 %all-to-all-start.2 = ((bf16[16,2,3,32,576]{4,3,2,1,0:T(8,128)(2,1)}), bf16[16,2,3,32,576]{4,3,2,1,0:T(8,128)(2,1)}, u32[]{:S(2)}, u32[]{:S(2)}) async-start(bf16[16,2,3,32,576]{4,3,2,1,0:T(8,128)(2,1)} %get-tuple-element.81), calls=%async_computation.2 | async-start | bytes 7864320 | tf_op jit(solution)/shard_map/all_to_all | solution.py:98
  176.3 4.3 %mixer_pass.1 = (bf16[16,2,32,1024]{3,2,1,0:T(8,128)(2,1)S(1)}, f32[512,1024]{1,0:T(8,128)S(1)}, f32[1,1024]{1,0:T(1,128)S(1)}, f32[3,256]{1,0:T(4,128)S(1)}) custom-call(bf16[512,1024]{1,0:T(8,128)(2,1)S(1)} %pad_maximum_fusion.3.branch_ref.branch_part_ref, bf16[1024,1152]{1,0:T(8,128)(2,1)S(1)} %bitcast.124, f32[512,768]{1,0:T(8,128)S(1)} %copy-done.3, ...), custom_call_target="tpu_custom_call" | custom-call | flops 2147483648 | bytes 10485760 | tf_op jit(solution)/shard_map/mixer_pass/pallas_call | solution.py:349
  192.5 27.7 %all-to-all-done.2 = bf16[16,2,3,32,576]{4,3,2,1,0:T(8,128)(2,1)} async-done(((bf16[16,2,3,32,576]{4,3,2,1,0:T(8,128)(2,1)}), bf16[16,2,3,32,576]{4,3,2,1,0:T(8,128)(2,1)}, u32[]{:S(2)}, u32[]{:S(2)}) %all-to-all-start.2) | async-done | bytes 3538976 | tf_op jit(solution)/shard_map/all_to_all | solution.py:98
  221.4 7.9 %all-to-all-start.3 = ((bf16[16,2,32,1152]{3,2,1,0:T(8,128)(2,1)}), bf16[16,2,32,1152]{3,2,1,0:T(8,128)(2,1)S(1)}, u32[]{:S(2)}, u32[]{:S(2)}) async-start(bf16[16,2,32,1152]{3,2,1,0:T(8,128)(2,1)} %pad_maximum_fusion), calls=%async_computation.3 | async-start | bytes 4718592 | tf_op jit(solution)/shard_map/all_to_all | solution.py:98
  229.3 2.4 collective-permute-done.13
  233.2 2.9 %convert_reduce_fusion = f32[2,3,32,576]{3,2,1,0:T(8,128)S(1)} fusion(bf16[16,2,3,32,576]{4,3,2,1,0:T(8,128)(2,1)} %all-to-all-done.2), kind=kLoop, calls=%fused_computation | loop fusion | flops 3428352 | bytes 3981312 | tf_op jit(solution)/shard_map/reduce_sum | solution.py:552
  237.2 8.8 %collective-permute-done.16 = bf16[256,1024]{1,0:T(8,128)(2,1)S(1)} collective-permute-done((bf16[256,1024]{1,0:T(8,128)(2,1)S(1)}, bf16[256,1024]{1,0:T(8,128)(2,1)S(1)}, u32[]{:S(2)}, u32[]{:S(2)}) %collective-permute-start.16) | collective-permute-done | bytes 524320 | tf_op jit(solution)/shard_map/ppermute | solution.py:49
  253.4 6.4 %all-to-all-done.3 = bf16[16,2,32,1152]{3,2,1,0:T(8,128)(2,1)S(1)} async-done(((bf16[16,2,32,1152]{3,2,1,0:T(8,128)(2,1)}), bf16[16,2,32,1152]{3,2,1,0:T(8,128)(2,1)S(1)}, u32[]{:S(2)}, u32[]{:S(2)}) %all-to-all-start.3) | async-done | bytes 2359328 | tf_op jit(solution)/shard_map/all_to_all | solution.py:98
  262.6 2.8 %collective-permute-done.19 = f32[32,1152]{1,0:T(8,128)S(1)} collective-permute-done((f32[32,1152]{1,0:T(8,128)S(1)}, f32[32,1152]{1,0:T(8,128)S(1)}, u32[]{:S(2)}, u32[]{:S(2)}) %collective-permute-start.19) | collective-permute-done | bytes 147488 | tf_op jit(solution)/shard_map/ppermute | solution.py:53
  265.6 6.6 %all_gather.3 = f32[4,2,32]{2,1,0:T(2,128)S(1)} all-gather(f32[1,2,32]{2,1,0:T(2,128)S(1)} %all_gather_reshape.3), channel_id=1, replica_groups=mesh['dp'=32,'tensor'=4] {'tensor'}, dimensions={0}, use_global_device_ids=true | all-gather | bytes 1280 | tf_op jit(solution)/shard_map/all_gather | solution.py:561
  (255 shorter events, 89.6 us)
Async XLA Ops:
  3.2 4.4 %collective-permute-start = (bf16[32,1152]{1,0:T(8,128)(2,1)S(1)}, bf16[32,1152]{1,0:T(8,128)(2,1)S(1)}, u32[]{:S(2)}, u32[]{:S(2)}) collective-permute-start(bf16[32,1152]{1,0:T(8,128)(2,1)S(1)} %constant_dynamic-update-slice_fusion), channel_id=1, source_target_pairs={{0,16},{4,20},{8,24},{12,28},{16,0},{20,4},{24,8},{28,12},{32,48},... | collective-permute-start | bytes 221192 | tf_op jit(solution)/shard_map/ppermute | solution.py:53
  9.3 39.0 %all-to-all-start = ((bf16[16,2,32,1152]{3,2,1,0:T(8,128)(2,1)}), bf16[16,2,32,1152]{3,2,1,0:T(8,128)(2,1)S(1)}, u32[]{:S(2)}, u32[]{:S(2)}) async-start(bf16[16,2,32,1152]{3,2,1,0:T(8,128)(2,1)} %broadcast_in_dim.51), calls=%async_computation | async-start | bytes 4718592 | tf_op jit(solution)/shard_map/all_to_all | solution.py:98
  19.8 22.0 %collective-permute-start.1 = (bf16[3,32,576]{2,1,0:T(8,128)(2,1)}, bf16[3,32,576]{2,1,0:T(8,128)(2,1)}, u32[]{:S(2)}, u32[]{:S(2)}) collective-permute-start(bf16[3,32,576]{2,1,0:T(8,128)(2,1)} %fusion.16), channel_id=1, source_target_pairs={{0,16},{4,20},{8,24},{12,28},{16,0},{20,4},{24,8},{28,12},{32,48},... | collective-permute-start | bytes 331784 | tf_op jit(solution)/shard_map/ppermute | solution.py:53
  24.0 12.3 %collective-permute-start.2 = (bf16[256,1024]{1,0:T(8,128)(2,1)}, bf16[256,1024]{1,0:T(8,128)(2,1)}, u32[]{:S(2)}, u32[]{:S(2)}) collective-permute-start(bf16[256,1024]{1,0:T(8,128)(2,1)} %get-tuple-element.175), channel_id=1, source_target_pairs={{0,16},{4,20},{8,24},{12,28},{16,0},{20,4},{24,8},{28,12},{32,48},... | collective-permute-start | bytes 1572872 | tf_op jit(solution)/shard_map/ppermute | solution.py:53
  36.2 9.2 %collective-permute-start.3 = (bf16[256,1024]{1,0:T(8,128)(2,1)}, bf16[256,1024]{1,0:T(8,128)(2,1)}, u32[]{:S(2)}, u32[]{:S(2)}) collective-permute-start(bf16[256,1024]{1,0:T(8,128)(2,1)} %collective-permute-done.2), channel_id=1, source_target_pairs={{0,1},{1,0},{2,3},{3,2},{4,5},{5,4},{6,7},{7,6},{8,9},{9,8},{10,11... | collective-permute-start | bytes 1572872 | tf_op jit(solution)/shard_map/ppermute | solution.py:45
  57.2 60.0 %all-to-all-start.1 = ((bf16[16,2,3,32,576]{4,3,2,1,0:T(8,128)(2,1)}), bf16[16,2,3,32,576]{4,3,2,1,0:T(8,128)(2,1)}, u32[]{:S(2)}, u32[]{:S(2)}) async-start(bf16[16,2,3,32,576]{4,3,2,1,0:T(8,128)(2,1)} %copy-done.1), calls=%async_computation.1 | async-start | bytes 7864320 | tf_op jit(solution)/shard_map/all_to_all | solution.py:98
  65.9 2.7 collective-permute-start.4
  68.8 16.3 %collective-permute-start.5 = (bf16[256,1024]{1,0:T(8,128)(2,1)S(1)}, bf16[256,1024]{1,0:T(8,128)(2,1)S(1)}, u32[]{:S(2)}, u32[]{:S(2)}) collective-permute-start(bf16[256,1024]{1,0:T(8,128)(2,1)S(1)} %add_convert_fusion), channel_id=1, source_target_pairs={{0,2},{2,0},{1,3},{3,1},{4,6},{6,4},{5,7},{7,5},{8,10},{10,8},{9,1... | collective-permute-start | bytes 1572872 | tf_op jit(solution)/shard_map/ppermute | solution.py:49
  86.5 13.7 %collective-permute-start.6 = (bf16[256,1024]{1,0:T(8,128)(2,1)S(1)}, bf16[256,1024]{1,0:T(8,128)(2,1)S(1)}, u32[]{:S(2)}, u32[]{:S(2)}) collective-permute-start(bf16[256,1024]{1,0:T(8,128)(2,1)S(1)} %multiply_convert_fusion.1), channel_id=1, source_target_pairs={{0,16},{4,20},{8,24},{12,28},{16,0},{20,4},{24,8},{28,12},{32,48},... | collective-permute-start | bytes 1572872 | tf_op jit(solution)/shard_map/ppermute | solution.py:53
  117.2 2.9 %collective-permute-start.7 = (bf16[512,1024]{1,0:T(8,128)(2,1)}, bf16[512,1024]{1,0:T(8,128)(2,1)S(1)}, u32[]{:S(2)}, u32[]{:S(2)}) collective-permute-start(bf16[512,1024]{1,0:T(8,128)(2,1)} %pad_maximum_fusion.2), channel_id=1, source_target_pairs={{0,1},{1,0},{2,3},{3,2},{4,5},{5,4},{6,7},{7,6},{8,9},{9,8},{10,11... | collective-permute-start | bytes 3145736 | tf_op jit(solution)/shard_map/ppermute | solution.py:45
  132.1 4.2 %collective-permute-start.8 = (f32[512,1024]{1,0:T(8,128)S(1)}, f32[512,1024]{1,0:T(8,128)S(1)}, u32[]{:S(2)}, u32[]{:S(2)}) collective-permute-start(f32[512,1024]{1,0:T(8,128)S(1)} %get-tuple-element.72), channel_id=1, source_target_pairs={{0,1},{1,0},{2,3},{3,2},{4,5},{5,4},{6,7},{7,6},{8,9},{9,8},{10,11... | collective-permute-start | bytes 6291464 | tf_op jit(solution)/shard_map/ppermute | solution.py:45
  136.9 14.2 %collective-permute-start.9 = (bf16[256,1024]{1,0:T(8,128)(2,1)S(1)}, bf16[256,1024]{1,0:T(8,128)(2,1)S(1)}, u32[]{:S(2)}, u32[]{:S(2)}) collective-permute-start(bf16[256,1024]{1,0:T(8,128)(2,1)S(1)} %slice.231), channel_id=1, source_target_pairs={{0,16},{4,20},{8,24},{12,28},{16,0},{20,4},{24,8},{28,12},{32,48},... | collective-permute-start | bytes 1572872 | tf_op jit(solution)/shard_map/ppermute | solution.py:53
  152.1 16.2 %collective-permute-start.10 = (bf16[256,1024]{1,0:T(8,128)(2,1)}, bf16[256,1024]{1,0:T(8,128)(2,1)}, u32[]{:S(2)}, u32[]{:S(2)}) collective-permute-start(bf16[256,1024]{1,0:T(8,128)(2,1)} %convert_add_fusion.2), channel_id=1, source_target_pairs={{0,2},{2,0},{1,3},{3,1},{4,6},{6,4},{5,7},{7,5},{8,10},{10,8},{9,1... | collective-permute-start | bytes 1572872 | tf_op jit(solution)/shard_map/ppermute | solution.py:49
  156.0 64.2 %all-to-all-start.2 = ((bf16[16,2,3,32,576]{4,3,2,1,0:T(8,128)(2,1)}), bf16[16,2,3,32,576]{4,3,2,1,0:T(8,128)(2,1)}, u32[]{:S(2)}, u32[]{:S(2)}) async-start(bf16[16,2,3,32,576]{4,3,2,1,0:T(8,128)(2,1)} %get-tuple-element.81), calls=%async_computation.2 | async-start | bytes 7864320 | tf_op jit(solution)/shard_map/all_to_all | solution.py:98
  172.3 14.2 %collective-permute-start.14 = (f32[512,1024]{1,0:T(8,128)}, f32[512,1024]{1,0:T(8,128)}, u32[]{:S(2)}, u32[]{:S(2)}) collective-permute-start(f32[512,1024]{1,0:T(8,128)} %get-tuple-element.95), channel_id=1, source_target_pairs={{0,1},{1,0},{2,3},{3,2},{4,5},{5,4},{6,7},{7,6},{8,9},{9,8},{10,11... | collective-permute-start | bytes 6291464 | tf_op jit(solution)/shard_map/ppermute | solution.py:45
  186.1 5.7 %collective-permute-start.12 = (f32[256,1024]{1,0:T(8,128)S(1)}, f32[256,1024]{1,0:T(8,128)S(1)}, u32[]{:S(2)}, u32[]{:S(2)}) collective-permute-start(f32[256,1024]{1,0:T(8,128)S(1)} %constant_dynamic-slice_fusion), channel_id=1, source_target_pairs={{0,1},{1,0},{2,3},{3,2},{4,5},{5,4},{6,7},{7,6},{8,9},{9,8},{10,11... | collective-permute-start | bytes 3145736 | tf_op jit(solution)/shard_map/ppermute | solution.py:45
  188.8 31.4 %collective-permute-start.15 = (bf16[256,1024]{1,0:T(8,128)(2,1)S(1)}, bf16[256,1024]{1,0:T(8,128)(2,1)}, u32[]{:S(2)}, u32[]{:S(2)}) collective-permute-start(bf16[256,1024]{1,0:T(8,128)(2,1)S(1)} %slice.230), channel_id=1, source_target_pairs={{0,16},{4,20},{8,24},{12,28},{16,0},{20,4},{24,8},{28,12},{32,48},... | collective-permute-start | bytes 1572872 | tf_op jit(solution)/shard_map/ppermute | solution.py:53
  220.2 11.5 %collective-permute-start.13 = (bf16[256,1024]{1,0:T(8,128)(2,1)S(1)}, bf16[256,1024]{1,0:T(8,128)(2,1)}, u32[]{:S(2)}, u32[]{:S(2)}) collective-permute-start(bf16[256,1024]{1,0:T(8,128)(2,1)S(1)} %dynamic-slice_add_fusion), channel_id=1, source_target_pairs={{0,2},{2,0},{1,3},{3,1},{4,6},{6,4},{5,7},{7,5},{8,10},{10,8},{9,1... | collective-permute-start | bytes 1572872 | tf_op jit(solution)/shard_map/ppermute | solution.py:49
  221.4 38.4 %all-to-all-start.3 = ((bf16[16,2,32,1152]{3,2,1,0:T(8,128)(2,1)}), bf16[16,2,32,1152]{3,2,1,0:T(8,128)(2,1)S(1)}, u32[]{:S(2)}, u32[]{:S(2)}) async-start(bf16[16,2,32,1152]{3,2,1,0:T(8,128)(2,1)} %pad_maximum_fusion), calls=%async_computation.3 | async-start | bytes 4718592 | tf_op jit(solution)/shard_map/all_to_all | solution.py:98
  232.9 13.1 %collective-permute-start.16 = (bf16[256,1024]{1,0:T(8,128)(2,1)S(1)}, bf16[256,1024]{1,0:T(8,128)(2,1)S(1)}, u32[]{:S(2)}, u32[]{:S(2)}) collective-permute-start(bf16[256,1024]{1,0:T(8,128)(2,1)S(1)} %slice_add_fusion), channel_id=1, source_target_pairs={{0,2},{2,0},{1,3},{3,1},{4,6},{6,4},{5,7},{7,5},{8,10},{10,8},{9,1... | collective-permute-start | bytes 1572872 | tf_op jit(solution)/shard_map/ppermute | solution.py:49
  236.2 11.7 %collective-permute-start.20 = (f32[3,32,576]{2,1,0:T(8,128)S(1)}, f32[3,32,576]{2,1,0:T(8,128)S(1)}, u32[]{:S(2)}, u32[]{:S(2)}) collective-permute-start(f32[3,32,576]{2,1,0:T(8,128)S(1)} %dynamic-slice_bitcast_fusion.2), channel_id=1, source_target_pairs={{0,16},{4,20},{8,24},{12,28},{16,0},{20,4},{24,8},{28,12},{32,48},... | collective-permute-start | bytes 663560 | tf_op jit(solution)/shard_map/ppermute | solution.py:53
  247.8 2.8 %collective-permute-start.17 = (f32[256,1024]{1,0:T(8,128)S(1)}, f32[256,1024]{1,0:T(8,128)S(1)}, u32[]{:S(2)}, u32[]{:S(2)}) collective-permute-start(f32[256,1024]{1,0:T(8,128)S(1)} %get-tuple-element.171), channel_id=1, source_target_pairs={{0,1},{1,0},{2,3},{3,2},{4,5},{5,4},{6,7},{7,6},{8,9},{9,8},{10,11... | collective-permute-start | bytes 3145736 | tf_op jit(solution)/shard_map/ppermute | solution.py:45
  248.0 4.3 %collective-permute-start.18 = (f32[256,1024]{1,0:T(8,128)S(1)}, f32[256,1024]{1,0:T(8,128)S(1)}, u32[]{:S(2)}, u32[]{:S(2)}) collective-permute-start(f32[256,1024]{1,0:T(8,128)S(1)} %get-tuple-element.170), channel_id=1, source_target_pairs={{0,1},{1,0},{2,3},{3,2},{4,5},{5,4},{6,7},{7,6},{8,9},{9,8},{10,11... | collective-permute-start | bytes 3145736 | tf_op jit(solution)/shard_map/ppermute | solution.py:45
  260.1 5.2 %collective-permute-start.19 = (f32[32,1152]{1,0:T(8,128)S(1)}, f32[32,1152]{1,0:T(8,128)S(1)}, u32[]{:S(2)}, u32[]{:S(2)}) collective-permute-start(f32[32,1152]{1,0:T(8,128)S(1)} %dynamic-slice_bitcast_fusion.3), channel_id=1, source_target_pairs={{0,16},{4,20},{8,24},{12,28},{16,0},{20,4},{24,8},{28,12},{32,48},... | collective-permute-start | bytes 442376 | tf_op jit(solution)/shard_map/ppermute | solution.py:53
  (57 other events, 289.0 us)

commit v6 on v4

--- a/solution.py
+++ b/solution.py
@@ -103,10 +103,32 @@
     return jnp.where(first, mine, theirs), jnp.where(first, theirs, mine)
 
 
+def places(units):
+    main = units // 128 * 128
+    rest = units - main
+    return main, [(k * main, 3 * main + k * rest, 3 * main + (k + 1) * rest) for k in range(3)]
+
+
+def packed(three):
+    main = places(three.shape[2])[0]
+    parts = [three[k, :, :main] for k in range(3)] + [three[k, :, main:] for k in range(3)]
+    return jnp.concatenate(parts, axis=1)
+
+
+def unpacked(rows):
+    main, where = places(rows.shape[1] // 3)
+    return jnp.stack(
+        [
+            jnp.concatenate([rows[:, start : start + main], rows[:, tail:end]], axis=1)
+            for start, tail, end in where
+        ]
+    )
+
+
 def whole_units(grad, near):
     keep = lax.dynamic_index_in_dim(grad, near, 0, keepdims=False)
     take = swap_near(lax.dynamic_index_in_dim(grad, 1 - near, 0, keepdims=False))
-    return jnp.concatenate(in_order(keep, take, near), axis=-1)
+    return jnp.concatenate(in_order(unpacked(keep), unpacked(take), near), axis=2)
 
 
 VMEM_BYTES = 40 * 1024 * 1024
@@ -128,7 +150,8 @@
     normed_ref, back_ref, weights_ref, gate_ref, up_ref, hidden_ref, keep_ref, give_ref, held
 ):
     step = pl.program_id(0)
-    rows = weights_ref.shape[3]
+    rows = weights_ref.shape[2]
+    main, where = places(gate_ref.shape[1])
 
     @pl.when(step == 0)
     def _():
@@ -136,8 +159,10 @@
             for z in range(NZ):
                 for y in range(NY):
                     start = ((x * NZ + z) * NY + y) * rows
-                    for k in range(3):
-                        held[k, start : start + rows, :] = weights_ref[x * NY + y, z, k]
+                    for k, (first, tail, end) in enumerate(where):
+                        block = weights_ref.at[x * NY + y, z]
+                        held[k, start : start + rows, :main] = block[:, first : first + main]
+                        held[k, start : start + rows, main:] = block[:, tail:end]
 
     normed = normed_ref[...]
     gate = dot_plain(normed, held[0])
@@ -163,7 +188,7 @@
 
 def hidden_pass(normed, back, weights):
     tokens, width = normed.shape
-    units = weights.shape[-1]
+    units = weights.shape[-1] // 3
     block = tokens // 4
     turned = lambda i: ((i + 2) % 4, 0)
     narrow = jax.ShapeDtypeStruct((tokens, units), jnp.bfloat16)
@@ -174,7 +199,7 @@
         in_specs=[
             pl.BlockSpec((block, width), turned),
             pl.BlockSpec((block, width), turned),
-            pl.BlockSpec(weights.shape, lambda i: (0, 0, 0, 0, 0)),
+            pl.BlockSpec(weights.shape, lambda i: (0, 0, 0, 0)),
         ],
         out_specs=[
             pl.BlockSpec((block, units), turned),
@@ -201,35 +226,42 @@
     gate_ref,
     up_ref,
     hidden_ref,
-    down_ref,
+    weights_ref,
     grads_ref,
     keep_ref,
     give_ref,
+    down,
 ):
-    rows, units = down_ref.shape[3:]
+    rows = weights_ref.shape[2]
+    units = hidden_ref.shape[1]
     plane = NY * rows
+    main, where = places(units)
     normed, hidden = normed_ref[...], hidden_ref[...]
     pairs = ((normed, gate_ref[...]), (normed, up_ref[...]), (back_ref[...], hidden))
-    for k, (left, right) in enumerate(pairs):
+    for (left, right), (first, tail, end) in zip(pairs, where):
         grad = low(dot_columns(left, right))
         for z in range(NZ):
             part = grad[z * plane : (z + 1) * plane]
-            grads_ref[:, z, k] = part.reshape(NY, rows, units)
-    down = jnp.concatenate(
-        [down_ref[:, z, 0].reshape(plane, units) for z in range(NZ)], axis=0
-    )
+            grads_ref[:, z, :, first : first + main] = part[:, :main].reshape(NY, rows, main)
+            grads_ref[:, z, :, tail:end] = part[:, main:].reshape(NY, rows, end - tail)
+    first, tail, end = where[2]
+    for z in range(NZ):
+        part = slice(z * plane, (z + 1) * plane)
+        down[part, :main] = weights_ref[:, z, :, first : first + main].reshape(plane, main)
+        down[part, main:] = weights_ref[:, z, :, tail:end].reshape(plane, end - tail)
     half = hidden.shape[0] // 2
-    keep_ref[...] = dot_rows(hidden[:half], down)
-    give_ref[...] = dot_rows(hidden[half:], down)
+    keep_ref[...] = dot_rows(hidden[:half], down[...])
+    give_ref[...] = dot_rows(hidden[half:], down[...])
 
 
 def grads_pass(normed, back, gate, up, hidden, weights):
     tokens, width = normed.shape
-    rows, units = weights.shape[3:]
+    units = hidden.shape[1]
     block = width // NX
     column = lambda i: (0, i)
     whole = lambda i: (0, 0)
     half = jax.ShapeDtypeStruct((tokens // 2, width), jnp.float32)
+    packed_block = pl.BlockSpec((NY,) + weights.shape[1:], lambda i: (i, 0, 0, 0))
     return pl.pallas_call(
         grads_kernel,
         grid=(NX,),
@@ -239,18 +271,15 @@
             pl.BlockSpec((tokens, units), whole),
             pl.BlockSpec((tokens, units), whole),
             pl.BlockSpec((tokens, units), whole),
-            pl.BlockSpec((NY, NZ, 1, rows, units), lambda i: (i, 0, 2, 0, 0)),
+            packed_block,
         ],
         out_specs=[
-            pl.BlockSpec((NY, NZ, 3, rows, units), lambda i: (i, 0, 0, 0, 0)),
+            packed_block,
             pl.BlockSpec((tokens // 2, block), column),
             pl.BlockSpec((tokens // 2, block), column),
         ],
-        out_shape=[
-            jax.ShapeDtypeStruct(weights.shape, jnp.bfloat16),
-            half,
-            half,
-        ],
+        out_shape=[jax.ShapeDtypeStruct(weights.shape, jnp.bfloat16), half, half],
+        scratch_shapes=[pltpu.VMEM((block, units), jnp.bfloat16)],
         compiler_params=pltpu.CompilerParams(vmem_limit_bytes=VMEM_BYTES),
         cost_estimate=pl.CostEstimate(
             flops=8 * tokens * width * units,
@@ -417,9 +446,15 @@
         axis=1,
     )
     low_mix = low(low_mix)
-    low_ffn = low(jnp.concatenate([gate_up_weight, down_weight.T[None]], axis=0))
-    keep = lax.dynamic_slice_in_dim(low_ffn, near * part_units, part_units, 2)
-    give = lax.dynamic_slice_in_dim(low_ffn, (1 - near) * part_units, part_units, 2)
+    low_mix = jnp.stack(in_order(low_mix, swap_near(low_mix), near), axis=0)
+    low_mix, gate_up_early, down_early, cotangent, tokens_in, segment_ids = (
+        lax.optimization_barrier(
+            (low_mix, gate_up_weight, down_weight, cotangent, tokens_in, segment_ids)
+        )
+    )
+    low_ffn = low(jnp.concatenate([gate_up_early, down_early.T[None]], axis=0))
+    keep = packed(lax.dynamic_slice_in_dim(low_ffn, near * part_units, part_units, 2))
+    give = packed(lax.dynamic_slice_in_dim(low_ffn, (1 - near) * part_units, part_units, 2))
     take = swap_near(give)
     low_ffn = jnp.stack(in_order(keep, take, near), axis=0)
     ffn_copies = jnp.broadcast_to(low_ffn[None], (NX * NY,) + low_ffn.shape)
@@ -437,7 +472,6 @@
     masks = wide(jnp.concatenate([mask_one, mask_two], axis=1))
     scale_one = lax.rsqrt(jnp.mean(flat * flat, axis=-1, keepdims=True) + epsilon_norm)
 
-    low_mix = jnp.stack(in_order(low_mix, swap_near(low_mix), near), axis=0)
     mix_full = exchange(jnp.broadcast_to(low_mix[None], (NX * NY,) + low_mix.shape))
     mix_full, ffn_copies, back_four, masks, scale_one = lax.optimization_barrier(
         (mix_full, ffn_copies, back_four, masks, scale_one)
@@ -522,7 +556,9 @@
     keep = lax.dynamic_index_in_dim(red_mix, near, 0, keepdims=False)
     red_mix = keep + swap_near(lax.dynamic_index_in_dim(red_mix, 1 - near, 0, keepdims=False))
     back_normed_one = across_high(back_normed_one)
-    grad_ffn, back_normed_one = lax.optimization_barrier((grad_ffn, back_normed_one))
+    grad_ffn, back_normed_one, ffn_half = lax.optimization_barrier(
+        (grad_ffn, back_normed_one, ffn_half)
+    )
     red_ffn = whole_units(jnp.sum(wide(grad_ffn), axis=0), near)
     result = middle + across_high(ffn_half)
     result = joined(result, swap_core(result), core)

time: 270 us -> 264 us (0.978)
  waiting for transfers between devices: 116 us -> 101 us
  local copies, waits for them, and re-layouts: 26.7 us -> 32.4 us
    all_to_all x4, waiting for transfers between devices: 59.9 us -> 36.6 us  [exchange(): lax.all_to_all(blocks, 'dp', 0, 0, tiled=True, axis_index_groups=PLANES)]
    ppermute x8, waiting for transfers between devices: 20.3 us -> 33.9 us  [swap_near(): return lax.ppermute(value, 'dp', NEAR_PAIRS)]
    ppermute x4, waiting for transfers between devices: 26.6 us -> 21.3 us  [swap_high(): return lax.ppermute(value, 'tensor', HIGH_PAIRS)]
    ppermute x8, starting transfers between devices: 5.79 us -> 10.2 us  [swap_near(): return lax.ppermute(value, 'dp', NEAR_PAIRS)]
    ppermute x4, starting transfers between devices: 10.8 us -> 7.85 us  [swap_high(): return lax.ppermute(value, 'tensor', HIGH_PAIRS)]
    unnamed x117 -> x113, local copies, waits for them, and re-layouts: 9.7 us -> 9.43 us
  transfers between devices with their start and end apart: 25 -> 25, of which waited for: 16 -> 18; matrix products, arithmetic and copies ran while one was open for 19% -> 19% of each run, Pallas kernels for 5% -> 5%
where the time goes in v6:
time: 264 us; the launch traced here: 259 us
  waiting for transfers between devices  101 us (38%)
  other arithmetic  44.8 us (17%)
  starting transfers between devices  43.8 us (17%)
  local copies, waits for them, and re-layouts  32.4 us (12%)
  Pallas kernels  26.2 us (10%)
  blocking collectives  6.56 us (2%)
  matrix products  2.79 us (1%)
    all_to_all x4, waiting for transfers between devices, exchange(): lax.all_to_all(blocks, 'dp', 0, 0, tiled=True, axis_index_groups=PLANES)  36.6 us
    ppermute x8, waiting for transfers between devices, swap_near(): return lax.ppermute(value, 'dp', NEAR_PAIRS)  33.9 us
    all_to_all x4, starting transfers between devices, exchange(): lax.all_to_all(blocks, 'dp', 0, 0, tiled=True, axis_index_groups=PLANES)  24.3 us
    ppermute x4, waiting for transfers between devices, swap_high(): return lax.ppermute(value, 'tensor', HIGH_PAIRS)  21.3 us
    pallas_call x1, Pallas kernels, hidden_pass(): pl.pallas_call(hidden_kernel, grid=(4,), in_specs=[pl.BlockSpec((block, w...  12 us
    ppermute x8, starting transfers between devices, swap_near(): return lax.ppermute(value, 'dp', NEAR_PAIRS)  10.2 us
    pallas_call x1, Pallas kernels, grads_pass(): pl.pallas_call(grads_kernel, grid=(NX,), in_specs=[pl.BlockSpec((tokens,...  9.88 us
    unnamed x113, local copies, waits for them, and re-layouts  9.43 us
  transfers between devices with their start and end apart: 25, of which 18 were waited for; matrix products, arithmetic and copies ran while one was open for 19% of the time, Pallas kernels for 5%

profile of v6, /device:TPU:0, one launch (start us, length us, event | category | flops | bytes accessed | tf_op | source)
XLA Modules:
  0.0 259.3 jit_solution(9301235547351380955)
XLA Ops:
  14.1 7.1 %all-to-all-start = ((bf16[16,2,32,1152]{3,2,1,0:T(8,128)(2,1)}), bf16[16,2,32,1152]{3,2,1,0:T(8,128)(2,1)S(1)}, u32[]{:S(2)}, u32[]{:S(2)}) async-start(bf16[16,2,32,1152]{3,2,1,0:T(8,128)(2,1)} %broadcast_in_dim.57), calls=%async_computation | async-start | bytes 4718592 | tf_op jit(solution)/shard_map/all_to_all | solution.py:98
  34.2 5.0 %collective-permute-done.2 = bf16[256,1024]{1,0:T(8,128)(2,1)} collective-permute-done((bf16[256,1024]{1,0:T(8,128)(2,1)}, bf16[256,1024]{1,0:T(8,128)(2,1)}, u32[]{:S(2)}, u32[]{:S(2)}) %collective-permute-start.2) | collective-permute-done | bytes 524320 | tf_op jit(solution)/shard_map/ppermute | solution.py:53
  41.3 2.8 %pad_maximum_fusion.1.back_ref = bf16[1024,1024]{1,0:T(8,128)(2,1)} fusion(bf16[256,1024]{1,0:T(8,128)(2,1)S(1)} %collective-permute-done.3, bf16[256,1024]{1,0:T(8,128)(2,1)} %get-tuple-element.174, bf16[256,1024]{1,0:T(8,128)(2,1)} %collective-permute-done.2, bf16[256,1024]{1,0:T(8,128)(2,1)} %get-tuple-element.175), kind=kLoop, calls=%fused_computation.3 | loop fusion | flops 8388608 | bytes 4194304 | tf_op jit(solution)/shard_map/concatenate | solution.py:464
  44.2 8.8 %all-to-all-done = bf16[16,2,32,1152]{3,2,1,0:T(8,128)(2,1)S(1)} async-done(((bf16[16,2,32,1152]{3,2,1,0:T(8,128)(2,1)}), bf16[16,2,32,1152]{3,2,1,0:T(8,128)(2,1)S(1)}, u32[]{:S(2)}, u32[]{:S(2)}) %all-to-all-start) | async-done | bytes 2359328 | tf_op jit(solution)/shard_map/all_to_all | solution.py:98
  53.0 3.4 %broadcast_in_dim.59 = bf16[16,2,32,1728]{3,2,1,0:T(8,128)(2,1)} broadcast(bf16[2,32,1728]{2,1,0:T(8,128)(2,1)} %pad_maximum_fusion.6), dimensions={1,2,3} | broadcast | bytes 3760128 | tf_op jit(solution)/shard_map/broadcast_in_dim | solution.py:460
  63.9 4.5 %all-to-all-start.1 = ((bf16[16,2,32,1728]{3,2,1,0:T(8,128)(2,1)}), bf16[16,2,32,1728]{3,2,1,0:T(8,128)(2,1)}, u32[]{:S(2)}, u32[]{:S(2)}) async-start(bf16[16,2,32,1728]{3,2,1,0:T(8,128)(2,1)} %broadcast_in_dim.59), calls=%async_computation.1 | async-start | bytes 7340032 | tf_op jit(solution)/shard_map/all_to_all | solution.py:98
  72.8 3.8 %collective-permute-start.5 = (bf16[256,1024]{1,0:T(8,128)(2,1)S(1)}, bf16[256,1024]{1,0:T(8,128)(2,1)S(1)}, u32[]{:S(2)}, u32[]{:S(2)}) collective-permute-start(bf16[256,1024]{1,0:T(8,128)(2,1)S(1)} %add_convert_fusion), channel_id=1, source_target_pairs={{0,2},{2,0},{1,3},{3,1},{4,6},{6,4},{5,7},{7,5},{8,10},{10,8},{9,1... | collective-permute-start | bytes 1572872 | tf_op jit(solution)/shard_map/ppermute | solution.py:49
  76.9 12.0 %collective-permute-done.5 = bf16[256,1024]{1,0:T(8,128)(2,1)S(1)} collective-permute-done((bf16[256,1024]{1,0:T(8,128)(2,1)S(1)}, bf16[256,1024]{1,0:T(8,128)(2,1)S(1)}, u32[]{:S(2)}, u32[]{:S(2)}) %collective-permute-start.5) | collective-permute-done | bytes 524320 | tf_op jit(solution)/shard_map/ppermute | solution.py:49
  91.6 12.3 %collective-permute-done.6 = bf16[256,1024]{1,0:T(8,128)(2,1)S(1)} collective-permute-done((bf16[256,1024]{1,0:T(8,128)(2,1)S(1)}, bf16[256,1024]{1,0:T(8,128)(2,1)S(1)}, u32[]{:S(2)}, u32[]{:S(2)}) %collective-permute-start.6) | collective-permute-done | bytes 524320 | tf_op jit(solution)/shard_map/ppermute | solution.py:53
  104.9 7.7 %all-to-all-done.1.weights_ref = bf16[16,2,32,1728]{3,2,1,0:T(8,128)(2,1)} async-done(((bf16[16,2,32,1728]{3,2,1,0:T(8,128)(2,1)}), bf16[16,2,32,1728]{3,2,1,0:T(8,128)(2,1)}, u32[]{:S(2)}, u32[]{:S(2)}) %all-to-all-start.1) | async-done | bytes 3538976 | tf_op jit(solution)/shard_map/all_to_all | solution.py:98
  115.6 12.0 %hidden_pass.1 = (bf16[1024,576]{1,0:T(8,128)(2,1)S(1)}, bf16[1024,576]{1,0:T(8,128)(2,1)S(1)}, bf16[1024,576]{1,0:T(8,128)(2,1)S(1)}, f32[512,1024]{1,0:T(8,128)S(1)}, f32[512,1024]{1,0:T(8,128)S(1)}) custom-call(bf16[1024,1024]{1,0:T(8,128)(2,1)S(1)} %constant_dynamic-update-slice_fusion.2.normed_ref, bf16[1024,1024]{1,0:T(8,128)(2,1)S(1)} %copy-done.11, ...), custom_call_target="tpu_custom_call" | custom-call | flops 6039797760 | bytes 16777216 | tf_op jit(solution)/shard_map/hidden_pass/pallas_call | solution.py:196
  127.7 4.0 %collective-permute-done.8 = f32[512,1024]{1,0:T(8,128)S(1)} collective-permute-done((f32[512,1024]{1,0:T(8,128)S(1)}, f32[512,1024]{1,0:T(8,128)S(1)}, u32[]{:S(2)}, u32[]{:S(2)}) %collective-permute-start.8) | collective-permute-done | bytes 2097184 | tf_op jit(solution)/shard_map/ppermute | solution.py:45
  134.4 9.9 %grads_pass.1 = (bf16[16,2,32,1728]{3,2,1,0:T(8,128)(2,1)}, f32[512,1024]{1,0:T(8,128)S(1)}, f32[512,1024]{1,0:T(8,128)}) custom-call(bf16[1024,1024]{1,0:T(8,128)(2,1)S(1)} %constant_dynamic-update-slice_fusion.2.normed_ref, bf16[1024,1024]{1,0:T(8,128)(2,1)S(1)} %copy-done.11, bf16[1024,576]{1,0:T(8,128)(2,1)S(1)} %get-tuple-element.77.gate_ref, ...), custom_call_target="tpu_custom_call" | custom-call | flops 4831838208 | bytes 14680064 | tf_op jit(solution)/shard_map/grads_pass/pallas_call | solution.py:265
  147.6 3.7 %collective-permute-start.10 = (bf16[256,1024]{1,0:T(8,128)(2,1)}, bf16[256,1024]{1,0:T(8,128)(2,1)}, u32[]{:S(2)}, u32[]{:S(2)}) collective-permute-start(bf16[256,1024]{1,0:T(8,128)(2,1)} %convert_add_fusion.2), channel_id=1, source_target_pairs={{0,2},{2,0},{1,3},{3,1},{4,6},{6,4},{5,7},{7,5},{8,10},{10,8},{9,1... | collective-permute-start | bytes 1572872 | tf_op jit(solution)/shard_map/ppermute | solution.py:49
  151.2 6.3 %all-to-all-start.2 = ((bf16[16,2,32,1728]{3,2,1,0:T(8,128)(2,1)}), bf16[16,2,32,1728]{3,2,1,0:T(8,128)(2,1)}, u32[]{:S(2)}, u32[]{:S(2)}) async-start(bf16[16,2,32,1728]{3,2,1,0:T(8,128)(2,1)} %get-tuple-element.81), calls=%async_computation.2 | async-start | bytes 7340032 | tf_op jit(solution)/shard_map/all_to_all | solution.py:98
  157.6 5.4 %collective-permute-done.10 = bf16[256,1024]{1,0:T(8,128)(2,1)} collective-permute-done((bf16[256,1024]{1,0:T(8,128)(2,1)}, bf16[256,1024]{1,0:T(8,128)(2,1)}, u32[]{:S(2)}, u32[]{:S(2)}) %collective-permute-start.10) | collective-permute-done | bytes 524320 | tf_op jit(solution)/shard_map/ppermute | solution.py:49
  170.9 4.3 %mixer_pass.1 = (bf16[16,2,32,1024]{3,2,1,0:T(8,128)(2,1)S(1)}, f32[512,1024]{1,0:T(8,128)S(1)}, f32[1,1024]{1,0:T(1,128)S(1)}, f32[3,256]{1,0:T(4,128)S(1)}) custom-call(bf16[512,1024]{1,0:T(8,128)(2,1)S(1)} %pad_maximum_fusion.3.branch_ref.branch_part_ref, bf16[1024,1152]{1,0:T(8,128)(2,1)S(1)} %bitcast.159, f32[512,768]{1,0:T(8,128)S(1)} %copy-done.2, ...), custom_call_target="tpu_custom_call" | custom-call | flops 2147483648 | bytes 10485760 | tf_op jit(solution)/shard_map/mixer_pass/pallas_call | solution.py:359
  187.2 19.1 %all-to-all-done.2 = bf16[16,2,32,1728]{3,2,1,0:T(8,128)(2,1)} async-done(((bf16[16,2,32,1728]{3,2,1,0:T(8,128)(2,1)}), bf16[16,2,32,1728]{3,2,1,0:T(8,128)(2,1)}, u32[]{:S(2)}, u32[]{:S(2)}) %all-to-all-start.2) | async-done | bytes 3538976 | tf_op jit(solution)/shard_map/all_to_all | solution.py:98
  207.5 6.3 %all-to-all-start.3 = ((bf16[16,2,32,1152]{3,2,1,0:T(8,128)(2,1)}), bf16[16,2,32,1152]{3,2,1,0:T(8,128)(2,1)S(1)}, u32[]{:S(2)}, u32[]{:S(2)}) async-start(bf16[16,2,32,1152]{3,2,1,0:T(8,128)(2,1)} %pad_maximum_fusion), calls=%async_computation.3 | async-start | bytes 4718592 | tf_op jit(solution)/shard_map/all_to_all | solution.py:98
  213.9 3.9 %collective-permute-done.13 = bf16[256,1024]{1,0:T(8,128)(2,1)} collective-permute-done((bf16[256,1024]{1,0:T(8,128)(2,1)S(1)}, bf16[256,1024]{1,0:T(8,128)(2,1)}, u32[]{:S(2)}, u32[]{:S(2)}) %collective-permute-start.13) | collective-permute-done | bytes 524320 | tf_op jit(solution)/shard_map/ppermute | solution.py:49
  219.0 2.8 %convert_reduce_fusion = f32[2,32,1728]{2,1,0:T(8,128)S(1)} fusion(bf16[16,2,32,1728]{3,2,1,0:T(8,128)(2,1)} %all-to-all-done.2), kind=kLoop, calls=%fused_computation | loop fusion | flops 3428352 | bytes 3981312 | tf_op jit(solution)/shard_map/reduce_sum | solution.py:562
  223.9 11.8 %collective-permute-done.20 = f32[32,1728]{1,0:T(8,128)S(1)} collective-permute-done((f32[32,1728]{1,0:T(8,128)S(1)}, f32[32,1728]{1,0:T(8,128)S(1)}, u32[]{:S(2)}, u32[]{:S(2)}) %collective-permute-start.20) | collective-permute-done | bytes 221216 | tf_op jit(solution)/shard_map/ppermute | solution.py:53
  247.1 2.8 %collective-permute-done.19 = f32[32,1152]{1,0:T(8,128)S(1)} collective-permute-done((f32[32,1152]{1,0:T(8,128)S(1)}, f32[32,1152]{1,0:T(8,128)S(1)}, u32[]{:S(2)}, u32[]{:S(2)}) %collective-permute-start.19) | collective-permute-done | bytes 147488 | tf_op jit(solution)/shard_map/ppermute | solution.py:53
  250.1 6.6 %all_gather.3 = f32[4,2,32]{2,1,0:T(2,128)S(1)} all-gather(f32[1,2,32]{2,1,0:T(2,128)S(1)} %all_gather_reshape.3), channel_id=1, replica_groups=mesh['dp'=32,'tensor'=4] {'tensor'}, dimensions={0}, use_global_device_ids=true | all-gather | bytes 1280 | tf_op jit(solution)/shard_map/all_gather | solution.py:571
  (263 shorter events, 91.4 us)
Async XLA Ops:
  3.2 4.4 %collective-permute-start = (bf16[32,1152]{1,0:T(8,128)(2,1)S(1)}, bf16[32,1152]{1,0:T(8,128)(2,1)S(1)}, u32[]{:S(2)}, u32[]{:S(2)}) collective-permute-start(bf16[32,1152]{1,0:T(8,128)(2,1)S(1)} %constant_dynamic-update-slice_fusion), channel_id=1, source_target_pairs={{0,16},{4,20},{8,24},{12,28},{16,0},{20,4},{24,8},{28,12},{32,48},... | collective-permute-start | bytes 221192 | tf_op jit(solution)/shard_map/ppermute | solution.py:53
  14.1 38.9 %all-to-all-start = ((bf16[16,2,32,1152]{3,2,1,0:T(8,128)(2,1)}), bf16[16,2,32,1152]{3,2,1,0:T(8,128)(2,1)S(1)}, u32[]{:S(2)}, u32[]{:S(2)}) async-start(bf16[16,2,32,1152]{3,2,1,0:T(8,128)(2,1)} %broadcast_in_dim.57), calls=%async_computation | async-start | bytes 4718592 | tf_op jit(solution)/shard_map/all_to_all | solution.py:98
  22.8 16.5 %collective-permute-start.1 = (bf16[32,1728]{1,0:T(8,128)(2,1)}, bf16[32,1728]{1,0:T(8,128)(2,1)}, u32[]{:S(2)}, u32[]{:S(2)}) collective-permute-start(bf16[32,1728]{1,0:T(8,128)(2,1)} %concatenate.125), channel_id=1, source_target_pairs={{0,16},{4,20},{8,24},{12,28},{16,0},{20,4},{24,8},{28,12},{32,48},... | collective-permute-start | bytes 331784 | tf_op jit(solution)/shard_map/ppermute | solution.py:53
  26.9 12.3 %collective-permute-start.2 = (bf16[256,1024]{1,0:T(8,128)(2,1)}, bf16[256,1024]{1,0:T(8,128)(2,1)}, u32[]{:S(2)}, u32[]{:S(2)}) collective-permute-start(bf16[256,1024]{1,0:T(8,128)(2,1)} %get-tuple-element.175), channel_id=1, source_target_pairs={{0,16},{4,20},{8,24},{12,28},{16,0},{20,4},{24,8},{28,12},{32,48},... | collective-permute-start | bytes 1572872 | tf_op jit(solution)/shard_map/ppermute | solution.py:53
  63.9 48.7 %all-to-all-start.1 = ((bf16[16,2,32,1728]{3,2,1,0:T(8,128)(2,1)}), bf16[16,2,32,1728]{3,2,1,0:T(8,128)(2,1)}, u32[]{:S(2)}, u32[]{:S(2)}) async-start(bf16[16,2,32,1728]{3,2,1,0:T(8,128)(2,1)} %broadcast_in_dim.59), calls=%async_computation.1 | async-start | bytes 7340032 | tf_op jit(solution)/shard_map/all_to_all | solution.py:98
  69.9 2.7 %collective-permute-start.4 = (f32[256,1024]{1,0:T(8,128)S(1)}, f32[256,1024]{1,0:T(8,128)S(1)}, u32[]{:S(2)}, u32[]{:S(2)}) collective-permute-start(f32[256,1024]{1,0:T(8,128)S(1)} %constant_dynamic-slice_fusion.1), channel_id=1, source_target_pairs={{0,1},{1,0},{2,3},{3,2},{4,5},{5,4},{6,7},{7,6},{8,9},{9,8},{10,11... | collective-permute-start | bytes 3145736 | tf_op jit(solution)/shard_map/ppermute | solution.py:45
  72.8 16.0 %collective-permute-start.5 = (bf16[256,1024]{1,0:T(8,128)(2,1)S(1)}, bf16[256,1024]{1,0:T(8,128)(2,1)S(1)}, u32[]{:S(2)}, u32[]{:S(2)}) collective-permute-start(bf16[256,1024]{1,0:T(8,128)(2,1)S(1)} %add_convert_fusion), channel_id=1, source_target_pairs={{0,2},{2,0},{1,3},{3,1},{4,6},{6,4},{5,7},{7,5},{8,10},{10,8},{9,1... | collective-permute-start | bytes 1572872 | tf_op jit(solution)/shard_map/ppermute | solution.py:49
  90.3 13.6 %collective-permute-start.6 = (bf16[256,1024]{1,0:T(8,128)(2,1)S(1)}, bf16[256,1024]{1,0:T(8,128)(2,1)S(1)}, u32[]{:S(2)}, u32[]{:S(2)}) collective-permute-start(bf16[256,1024]{1,0:T(8,128)(2,1)S(1)} %multiply_convert_fusion.1), channel_id=1, source_target_pairs={{0,16},{4,20},{8,24},{12,28},{16,0},{20,4},{24,8},{28,12},{32,48},... | collective-permute-start | bytes 1572872 | tf_op jit(solution)/shard_map/ppermute | solution.py:53
  112.6 2.9 %collective-permute-start.7 = (bf16[512,1024]{1,0:T(8,128)(2,1)}, bf16[512,1024]{1,0:T(8,128)(2,1)S(1)}, u32[]{:S(2)}, u32[]{:S(2)}) collective-permute-start(bf16[512,1024]{1,0:T(8,128)(2,1)} %pad_maximum_fusion.2), channel_id=1, source_target_pairs={{0,1},{1,0},{2,3},{3,2},{4,5},{5,4},{6,7},{7,6},{8,9},{9,8},{10,11... | collective-permute-start | bytes 3145736 | tf_op jit(solution)/shard_map/ppermute | solution.py:45
  127.5 4.2 %collective-permute-start.8 = (f32[512,1024]{1,0:T(8,128)S(1)}, f32[512,1024]{1,0:T(8,128)S(1)}, u32[]{:S(2)}, u32[]{:S(2)}) collective-permute-start(f32[512,1024]{1,0:T(8,128)S(1)} %get-tuple-element.72), channel_id=1, source_target_pairs={{0,1},{1,0},{2,3},{3,2},{4,5},{5,4},{6,7},{7,6},{8,9},{9,8},{10,11... | collective-permute-start | bytes 6291464 | tf_op jit(solution)/shard_map/ppermute | solution.py:45
  132.4 14.2 %collective-permute-start.9 = (bf16[256,1024]{1,0:T(8,128)(2,1)S(1)}, bf16[256,1024]{1,0:T(8,128)(2,1)S(1)}, u32[]{:S(2)}, u32[]{:S(2)}) collective-permute-start(bf16[256,1024]{1,0:T(8,128)(2,1)S(1)} %slice.363), channel_id=1, source_target_pairs={{0,16},{4,20},{8,24},{12,28},{16,0},{20,4},{24,8},{28,12},{32,48},... | collective-permute-start | bytes 1572872 | tf_op jit(solution)/shard_map/ppermute | solution.py:53
  147.6 15.4 %collective-permute-start.10 = (bf16[256,1024]{1,0:T(8,128)(2,1)}, bf16[256,1024]{1,0:T(8,128)(2,1)}, u32[]{:S(2)}, u32[]{:S(2)}) collective-permute-start(bf16[256,1024]{1,0:T(8,128)(2,1)} %convert_add_fusion.2), channel_id=1, source_target_pairs={{0,2},{2,0},{1,3},{3,1},{4,6},{6,4},{5,7},{7,5},{8,10},{10,8},{9,1... | collective-permute-start | bytes 1572872 | tf_op jit(solution)/shard_map/ppermute | solution.py:49
  151.2 55.1 %all-to-all-start.2 = ((bf16[16,2,32,1728]{3,2,1,0:T(8,128)(2,1)}), bf16[16,2,32,1728]{3,2,1,0:T(8,128)(2,1)}, u32[]{:S(2)}, u32[]{:S(2)}) async-start(bf16[16,2,32,1728]{3,2,1,0:T(8,128)(2,1)} %get-tuple-element.81), calls=%async_computation.2 | async-start | bytes 7340032 | tf_op jit(solution)/shard_map/all_to_all | solution.py:98
  166.9 2.3 collective-permute-start.11
  166.9 14.2 %collective-permute-start.14 = (f32[512,1024]{1,0:T(8,128)}, f32[512,1024]{1,0:T(8,128)}, u32[]{:S(2)}, u32[]{:S(2)}) collective-permute-start(f32[512,1024]{1,0:T(8,128)} %get-tuple-element.95), channel_id=1, source_target_pairs={{0,1},{1,0},{2,3},{3,2},{4,5},{5,4},{6,7},{7,6},{8,9},{9,8},{10,11... | collective-permute-start | bytes 6291464 | tf_op jit(solution)/shard_map/ppermute | solution.py:45
  180.7 5.8 %collective-permute-start.12 = (f32[256,1024]{1,0:T(8,128)S(1)}, f32[256,1024]{1,0:T(8,128)S(1)}, u32[]{:S(2)}, u32[]{:S(2)}) collective-permute-start(f32[256,1024]{1,0:T(8,128)S(1)} %constant_dynamic-slice_fusion), channel_id=1, source_target_pairs={{0,1},{1,0},{2,3},{3,2},{4,5},{5,4},{6,7},{7,6},{8,9},{9,8},{10,11... | collective-permute-start | bytes 3145736 | tf_op jit(solution)/shard_map/ppermute | solution.py:45
  183.3 23.0 %collective-permute-start.15 = (bf16[256,1024]{1,0:T(8,128)(2,1)S(1)}, bf16[256,1024]{1,0:T(8,128)(2,1)}, u32[]{:S(2)}, u32[]{:S(2)}) collective-permute-start(bf16[256,1024]{1,0:T(8,128)(2,1)S(1)} %slice.362), channel_id=1, source_target_pairs={{0,16},{4,20},{8,24},{12,28},{16,0},{20,4},{24,8},{28,12},{32,48},... | collective-permute-start | bytes 1572872 | tf_op jit(solution)/shard_map/ppermute | solution.py:53
  206.3 11.5 %collective-permute-start.13 = (bf16[256,1024]{1,0:T(8,128)(2,1)S(1)}, bf16[256,1024]{1,0:T(8,128)(2,1)}, u32[]{:S(2)}, u32[]{:S(2)}) collective-permute-start(bf16[256,1024]{1,0:T(8,128)(2,1)S(1)} %dynamic-slice_add_fusion), channel_id=1, source_target_pairs={{0,2},{2,0},{1,3},{3,1},{4,6},{6,4},{5,7},{7,5},{8,10},{10,8},{9,1... | collective-permute-start | bytes 1572872 | tf_op jit(solution)/shard_map/ppermute | solution.py:49
  207.5 36.7 %all-to-all-start.3 = ((bf16[16,2,32,1152]{3,2,1,0:T(8,128)(2,1)}), bf16[16,2,32,1152]{3,2,1,0:T(8,128)(2,1)S(1)}, u32[]{:S(2)}, u32[]{:S(2)}) async-start(bf16[16,2,32,1152]{3,2,1,0:T(8,128)(2,1)} %pad_maximum_fusion), calls=%async_computation.3 | async-start | bytes 4718592 | tf_op jit(solution)/shard_map/all_to_all | solution.py:98
  222.2 13.6 %collective-permute-start.16 = (bf16[256,1024]{1,0:T(8,128)(2,1)S(1)}, bf16[256,1024]{1,0:T(8,128)(2,1)S(1)}, u32[]{:S(2)}, u32[]{:S(2)}) collective-permute-start(bf16[256,1024]{1,0:T(8,128)(2,1)S(1)} %slice_add_fusion), channel_id=1, source_target_pairs={{0,2},{2,0},{1,3},{3,1},{4,6},{6,4},{5,7},{7,5},{8,10},{10,8},{9,1... | collective-permute-start | bytes 1572872 | tf_op jit(solution)/shard_map/ppermute | solution.py:49
  222.6 13.1 %collective-permute-start.20 = (f32[32,1728]{1,0:T(8,128)S(1)}, f32[32,1728]{1,0:T(8,128)S(1)}, u32[]{:S(2)}, u32[]{:S(2)}) collective-permute-start(f32[32,1728]{1,0:T(8,128)S(1)} %get-tuple-element.179), channel_id=1, source_target_pairs={{0,16},{4,20},{8,24},{12,28},{16,0},{20,4},{24,8},{28,12},{32,48},... | collective-permute-start | bytes 663560 | tf_op jit(solution)/shard_map/ppermute | solution.py:53
  237.7 2.8 %collective-permute-start.17 = (f32[256,1024]{1,0:T(8,128)S(1)}, f32[256,1024]{1,0:T(8,128)S(1)}, u32[]{:S(2)}, u32[]{:S(2)}) collective-permute-start(f32[256,1024]{1,0:T(8,128)S(1)} %get-tuple-element.171), channel_id=1, source_target_pairs={{0,1},{1,0},{2,3},{3,2},{4,5},{5,4},{6,7},{7,6},{8,9},{9,8},{10,11... | collective-permute-start | bytes 3145736 | tf_op jit(solution)/shard_map/ppermute | solution.py:45
  237.8 4.3 %collective-permute-start.18 = (f32[256,1024]{1,0:T(8,128)S(1)}, f32[256,1024]{1,0:T(8,128)S(1)}, u32[]{:S(2)}, u32[]{:S(2)}) collective-permute-start(f32[256,1024]{1,0:T(8,128)S(1)} %get-tuple-element.170), channel_id=1, source_target_pairs={{0,1},{1,0},{2,3},{3,2},{4,5},{5,4},{6,7},{7,6},{8,9},{9,8},{10,11... | collective-permute-start | bytes 3145736 | tf_op jit(solution)/shard_map/ppermute | solution.py:45
  244.6 5.2 %collective-permute-start.19 = (f32[32,1152]{1,0:T(8,128)S(1)}, f32[32,1152]{1,0:T(8,128)S(1)}, u32[]{:S(2)}, u32[]{:S(2)}) collective-permute-start(f32[32,1152]{1,0:T(8,128)S(1)} %dynamic-slice_bitcast_fusion.4), channel_id=1, source_target_pairs={{0,16},{4,20},{8,24},{12,28},{16,0},{20,4},{24,8},{28,12},{32,48},... | collective-permute-start | bytes 442376 | tf_op jit(solution)/shard_map/ppermute | solution.py:53
  (54 other events, 291.0 us)

commit v7 on v6

--- a/solution.py
+++ b/solution.py
@@ -129,6 +129,30 @@
     keep = lax.dynamic_index_in_dim(grad, near, 0, keepdims=False)
     take = swap_near(lax.dynamic_index_in_dim(grad, 1 - near, 0, keepdims=False))
     return jnp.concatenate(in_order(unpacked(keep), unpacked(take), near), axis=2)
+
+
+def spread_kernel(block_ref, copies_ref, sems):
+    copies = [
+        pltpu.make_async_copy(block_ref, copies_ref.at[i], sems.at[i]) for i in range(NX * NY)
+    ]
+    for copy in copies:
+        copy.start()
+    for copy in copies:
+        copy.wait()
+
+
+def spread_pass(block):
+    return pl.pallas_call(
+        spread_kernel,
+        in_specs=[pl.BlockSpec(memory_space=pltpu.VMEM)],
+        out_specs=pl.BlockSpec(memory_space=pltpu.HBM),
+        out_shape=jax.ShapeDtypeStruct((NX * NY,) + block.shape, block.dtype),
+        scratch_shapes=[pltpu.SemaphoreType.DMA((NX * NY,))],
+        cost_estimate=pl.CostEstimate(
+            flops=0, bytes_accessed=2 * NX * NY * block.size, transcendentals=0
+        ),
+        name="spread_pass",
+    )(block)
 
 
 VMEM_BYTES = 40 * 1024 * 1024
@@ -457,11 +481,11 @@
     give = packed(lax.dynamic_slice_in_dim(low_ffn, (1 - near) * part_units, part_units, 2))
     take = swap_near(give)
     low_ffn = jnp.stack(in_order(keep, take, near), axis=0)
-    ffn_copies = jnp.broadcast_to(low_ffn[None], (NX * NY,) + low_ffn.shape)
+    ffn_copies = spread_pass(low_ffn)
     back_out = cotangent.reshape(count, width)
     back_own, back_other = halves(back_out, core)
     back_near = swap_near(back_own)
-    back_four = jnp.concatenate([back_own, back_near, back_other, swap_core(back_near)], axis=0)
+    back_twin = swap_core(back_near)
 
     flat = wide(tokens_in.reshape(count, width))
     flat_half = halves(flat, core)[0]
@@ -473,8 +497,8 @@
     scale_one = lax.rsqrt(jnp.mean(flat * flat, axis=-1, keepdims=True) + epsilon_norm)
 
     mix_full = exchange(jnp.broadcast_to(low_mix[None], (NX * NY,) + low_mix.shape))
-    mix_full, ffn_copies, back_four, masks, scale_one = lax.optimization_barrier(
-        (mix_full, ffn_copies, back_four, masks, scale_one)
+    mix_full, ffn_copies, back_near, back_twin = lax.optimization_barrier(
+        (mix_full, ffn_copies, back_near, back_twin)
     )
     ffn_full = exchange(ffn_copies)
     mix_full = mix_full.reshape(NX, NY, NZ, own_rows, -1).transpose(0, 2, 1, 3, 4).reshape(width, -1)
@@ -498,7 +522,10 @@
     normed_two_f, norm_two_pull = jax.vjp(rms_gain, middle, gains_value[1])
     normed_two = low(normed_two_f)
     normed_two = jnp.concatenate([normed_two, swap_near(normed_two)], axis=0)
-    normed_two, ffn_full = lax.optimization_barrier((normed_two, ffn_full))
+    back_four = jnp.concatenate([back_own, back_near, back_other, back_twin], axis=0)
+    normed_two, ffn_full, back_four, masks, scale_one = lax.optimization_barrier(
+        (normed_two, ffn_full, back_four, masks, scale_one)
+    )
     normed_two = jnp.concatenate([normed_two, swap_core(normed_two)], axis=0)
 
     back_gate, back_up, hidden, back_keep, back_give = hidden_pass(

time: 264 us -> 257 us (0.973)
  waiting for transfers between devices: 101 us -> 92.3 us
  Pallas kernels: 26.2 us -> 29.2 us
    all_to_all x4, waiting for transfers between devices: 36.6 us -> 32.4 us  [exchange(): lax.all_to_all(blocks, 'dp', 0, 0, tiled=True, axis_index_groups=PLANES)]
    ppermute x8, waiting for transfers between devices: 33.9 us -> 29.9 us  [swap_near(): return lax.ppermute(value, 'dp', NEAR_PAIRS)]
    broadcast_in_dim x1 -> x0, local copies, waits for them, and re-layouts: 3.43 us -> none  [shards(): ffn_copies = jnp.broadcast_to(low_ffn[None], (NX * NY,) + low_ffn.shape)]
    pallas_call x0 -> x1, Pallas kernels: none -> 2.94 us  [spread_pass(): pl.pallas_call(spread_kernel, in_specs=[pl.BlockSpec(memory_space=pltpu.V...]
    unnamed x113 -> x123, local copies, waits for them, and re-layouts: 9.43 us -> 10.8 us
  transfers between devices with their start and end apart: 25 -> 25, of which waited for: 18 -> 17; matrix products, arithmetic and copies ran while one was open for 19% -> 22% of each run, Pallas kernels for 5% -> 7%
where the time goes in v7:
time: 257 us; the launch traced here: 253 us
  waiting for transfers between devices  92.3 us (36%)
  other arithmetic  44.9 us (17%)
  starting transfers between devices  43.8 us (17%)
  local copies, waits for them, and re-layouts  31.4 us (12%)
  Pallas kernels  29.2 us (11%)
  blocking collectives  6.56 us (3%)
  matrix products  2.78 us (1%)
    all_to_all x4, waiting for transfers between devices, exchange(): lax.all_to_all(blocks, 'dp', 0, 0, tiled=True, axis_index_groups=PLANES)  32.4 us
    ppermute x8, waiting for transfers between devices, swap_near(): return lax.ppermute(value, 'dp', NEAR_PAIRS)  29.9 us
    all_to_all x4, starting transfers between devices, exchange(): lax.all_to_all(blocks, 'dp', 0, 0, tiled=True, axis_index_groups=PLANES)  24.4 us
    ppermute x4, waiting for transfers between devices, swap_high(): return lax.ppermute(value, 'tensor', HIGH_PAIRS)  21.2 us
    pallas_call x1, Pallas kernels, hidden_pass(): pl.pallas_call(hidden_kernel, grid=(4,), in_specs=[pl.BlockSpec((block, w...  12 us
    unnamed x123, local copies, waits for them, and re-layouts  10.8 us
    ppermute x8, starting transfers between devices, swap_near(): return lax.ppermute(value, 'dp', NEAR_PAIRS)  10 us
    pallas_call x1, Pallas kernels, grads_pass(): pl.pallas_call(grads_kernel, grid=(NX,), in_specs=[pl.BlockSpec((tokens,...  9.93 us
  transfers between devices with their start and end apart: 25, of which 17 were waited for; matrix products, arithmetic and copies ran while one was open for 22% of the time, Pallas kernels for 7%

profile of v7, /device:TPU:0, one launch (start us, length us, event | category | flops | bytes accessed | tf_op | source)
XLA Modules:
  0.0 252.7 jit_solution(600858526410153655)
XLA Ops:
  9.3 7.2 %all-to-all-start = ((bf16[16,2,32,1152]{3,2,1,0:T(8,128)(2,1)}), bf16[16,2,32,1152]{3,2,1,0:T(8,128)(2,1)S(1)}, u32[]{:S(2)}, u32[]{:S(2)}) async-start(bf16[16,2,32,1152]{3,2,1,0:T(8,128)(2,1)} %broadcast_in_dim.51), calls=%async_computation | async-start | bytes 4718592 | tf_op jit(solution)/shard_map/all_to_all | solution.py:98
  31.6 5.4 %collective-permute-done.2 = bf16[256,1024]{1,0:T(8,128)(2,1)} collective-permute-done((bf16[256,1024]{1,0:T(8,128)(2,1)}, bf16[256,1024]{1,0:T(8,128)(2,1)}, u32[]{:S(2)}, u32[]{:S(2)}) %collective-permute-start.2) | collective-permute-done | bytes 524320 | tf_op jit(solution)/shard_map/ppermute | solution.py:53
  38.6 2.9 %spread_pass.1 = bf16[16,2,32,1728]{3,2,1,0:T(8,128)(2,1)} custom-call(bf16[2,32,1728]{2,1,0:T(8,128)(2,1)} %pad_maximum_fusion.6.block_ref), custom_call_target="tpu_custom_call" | custom-call | bytes 3538944 | tf_op jit(solution)/shard_map/spread_pass/pallas_call | solution.py:145
  41.6 6.7 %all-to-all-done = bf16[16,2,32,1152]{3,2,1,0:T(8,128)(2,1)S(1)} async-done(((bf16[16,2,32,1152]{3,2,1,0:T(8,128)(2,1)}), bf16[16,2,32,1152]{3,2,1,0:T(8,128)(2,1)S(1)}, u32[]{:S(2)}, u32[]{:S(2)}) %all-to-all-start) | async-done | bytes 2359328 | tf_op jit(solution)/shard_map/all_to_all | solution.py:98
  57.2 4.5 %all-to-all-start.1 = ((bf16[16,2,32,1728]{3,2,1,0:T(8,128)(2,1)}), bf16[16,2,32,1728]{3,2,1,0:T(8,128)(2,1)}, u32[]{:S(2)}, u32[]{:S(2)}) async-start(bf16[16,2,32,1728]{3,2,1,0:T(8,128)(2,1)} %spread_pass.1), calls=%async_computation.1 | async-start | bytes 7340032 | tf_op jit(solution)/shard_map/all_to_all | solution.py:98
  66.1 3.8 %collective-permute-start.5 = (bf16[256,1024]{1,0:T(8,128)(2,1)S(1)}, bf16[256,1024]{1,0:T(8,128)(2,1)S(1)}, u32[]{:S(2)}, u32[]{:S(2)}) collective-permute-start(bf16[256,1024]{1,0:T(8,128)(2,1)S(1)} %add_convert_fusion), channel_id=1, source_target_pairs={{0,2},{2,0},{1,3},{3,1},{4,6},{6,4},{5,7},{7,5},{8,10},{10,8},{9,1... | collective-permute-start | bytes 1572872 | tf_op jit(solution)/shard_map/ppermute | solution.py:49
  70.2 11.9 %collective-permute-done.5 = bf16[256,1024]{1,0:T(8,128)(2,1)S(1)} collective-permute-done((bf16[256,1024]{1,0:T(8,128)(2,1)S(1)}, bf16[256,1024]{1,0:T(8,128)(2,1)S(1)}, u32[]{:S(2)}, u32[]{:S(2)}) %collective-permute-start.5) | collective-permute-done | bytes 524320 | tf_op jit(solution)/shard_map/ppermute | solution.py:49
  87.3 3.0 %pad_maximum_fusion.1.back_ref = bf16[1024,1024]{1,0:T(8,128)(2,1)} fusion(bf16[256,1024]{1,0:T(8,128)(2,1)} %collective-permute-done.3, bf16[256,1024]{1,0:T(8,128)(2,1)} %get-tuple-element.178, bf16[256,1024]{1,0:T(8,128)(2,1)} %collective-permute-done.2, bf16[256,1024]{1,0:T(8,128)(2,1)} %get-tuple-element.179), kind=kLoop, calls=%fused_computation.3 | loop fusion | flops 8388608 | bytes 4194304 | tf_op jit(solution)/shard_map/concatenate | solution.py:525
  90.3 7.9 %collective-permute-done.6 = bf16[256,1024]{1,0:T(8,128)(2,1)} collective-permute-done((bf16[256,1024]{1,0:T(8,128)(2,1)}, bf16[256,1024]{1,0:T(8,128)(2,1)}, u32[]{:S(2)}, u32[]{:S(2)}) %collective-permute-start.6) | collective-permute-done | bytes 524320 | tf_op jit(solution)/shard_map/ppermute | solution.py:53
  100.4 5.5 %all-to-all-done.1.weights_ref = bf16[16,2,32,1728]{3,2,1,0:T(8,128)(2,1)} async-done(((bf16[16,2,32,1728]{3,2,1,0:T(8,128)(2,1)}), bf16[16,2,32,1728]{3,2,1,0:T(8,128)(2,1)}, u32[]{:S(2)}, u32[]{:S(2)}) %all-to-all-start.1) | async-done | bytes 3538976 | tf_op jit(solution)/shard_map/all_to_all | solution.py:98
  108.9 12.0 %hidden_pass.1 = (bf16[1024,576]{1,0:T(8,128)(2,1)S(1)}, bf16[1024,576]{1,0:T(8,128)(2,1)S(1)}, bf16[1024,576]{1,0:T(8,128)(2,1)S(1)}, f32[512,1024]{1,0:T(8,128)S(1)}, f32[512,1024]{1,0:T(8,128)S(1)}) custom-call(bf16[1024,1024]{1,0:T(8,128)(2,1)S(1)} %constant_dynamic-update-slice_fusion.2.normed_ref, bf16[1024,1024]{1,0:T(8,128)(2,1)S(1)} %copy-done.13, ...), custom_call_target="tpu_custom_call" | custom-call | flops 6039797760 | bytes 16777216 | tf_op jit(solution)/shard_map/hidden_pass/pallas_call | solution.py:220
  121.1 4.0 %collective-permute-done.8 = f32[512,1024]{1,0:T(8,128)S(1)} collective-permute-done((f32[512,1024]{1,0:T(8,128)S(1)}, f32[512,1024]{1,0:T(8,128)S(1)}, u32[]{:S(2)}, u32[]{:S(2)}) %collective-permute-start.8) | collective-permute-done | bytes 2097184 | tf_op jit(solution)/shard_map/ppermute | solution.py:45
  127.7 9.9 %grads_pass.1 = (bf16[16,2,32,1728]{3,2,1,0:T(8,128)(2,1)}, f32[512,1024]{1,0:T(8,128)S(1)}, f32[512,1024]{1,0:T(8,128)}) custom-call(bf16[1024,1024]{1,0:T(8,128)(2,1)S(1)} %constant_dynamic-update-slice_fusion.2.normed_ref, bf16[1024,1024]{1,0:T(8,128)(2,1)S(1)} %copy-done.13, bf16[1024,576]{1,0:T(8,128)(2,1)S(1)} %get-tuple-element.81.gate_ref, ...), custom_call_target="tpu_custom_call" | custom-call | flops 4831838208 | bytes 14680064 | tf_op jit(solution)/shard_map/grads_pass/pallas_call | solution.py:289
  140.9 3.7 %collective-permute-start.10 = (bf16[256,1024]{1,0:T(8,128)(2,1)}, bf16[256,1024]{1,0:T(8,128)(2,1)}, u32[]{:S(2)}, u32[]{:S(2)}) collective-permute-start(bf16[256,1024]{1,0:T(8,128)(2,1)} %convert_add_fusion.2), channel_id=1, source_target_pairs={{0,2},{2,0},{1,3},{3,1},{4,6},{6,4},{5,7},{7,5},{8,10},{10,8},{9,1... | collective-permute-start | bytes 1572872 | tf_op jit(solution)/shard_map/ppermute | solution.py:49
  144.6 6.3 %all-to-all-start.2 = ((bf16[16,2,32,1728]{3,2,1,0:T(8,128)(2,1)}), bf16[16,2,32,1728]{3,2,1,0:T(8,128)(2,1)}, u32[]{:S(2)}, u32[]{:S(2)}) async-start(bf16[16,2,32,1728]{3,2,1,0:T(8,128)(2,1)} %get-tuple-element.85), calls=%async_computation.2 | async-start | bytes 7340032 | tf_op jit(solution)/shard_map/all_to_all | solution.py:98
  150.9 5.4 %collective-permute-done.10 = bf16[256,1024]{1,0:T(8,128)(2,1)} collective-permute-done((bf16[256,1024]{1,0:T(8,128)(2,1)}, bf16[256,1024]{1,0:T(8,128)(2,1)}, u32[]{:S(2)}, u32[]{:S(2)}) %collective-permute-start.10) | collective-permute-done | bytes 524320 | tf_op jit(solution)/shard_map/ppermute | solution.py:49
  164.2 4.3 %mixer_pass.1 = (bf16[16,2,32,1024]{3,2,1,0:T(8,128)(2,1)S(1)}, f32[512,1024]{1,0:T(8,128)S(1)}, f32[1,1024]{1,0:T(1,128)S(1)}, f32[3,256]{1,0:T(4,128)S(1)}) custom-call(bf16[512,1024]{1,0:T(8,128)(2,1)S(1)} %pad_maximum_fusion.3.branch_ref.branch_part_ref, bf16[1024,1152]{1,0:T(8,128)(2,1)S(1)} %bitcast.159, f32[512,768]{1,0:T(8,128)S(1)} %copy-done.2, ...), custom_call_target="tpu_custom_call" | custom-call | flops 2147483648 | bytes 10485760 | tf_op jit(solution)/shard_map/mixer_pass/pallas_call | solution.py:383
  180.5 19.2 %all-to-all-done.2 = bf16[16,2,32,1728]{3,2,1,0:T(8,128)(2,1)} async-done(((bf16[16,2,32,1728]{3,2,1,0:T(8,128)(2,1)}), bf16[16,2,32,1728]{3,2,1,0:T(8,128)(2,1)}, u32[]{:S(2)}, u32[]{:S(2)}) %all-to-all-start.2) | async-done | bytes 3538976 | tf_op jit(solution)/shard_map/all_to_all | solution.py:98
  200.9 6.3 %all-to-all-start.3 = ((bf16[16,2,32,1152]{3,2,1,0:T(8,128)(2,1)}), bf16[16,2,32,1152]{3,2,1,0:T(8,128)(2,1)S(1)}, u32[]{:S(2)}, u32[]{:S(2)}) async-start(bf16[16,2,32,1152]{3,2,1,0:T(8,128)(2,1)} %pad_maximum_fusion), calls=%async_computation.3 | async-start | bytes 4718592 | tf_op jit(solution)/shard_map/all_to_all | solution.py:98
  207.2 3.9 %collective-permute-done.13 = bf16[256,1024]{1,0:T(8,128)(2,1)} collective-permute-done((bf16[256,1024]{1,0:T(8,128)(2,1)S(1)}, bf16[256,1024]{1,0:T(8,128)(2,1)}, u32[]{:S(2)}, u32[]{:S(2)}) %collective-permute-start.13) | collective-permute-done | bytes 524320 | tf_op jit(solution)/shard_map/ppermute | solution.py:49
  212.4 2.8 %convert_reduce_fusion = f32[2,32,1728]{2,1,0:T(8,128)S(1)} fusion(bf16[16,2,32,1728]{3,2,1,0:T(8,128)(2,1)} %all-to-all-done.2), kind=kLoop, calls=%fused_computation | loop fusion | flops 3428352 | bytes 3981312 | tf_op jit(solution)/shard_map/reduce_sum | solution.py:589
  217.3 11.8 %collective-permute-done.20 = f32[32,1728]{1,0:T(8,128)S(1)} collective-permute-done((f32[32,1728]{1,0:T(8,128)S(1)}, f32[32,1728]{1,0:T(8,128)S(1)}, u32[]{:S(2)}, u32[]{:S(2)}) %collective-permute-start.20) | collective-permute-done | bytes 221216 | tf_op jit(solution)/shard_map/ppermute | solution.py:53
  240.4 2.8 %collective-permute-done.19 = f32[32,1152]{1,0:T(8,128)S(1)} collective-permute-done((f32[32,1152]{1,0:T(8,128)S(1)}, f32[32,1152]{1,0:T(8,128)S(1)}, u32[]{:S(2)}, u32[]{:S(2)}) %collective-permute-start.19) | collective-permute-done | bytes 147488 | tf_op jit(solution)/shard_map/ppermute | solution.py:53
  243.5 6.6 %all_gather.3 = f32[4,2,32]{2,1,0:T(2,128)S(1)} all-gather(f32[1,2,32]{2,1,0:T(2,128)S(1)} %all_gather_reshape.3), channel_id=1, replica_groups=mesh['dp'=32,'tensor'=4] {'tensor'}, dimensions={0}, use_global_device_ids=true | all-gather | bytes 1280 | tf_op jit(solution)/shard_map/all_gather | solution.py:598
  (273 shorter events, 93.1 us)
Async XLA Ops:
  3.2 4.4 %collective-permute-start = (bf16[32,1152]{1,0:T(8,128)(2,1)S(1)}, bf16[32,1152]{1,0:T(8,128)(2,1)S(1)}, u32[]{:S(2)}, u32[]{:S(2)}) collective-permute-start(bf16[32,1152]{1,0:T(8,128)(2,1)S(1)} %constant_dynamic-update-slice_fusion), channel_id=1, source_target_pairs={{0,16},{4,20},{8,24},{12,28},{16,0},{20,4},{24,8},{28,12},{32,48},... | collective-permute-start | bytes 221192 | tf_op jit(solution)/shard_map/ppermute | solution.py:53
  9.3 39.0 %all-to-all-start = ((bf16[16,2,32,1152]{3,2,1,0:T(8,128)(2,1)}), bf16[16,2,32,1152]{3,2,1,0:T(8,128)(2,1)S(1)}, u32[]{:S(2)}, u32[]{:S(2)}) async-start(bf16[16,2,32,1152]{3,2,1,0:T(8,128)(2,1)} %broadcast_in_dim.51), calls=%async_computation | async-start | bytes 4718592 | tf_op jit(solution)/shard_map/all_to_all | solution.py:98
  20.5 16.5 %collective-permute-start.1 = (bf16[32,1728]{1,0:T(8,128)(2,1)}, bf16[32,1728]{1,0:T(8,128)(2,1)}, u32[]{:S(2)}, u32[]{:S(2)}) collective-permute-start(bf16[32,1728]{1,0:T(8,128)(2,1)} %concatenate.125), channel_id=1, source_target_pairs={{0,16},{4,20},{8,24},{12,28},{16,0},{20,4},{24,8},{28,12},{32,48},... | collective-permute-start | bytes 331784 | tf_op jit(solution)/shard_map/ppermute | solution.py:53
  24.7 12.3 %collective-permute-start.2 = (bf16[256,1024]{1,0:T(8,128)(2,1)}, bf16[256,1024]{1,0:T(8,128)(2,1)}, u32[]{:S(2)}, u32[]{:S(2)}) collective-permute-start(bf16[256,1024]{1,0:T(8,128)(2,1)} %get-tuple-element.179), channel_id=1, source_target_pairs={{0,16},{4,20},{8,24},{12,28},{16,0},{20,4},{24,8},{28,12},{32,48},... | collective-permute-start | bytes 1572872 | tf_op jit(solution)/shard_map/ppermute | solution.py:53
  37.0 4.6 %collective-permute-start.3 = (bf16[256,1024]{1,0:T(8,128)(2,1)}, bf16[256,1024]{1,0:T(8,128)(2,1)}, u32[]{:S(2)}, u32[]{:S(2)}) collective-permute-start(bf16[256,1024]{1,0:T(8,128)(2,1)} %collective-permute-done.2), channel_id=1, source_target_pairs={{0,1},{1,0},{2,3},{3,2},{4,5},{5,4},{6,7},{7,6},{8,9},{9,8},{10,11... | collective-permute-start | bytes 1572872 | tf_op jit(solution)/shard_map/ppermute | solution.py:45
  57.2 48.7 %all-to-all-start.1 = ((bf16[16,2,32,1728]{3,2,1,0:T(8,128)(2,1)}), bf16[16,2,32,1728]{3,2,1,0:T(8,128)(2,1)}, u32[]{:S(2)}, u32[]{:S(2)}) async-start(bf16[16,2,32,1728]{3,2,1,0:T(8,128)(2,1)} %spread_pass.1), calls=%async_computation.1 | async-start | bytes 7340032 | tf_op jit(solution)/shard_map/all_to_all | solution.py:98
  63.2 2.7 %collective-permute-start.4 = (f32[256,1024]{1,0:T(8,128)S(1)}, f32[256,1024]{1,0:T(8,128)S(1)}, u32[]{:S(2)}, u32[]{:S(2)}) collective-permute-start(f32[256,1024]{1,0:T(8,128)S(1)} %constant_dynamic-slice_fusion.1), channel_id=1, source_target_pairs={{0,1},{1,0},{2,3},{3,2},{4,5},{5,4},{6,7},{7,6},{8,9},{9,8},{10,11... | collective-permute-start | bytes 3145736 | tf_op jit(solution)/shard_map/ppermute | solution.py:45
  66.1 16.0 %collective-permute-start.5 = (bf16[256,1024]{1,0:T(8,128)(2,1)S(1)}, bf16[256,1024]{1,0:T(8,128)(2,1)S(1)}, u32[]{:S(2)}, u32[]{:S(2)}) collective-permute-start(bf16[256,1024]{1,0:T(8,128)(2,1)S(1)} %add_convert_fusion), channel_id=1, source_target_pairs={{0,2},{2,0},{1,3},{3,1},{4,6},{6,4},{5,7},{7,5},{8,10},{10,8},{9,1... | collective-permute-start | bytes 1572872 | tf_op jit(solution)/shard_map/ppermute | solution.py:49
  84.3 13.9 %collective-permute-start.6 = (bf16[256,1024]{1,0:T(8,128)(2,1)}, bf16[256,1024]{1,0:T(8,128)(2,1)}, u32[]{:S(2)}, u32[]{:S(2)}) collective-permute-start(bf16[256,1024]{1,0:T(8,128)(2,1)} %multiply_convert_fusion.1), channel_id=1, source_target_pairs={{0,16},{4,20},{8,24},{12,28},{16,0},{20,4},{24,8},{28,12},{32,48},... | collective-permute-start | bytes 1572872 | tf_op jit(solution)/shard_map/ppermute | solution.py:53
  105.9 2.9 %collective-permute-start.7 = (bf16[512,1024]{1,0:T(8,128)(2,1)}, bf16[512,1024]{1,0:T(8,128)(2,1)S(1)}, u32[]{:S(2)}, u32[]{:S(2)}) collective-permute-start(bf16[512,1024]{1,0:T(8,128)(2,1)} %pad_maximum_fusion.2), channel_id=1, source_target_pairs={{0,1},{1,0},{2,3},{3,2},{4,5},{5,4},{6,7},{7,6},{8,9},{9,8},{10,11... | collective-permute-start | bytes 3145736 | tf_op jit(solution)/shard_map/ppermute | solution.py:45
  120.8 4.2 %collective-permute-start.8 = (f32[512,1024]{1,0:T(8,128)S(1)}, f32[512,1024]{1,0:T(8,128)S(1)}, u32[]{:S(2)}, u32[]{:S(2)}) collective-permute-start(f32[512,1024]{1,0:T(8,128)S(1)} %get-tuple-element.76), channel_id=1, source_target_pairs={{0,1},{1,0},{2,3},{3,2},{4,5},{5,4},{6,7},{7,6},{8,9},{9,8},{10,11... | collective-permute-start | bytes 6291464 | tf_op jit(solution)/shard_map/ppermute | solution.py:45
  125.7 14.2 %collective-permute-start.9 = (bf16[256,1024]{1,0:T(8,128)(2,1)S(1)}, bf16[256,1024]{1,0:T(8,128)(2,1)S(1)}, u32[]{:S(2)}, u32[]{:S(2)}) collective-permute-start(bf16[256,1024]{1,0:T(8,128)(2,1)S(1)} %slice.363), channel_id=1, source_target_pairs={{0,16},{4,20},{8,24},{12,28},{16,0},{20,4},{24,8},{28,12},{32,48},... | collective-permute-start | bytes 1572872 | tf_op jit(solution)/shard_map/ppermute | solution.py:53
  140.9 15.4 %collective-permute-start.10 = (bf16[256,1024]{1,0:T(8,128)(2,1)}, bf16[256,1024]{1,0:T(8,128)(2,1)}, u32[]{:S(2)}, u32[]{:S(2)}) collective-permute-start(bf16[256,1024]{1,0:T(8,128)(2,1)} %convert_add_fusion.2), channel_id=1, source_target_pairs={{0,2},{2,0},{1,3},{3,1},{4,6},{6,4},{5,7},{7,5},{8,10},{10,8},{9,1... | collective-permute-start | bytes 1572872 | tf_op jit(solution)/shard_map/ppermute | solution.py:49
  144.6 55.1 %all-to-all-start.2 = ((bf16[16,2,32,1728]{3,2,1,0:T(8,128)(2,1)}), bf16[16,2,32,1728]{3,2,1,0:T(8,128)(2,1)}, u32[]{:S(2)}, u32[]{:S(2)}) async-start(bf16[16,2,32,1728]{3,2,1,0:T(8,128)(2,1)} %get-tuple-element.85), calls=%async_computation.2 | async-start | bytes 7340032 | tf_op jit(solution)/shard_map/all_to_all | solution.py:98
  160.2 14.3 %collective-permute-start.14 = (f32[512,1024]{1,0:T(8,128)}, f32[512,1024]{1,0:T(8,128)}, u32[]{:S(2)}, u32[]{:S(2)}) collective-permute-start(f32[512,1024]{1,0:T(8,128)} %get-tuple-element.99), channel_id=1, source_target_pairs={{0,1},{1,0},{2,3},{3,2},{4,5},{5,4},{6,7},{7,6},{8,9},{9,8},{10,11... | collective-permute-start | bytes 6291464 | tf_op jit(solution)/shard_map/ppermute | solution.py:45
  174.1 5.7 %collective-permute-start.12 = (f32[256,1024]{1,0:T(8,128)S(1)}, f32[256,1024]{1,0:T(8,128)S(1)}, u32[]{:S(2)}, u32[]{:S(2)}) collective-permute-start(f32[256,1024]{1,0:T(8,128)S(1)} %constant_dynamic-slice_fusion), channel_id=1, source_target_pairs={{0,1},{1,0},{2,3},{3,2},{4,5},{5,4},{6,7},{7,6},{8,9},{9,8},{10,11... | collective-permute-start | bytes 3145736 | tf_op jit(solution)/shard_map/ppermute | solution.py:45
  176.7 22.9 %collective-permute-start.15 = (bf16[256,1024]{1,0:T(8,128)(2,1)S(1)}, bf16[256,1024]{1,0:T(8,128)(2,1)}, u32[]{:S(2)}, u32[]{:S(2)}) collective-permute-start(bf16[256,1024]{1,0:T(8,128)(2,1)S(1)} %slice.362), channel_id=1, source_target_pairs={{0,16},{4,20},{8,24},{12,28},{16,0},{20,4},{24,8},{28,12},{32,48},... | collective-permute-start | bytes 1572872 | tf_op jit(solution)/shard_map/ppermute | solution.py:53
  199.7 11.5 %collective-permute-start.13 = (bf16[256,1024]{1,0:T(8,128)(2,1)S(1)}, bf16[256,1024]{1,0:T(8,128)(2,1)}, u32[]{:S(2)}, u32[]{:S(2)}) collective-permute-start(bf16[256,1024]{1,0:T(8,128)(2,1)S(1)} %dynamic-slice_add_fusion), channel_id=1, source_target_pairs={{0,2},{2,0},{1,3},{3,1},{4,6},{6,4},{5,7},{7,5},{8,10},{10,8},{9,1... | collective-permute-start | bytes 1572872 | tf_op jit(solution)/shard_map/ppermute | solution.py:49
  200.9 36.7 %all-to-all-start.3 = ((bf16[16,2,32,1152]{3,2,1,0:T(8,128)(2,1)}), bf16[16,2,32,1152]{3,2,1,0:T(8,128)(2,1)S(1)}, u32[]{:S(2)}, u32[]{:S(2)}) async-start(bf16[16,2,32,1152]{3,2,1,0:T(8,128)(2,1)} %pad_maximum_fusion), calls=%async_computation.3 | async-start | bytes 4718592 | tf_op jit(solution)/shard_map/all_to_all | solution.py:98
  215.6 13.6 %collective-permute-start.16 = (bf16[256,1024]{1,0:T(8,128)(2,1)S(1)}, bf16[256,1024]{1,0:T(8,128)(2,1)S(1)}, u32[]{:S(2)}, u32[]{:S(2)}) collective-permute-start(bf16[256,1024]{1,0:T(8,128)(2,1)S(1)} %slice_add_fusion), channel_id=1, source_target_pairs={{0,2},{2,0},{1,3},{3,1},{4,6},{6,4},{5,7},{7,5},{8,10},{10,8},{9,1... | collective-permute-start | bytes 1572872 | tf_op jit(solution)/shard_map/ppermute | solution.py:49
  216.0 13.0 %collective-permute-start.20 = (f32[32,1728]{1,0:T(8,128)S(1)}, f32[32,1728]{1,0:T(8,128)S(1)}, u32[]{:S(2)}, u32[]{:S(2)}) collective-permute-start(f32[32,1728]{1,0:T(8,128)S(1)} %get-tuple-element.183), channel_id=1, source_target_pairs={{0,16},{4,20},{8,24},{12,28},{16,0},{20,4},{24,8},{28,12},{32,48},... | collective-permute-start | bytes 663560 | tf_op jit(solution)/shard_map/ppermute | solution.py:53
  231.0 2.8 %collective-permute-start.17 = (f32[256,1024]{1,0:T(8,128)S(1)}, f32[256,1024]{1,0:T(8,128)S(1)}, u32[]{:S(2)}, u32[]{:S(2)}) collective-permute-start(f32[256,1024]{1,0:T(8,128)S(1)} %get-tuple-element.175), channel_id=1, source_target_pairs={{0,1},{1,0},{2,3},{3,2},{4,5},{5,4},{6,7},{7,6},{8,9},{9,8},{10,11... | collective-permute-start | bytes 3145736 | tf_op jit(solution)/shard_map/ppermute | solution.py:45
  231.2 4.3 %collective-permute-start.18 = (f32[256,1024]{1,0:T(8,128)S(1)}, f32[256,1024]{1,0:T(8,128)S(1)}, u32[]{:S(2)}, u32[]{:S(2)}) collective-permute-start(f32[256,1024]{1,0:T(8,128)S(1)} %get-tuple-element.174), channel_id=1, source_target_pairs={{0,1},{1,0},{2,3},{3,2},{4,5},{5,4},{6,7},{7,6},{8,9},{9,8},{10,11... | collective-permute-start | bytes 3145736 | tf_op jit(solution)/shard_map/ppermute | solution.py:45
  238.0 5.2 %collective-permute-start.19 = (f32[32,1152]{1,0:T(8,128)S(1)}, f32[32,1152]{1,0:T(8,128)S(1)}, u32[]{:S(2)}, u32[]{:S(2)}) collective-permute-start(f32[32,1152]{1,0:T(8,128)S(1)} %dynamic-slice_bitcast_fusion.4), channel_id=1, source_target_pairs={{0,16},{4,20},{8,24},{12,28},{16,0},{20,4},{24,8},{28,12},{32,48},... | collective-permute-start | bytes 442376 | tf_op jit(solution)/shard_map/ppermute | solution.py:53
  (59 other events, 359.0 us)

commit v8 on v7

--- a/solution.py
+++ b/solution.py
@@ -203,7 +203,7 @@
 
     @pl.when(step < 2)
     def _():
-        give_ref[...] = part
+        give_ref[...] = low(part)
 
     @pl.when(step >= 2)
     def _():
@@ -232,7 +232,7 @@
             pl.BlockSpec((block, width), lambda i: (jnp.maximum(i - 2, 0), 0)),
             pl.BlockSpec((block, width), lambda i: (jnp.minimum(i, 1), 0)),
         ],
-        out_shape=[narrow, narrow, narrow, half, half],
+        out_shape=[narrow, narrow, narrow, half, jax.ShapeDtypeStruct(half.shape, jnp.bfloat16)],
         scratch_shapes=[pltpu.VMEM((3, width, units), jnp.bfloat16)],
         compiler_params=pltpu.CompilerParams(vmem_limit_bytes=VMEM_BYTES),
         cost_estimate=pl.CostEstimate(
@@ -521,17 +521,19 @@
     middle = flat_half + sum_four(product_of("tc,dc->td", gated, out_full), core)
     normed_two_f, norm_two_pull = jax.vjp(rms_gain, middle, gains_value[1])
     normed_two = low(normed_two_f)
-    normed_two = jnp.concatenate([normed_two, swap_near(normed_two)], axis=0)
+    normed_near = swap_near(normed_two)
     back_four = jnp.concatenate([back_own, back_near, back_other, back_twin], axis=0)
-    normed_two, ffn_full, back_four, masks, scale_one = lax.optimization_barrier(
-        (normed_two, ffn_full, back_four, masks, scale_one)
-    )
-    normed_two = jnp.concatenate([normed_two, swap_core(normed_two)], axis=0)
+    normed_near, ffn_full, back_four, masks, scale_one = lax.optimization_barrier(
+        (normed_near, ffn_full, back_four, masks, scale_one)
+    )
+    normed_two = jnp.concatenate(
+        [normed_two, normed_near, swap_core(normed_two), swap_core(normed_near)], axis=0
+    )
 
     back_gate, back_up, hidden, back_keep, back_give = hidden_pass(
         normed_two, back_four, ffn_full
     )
-    back_pair = back_keep + swap_core(back_give)
+    back_pair = back_keep + wide(swap_core(back_give))
     back_pair, back_gate, back_up, hidden = lax.optimization_barrier(
         (back_pair, back_gate, back_up, hidden)
     )

time: 257 us -> 255 us (level)
    unnamed x123 -> x122, local copies, waits for them, and re-layouts: 10.8 us -> 9.93 us
    ppermute x9 -> x10, waiting for transfers between devices: 8.74 us -> 7.95 us  [swap_core(): return lax.ppermute(value, 'tensor', CORE_PAIRS)]
  transfers between devices with their start and end apart: 25 -> 26, of which waited for: 17 -> 17; matrix products, arithmetic and copies ran while one was open for 22% -> 21% of each run, Pallas kernels for 7% -> 7%
where the time goes in v8:
time: 255 us; the launch traced here: 250 us
  waiting for transfers between devices  92.3 us (36%)
  other arithmetic  45.9 us (18%)
  starting transfers between devices  44 us (17%)
  Pallas kernels  29.2 us (11%)
  local copies, waits for them, and re-layouts  29.1 us (11%)
  blocking collectives  6.56 us (3%)
    all_to_all x4, waiting for transfers between devices, exchange(): lax.all_to_all(blocks, 'dp', 0, 0, tiled=True, axis_index_groups=PLANES)  33.4 us
    ppermute x8, waiting for transfers between devices, swap_near(): return lax.ppermute(value, 'dp', NEAR_PAIRS)  29.8 us
    all_to_all x4, starting transfers between devices, exchange(): lax.all_to_all(blocks, 'dp', 0, 0, tiled=True, axis_index_groups=PLANES)  24.6 us
    ppermute x4, waiting for transfers between devices, swap_high(): return lax.ppermute(value, 'tensor', HIGH_PAIRS)  21.2 us
    pallas_call x1, Pallas kernels, hidden_pass(): pl.pallas_call(hidden_kernel, grid=(4,), in_specs=[pl.BlockSpec((block, w...  12 us
    ppermute x8, starting transfers between devices, swap_near(): return lax.ppermute(value, 'dp', NEAR_PAIRS)  10.1 us
    pallas_call x1, Pallas kernels, grads_pass(): pl.pallas_call(grads_kernel, grid=(NX,), in_specs=[pl.BlockSpec((tokens,...  9.94 us
    unnamed x122, local copies, waits for them, and re-layouts  9.93 us
  transfers between devices with their start and end apart: 26, of which 17 were waited for; matrix products, arithmetic and copies ran while one was open for 21% of the time, Pallas kernels for 7%

profile of v8, /device:TPU:0, one launch (start us, length us, event | category | flops | bytes accessed | tf_op | source)
XLA Modules:
  0.0 250.3 jit_solution(1003643730242128181)
XLA Ops:
  9.3 7.2 %all-to-all-start = ((bf16[16,2,32,1152]{3,2,1,0:T(8,128)(2,1)}), bf16[16,2,32,1152]{3,2,1,0:T(8,128)(2,1)S(1)}, u32[]{:S(2)}, u32[]{:S(2)}) async-start(bf16[16,2,32,1152]{3,2,1,0:T(8,128)(2,1)} %broadcast_in_dim.51), calls=%async_computation | async-start | bytes 4718592 | tf_op jit(solution)/shard_map/all_to_all | solution.py:98
  31.6 5.4 %collective-permute-done.2 = bf16[256,1024]{1,0:T(8,128)(2,1)} collective-permute-done((bf16[256,1024]{1,0:T(8,128)(2,1)}, bf16[256,1024]{1,0:T(8,128)(2,1)}, u32[]{:S(2)}, u32[]{:S(2)}) %collective-permute-start.2) | collective-permute-done | bytes 524320 | tf_op jit(solution)/shard_map/ppermute | solution.py:53
  38.6 2.9 %spread_pass.1 = bf16[16,2,32,1728]{3,2,1,0:T(8,128)(2,1)} custom-call(bf16[2,32,1728]{2,1,0:T(8,128)(2,1)} %pad_maximum_fusion.6.block_ref), custom_call_target="tpu_custom_call" | custom-call | bytes 3538944 | tf_op jit(solution)/shard_map/spread_pass/pallas_call | solution.py:145
  41.6 6.7 %all-to-all-done = bf16[16,2,32,1152]{3,2,1,0:T(8,128)(2,1)S(1)} async-done(((bf16[16,2,32,1152]{3,2,1,0:T(8,128)(2,1)}), bf16[16,2,32,1152]{3,2,1,0:T(8,128)(2,1)S(1)}, u32[]{:S(2)}, u32[]{:S(2)}) %all-to-all-start) | async-done | bytes 2359328 | tf_op jit(solution)/shard_map/all_to_all | solution.py:98
  55.5 4.7 %all-to-all-start.1 = ((bf16[16,2,32,1728]{3,2,1,0:T(8,128)(2,1)}), bf16[16,2,32,1728]{3,2,1,0:T(8,128)(2,1)}, u32[]{:S(2)}, u32[]{:S(2)}) async-start(bf16[16,2,32,1728]{3,2,1,0:T(8,128)(2,1)} %spread_pass.1), calls=%async_computation.1 | async-start | bytes 7340032 | tf_op jit(solution)/shard_map/all_to_all | solution.py:98
  62.9 2.7 %collective-permute-done.4 = f32[256,1024]{1,0:T(8,128)S(1)} collective-permute-done((f32[256,1024]{1,0:T(8,128)S(1)}, f32[256,1024]{1,0:T(8,128)S(1)}, u32[]{:S(2)}, u32[]{:S(2)}) %collective-permute-start.4) | collective-permute-done | bytes 1048608 | tf_op jit(solution)/shard_map/ppermute | solution.py:45
  65.8 3.8 %collective-permute-start.5 = (bf16[256,1024]{1,0:T(8,128)(2,1)S(1)}, bf16[256,1024]{1,0:T(8,128)(2,1)S(1)}, u32[]{:S(2)}, u32[]{:S(2)}) collective-permute-start(bf16[256,1024]{1,0:T(8,128)(2,1)S(1)} %add_convert_fusion), channel_id=1, source_target_pairs={{0,2},{2,0},{1,3},{3,1},{4,6},{6,4},{5,7},{7,5},{8,10},{10,8},{9,1... | collective-permute-start | bytes 1572872 | tf_op jit(solution)/shard_map/ppermute | solution.py:49
  69.8 11.9 %collective-permute-done.5 = bf16[256,1024]{1,0:T(8,128)(2,1)S(1)} collective-permute-done((bf16[256,1024]{1,0:T(8,128)(2,1)S(1)}, bf16[256,1024]{1,0:T(8,128)(2,1)S(1)}, u32[]{:S(2)}, u32[]{:S(2)}) %collective-permute-start.5) | collective-permute-done | bytes 524320 | tf_op jit(solution)/shard_map/ppermute | solution.py:49
  87.0 3.0 %pad_maximum_fusion.1.back_ref = bf16[1024,1024]{1,0:T(8,128)(2,1)} fusion(bf16[256,1024]{1,0:T(8,128)(2,1)} %collective-permute-done.3, bf16[256,1024]{1,0:T(8,128)(2,1)} %get-tuple-element.178, bf16[256,1024]{1,0:T(8,128)(2,1)} %collective-permute-done.2, bf16[256,1024]{1,0:T(8,128)(2,1)} %get-tuple-element.179), kind=kLoop, calls=%fused_computation.3 | loop fusion | flops 8388608 | bytes 4194304 | tf_op jit(solution)/shard_map/concatenate | solution.py:525
  90.0 7.9 %collective-permute-done.6 = bf16[256,1024]{1,0:T(8,128)(2,1)} collective-permute-done((bf16[256,1024]{1,0:T(8,128)(2,1)}, bf16[256,1024]{1,0:T(8,128)(2,1)}, u32[]{:S(2)}, u32[]{:S(2)}) %collective-permute-start.6) | collective-permute-done | bytes 524320 | tf_op jit(solution)/shard_map/ppermute | solution.py:53
  97.9 6.4 %all-to-all-done.1.weights_ref = bf16[16,2,32,1728]{3,2,1,0:T(8,128)(2,1)} async-done(((bf16[16,2,32,1728]{3,2,1,0:T(8,128)(2,1)}), bf16[16,2,32,1728]{3,2,1,0:T(8,128)(2,1)}, u32[]{:S(2)}, u32[]{:S(2)}) %all-to-all-start.1) | async-done | bytes 3538976 | tf_op jit(solution)/shard_map/all_to_all | solution.py:98
  108.1 12.0 %hidden_pass.1 = (bf16[1024,576]{1,0:T(8,128)(2,1)S(1)}, bf16[1024,576]{1,0:T(8,128)(2,1)S(1)}, bf16[1024,576]{1,0:T(8,128)(2,1)S(1)}, f32[512,1024]{1,0:T(8,128)S(1)}, bf16[512,1024]{1,0:T(8,128)(2,1)S(1)}) custom-call(bf16[1024,1024]{1,0:T(8,128)(2,1)S(1)} %pad_maximum_fusion.2.normed_ref, bf16[1024,1024]{1,0:T(8,128)(2,1)S(1)} %copy-done.13, ...), custom_call_target="tpu_custom_call" | custom-call | flops 6039797760 | bytes 16777216 | tf_op jit(solution)/shard_map/hidden_pass/pallas_call | solution.py:220
  125.2 9.9 %grads_pass.1 = (bf16[16,2,32,1728]{3,2,1,0:T(8,128)(2,1)}, f32[512,1024]{1,0:T(8,128)S(1)}, f32[512,1024]{1,0:T(8,128)}) custom-call(bf16[1024,1024]{1,0:T(8,128)(2,1)S(1)} %pad_maximum_fusion.2.normed_ref, bf16[1024,1024]{1,0:T(8,128)(2,1)S(1)} %copy-done.13, bf16[1024,576]{1,0:T(8,128)(2,1)S(1)} %get-tuple-element.81.gate_ref, ...), custom_call_target="tpu_custom_call" | custom-call | flops 4831838208 | bytes 14680064 | tf_op jit(solution)/shard_map/grads_pass/pallas_call | solution.py:289
  138.4 3.7 %collective-permute-start.11 = (bf16[256,1024]{1,0:T(8,128)(2,1)}, bf16[256,1024]{1,0:T(8,128)(2,1)}, u32[]{:S(2)}, u32[]{:S(2)}) collective-permute-start(bf16[256,1024]{1,0:T(8,128)(2,1)} %convert_add_fusion.3), channel_id=1, source_target_pairs={{0,2},{2,0},{1,3},{3,1},{4,6},{6,4},{5,7},{7,5},{8,10},{10,8},{9,1... | collective-permute-start | bytes 1572872 | tf_op jit(solution)/shard_map/ppermute | solution.py:49
  142.1 6.3 %all-to-all-start.2 = ((bf16[16,2,32,1728]{3,2,1,0:T(8,128)(2,1)}), bf16[16,2,32,1728]{3,2,1,0:T(8,128)(2,1)}, u32[]{:S(2)}, u32[]{:S(2)}) async-start(bf16[16,2,32,1728]{3,2,1,0:T(8,128)(2,1)} %get-tuple-element.85), calls=%async_computation.2 | async-start | bytes 7340032 | tf_op jit(solution)/shard_map/all_to_all | solution.py:98
  148.5 5.4 %collective-permute-done.11 = bf16[256,1024]{1,0:T(8,128)(2,1)} collective-permute-done((bf16[256,1024]{1,0:T(8,128)(2,1)}, bf16[256,1024]{1,0:T(8,128)(2,1)}, u32[]{:S(2)}, u32[]{:S(2)}) %collective-permute-start.11) | collective-permute-done | bytes 524320 | tf_op jit(solution)/shard_map/ppermute | solution.py:49
  161.7 4.3 %mixer_pass.1 = (bf16[16,2,32,1024]{3,2,1,0:T(8,128)(2,1)S(1)}, f32[512,1024]{1,0:T(8,128)S(1)}, f32[1,1024]{1,0:T(1,128)S(1)}, f32[3,256]{1,0:T(4,128)S(1)}) custom-call(bf16[512,1024]{1,0:T(8,128)(2,1)S(1)} %pad_maximum_fusion.3.branch_ref.branch_part_ref, bf16[1024,1152]{1,0:T(8,128)(2,1)S(1)} %bitcast.159, f32[512,768]{1,0:T(8,128)S(1)} %copy-done.2, ...), custom_call_target="tpu_custom_call" | custom-call | flops 2147483648 | bytes 10485760 | tf_op jit(solution)/shard_map/mixer_pass/pallas_call | solution.py:383
  178.1 19.2 %all-to-all-done.2 = bf16[16,2,32,1728]{3,2,1,0:T(8,128)(2,1)} async-done(((bf16[16,2,32,1728]{3,2,1,0:T(8,128)(2,1)}), bf16[16,2,32,1728]{3,2,1,0:T(8,128)(2,1)}, u32[]{:S(2)}, u32[]{:S(2)}) %all-to-all-start.2) | async-done | bytes 3538976 | tf_op jit(solution)/shard_map/all_to_all | solution.py:98
  198.4 6.3 %all-to-all-start.3 = ((bf16[16,2,32,1152]{3,2,1,0:T(8,128)(2,1)}), bf16[16,2,32,1152]{3,2,1,0:T(8,128)(2,1)S(1)}, u32[]{:S(2)}, u32[]{:S(2)}) async-start(bf16[16,2,32,1152]{3,2,1,0:T(8,128)(2,1)} %pad_maximum_fusion), calls=%async_computation.3 | async-start | bytes 4718592 | tf_op jit(solution)/shard_map/all_to_all | solution.py:98
  204.8 3.9 %collective-permute-done.14 = bf16[256,1024]{1,0:T(8,128)(2,1)} collective-permute-done((bf16[256,1024]{1,0:T(8,128)(2,1)S(1)}, bf16[256,1024]{1,0:T(8,128)(2,1)}, u32[]{:S(2)}, u32[]{:S(2)}) %collective-permute-start.14) | collective-permute-done | bytes 524320 | tf_op jit(solution)/shard_map/ppermute | solution.py:49
  209.9 2.8 %convert_reduce_fusion = f32[2,32,1728]{2,1,0:T(8,128)S(1)} fusion(bf16[16,2,32,1728]{3,2,1,0:T(8,128)(2,1)} %all-to-all-done.2), kind=kLoop, calls=%fused_computation | loop fusion | flops 3428352 | bytes 3981312 | tf_op jit(solution)/shard_map/reduce_sum | solution.py:591
  214.8 11.8 %collective-permute-done.21 = f32[32,1728]{1,0:T(8,128)S(1)} collective-permute-done((f32[32,1728]{1,0:T(8,128)S(1)}, f32[32,1728]{1,0:T(8,128)S(1)}, u32[]{:S(2)}, u32[]{:S(2)}) %collective-permute-start.21) | collective-permute-done | bytes 221216 | tf_op jit(solution)/shard_map/ppermute | solution.py:53
  238.0 2.8 %collective-permute-done.20 = f32[32,1152]{1,0:T(8,128)S(1)} collective-permute-done((f32[32,1152]{1,0:T(8,128)S(1)}, f32[32,1152]{1,0:T(8,128)S(1)}, u32[]{:S(2)}, u32[]{:S(2)}) %collective-permute-start.20) | collective-permute-done | bytes 147488 | tf_op jit(solution)/shard_map/ppermute | solution.py:53
  241.0 6.6 %all_gather.3 = f32[4,2,32]{2,1,0:T(2,128)S(1)} all-gather(f32[1,2,32]{2,1,0:T(2,128)S(1)} %all_gather_reshape.3), channel_id=1, replica_groups=mesh['dp'=32,'tensor'=4] {'tensor'}, dimensions={0}, use_global_device_ids=true | all-gather | bytes 1280 | tf_op jit(solution)/shard_map/all_gather | solution.py:600
  (273 shorter events, 91.0 us)
Async XLA Ops:
  3.2 4.4 %collective-permute-start = (bf16[32,1152]{1,0:T(8,128)(2,1)S(1)}, bf16[32,1152]{1,0:T(8,128)(2,1)S(1)}, u32[]{:S(2)}, u32[]{:S(2)}) collective-permute-start(bf16[32,1152]{1,0:T(8,128)(2,1)S(1)} %constant_dynamic-update-slice_fusion), channel_id=1, source_target_pairs={{0,16},{4,20},{8,24},{12,28},{16,0},{20,4},{24,8},{28,12},{32,48},... | collective-permute-start | bytes 221192 | tf_op jit(solution)/shard_map/ppermute | solution.py:53
  9.3 39.0 %all-to-all-start = ((bf16[16,2,32,1152]{3,2,1,0:T(8,128)(2,1)}), bf16[16,2,32,1152]{3,2,1,0:T(8,128)(2,1)S(1)}, u32[]{:S(2)}, u32[]{:S(2)}) async-start(bf16[16,2,32,1152]{3,2,1,0:T(8,128)(2,1)} %broadcast_in_dim.51), calls=%async_computation | async-start | bytes 4718592 | tf_op jit(solution)/shard_map/all_to_all | solution.py:98
  20.5 16.5 %collective-permute-start.1 = (bf16[32,1728]{1,0:T(8,128)(2,1)}, bf16[32,1728]{1,0:T(8,128)(2,1)}, u32[]{:S(2)}, u32[]{:S(2)}) collective-permute-start(bf16[32,1728]{1,0:T(8,128)(2,1)} %concatenate.122), channel_id=1, source_target_pairs={{0,16},{4,20},{8,24},{12,28},{16,0},{20,4},{24,8},{28,12},{32,48},... | collective-permute-start | bytes 331784 | tf_op jit(solution)/shard_map/ppermute | solution.py:53
  24.7 12.3 %collective-permute-start.2 = (bf16[256,1024]{1,0:T(8,128)(2,1)}, bf16[256,1024]{1,0:T(8,128)(2,1)}, u32[]{:S(2)}, u32[]{:S(2)}) collective-permute-start(bf16[256,1024]{1,0:T(8,128)(2,1)} %get-tuple-element.179), channel_id=1, source_target_pairs={{0,16},{4,20},{8,24},{12,28},{16,0},{20,4},{24,8},{28,12},{32,48},... | collective-permute-start | bytes 1572872 | tf_op jit(solution)/shard_map/ppermute | solution.py:53
  37.0 4.6 %collective-permute-start.3 = (bf16[256,1024]{1,0:T(8,128)(2,1)}, bf16[256,1024]{1,0:T(8,128)(2,1)}, u32[]{:S(2)}, u32[]{:S(2)}) collective-permute-start(bf16[256,1024]{1,0:T(8,128)(2,1)} %collective-permute-done.2), channel_id=1, source_target_pairs={{0,1},{1,0},{2,3},{3,2},{4,5},{5,4},{6,7},{7,6},{8,9},{9,8},{10,11... | collective-permute-start | bytes 1572872 | tf_op jit(solution)/shard_map/ppermute | solution.py:45
  55.5 48.8 %all-to-all-start.1 = ((bf16[16,2,32,1728]{3,2,1,0:T(8,128)(2,1)}), bf16[16,2,32,1728]{3,2,1,0:T(8,128)(2,1)}, u32[]{:S(2)}, u32[]{:S(2)}) async-start(bf16[16,2,32,1728]{3,2,1,0:T(8,128)(2,1)} %spread_pass.1), calls=%async_computation.1 | async-start | bytes 7340032 | tf_op jit(solution)/shard_map/all_to_all | solution.py:98
  62.9 2.7 %collective-permute-start.4 = (f32[256,1024]{1,0:T(8,128)S(1)}, f32[256,1024]{1,0:T(8,128)S(1)}, u32[]{:S(2)}, u32[]{:S(2)}) collective-permute-start(f32[256,1024]{1,0:T(8,128)S(1)} %constant_dynamic-slice_fusion.1), channel_id=1, source_target_pairs={{0,1},{1,0},{2,3},{3,2},{4,5},{5,4},{6,7},{7,6},{8,9},{9,8},{10,11... | collective-permute-start | bytes 3145736 | tf_op jit(solution)/shard_map/ppermute | solution.py:45
  65.8 16.0 %collective-permute-start.5 = (bf16[256,1024]{1,0:T(8,128)(2,1)S(1)}, bf16[256,1024]{1,0:T(8,128)(2,1)S(1)}, u32[]{:S(2)}, u32[]{:S(2)}) collective-permute-start(bf16[256,1024]{1,0:T(8,128)(2,1)S(1)} %add_convert_fusion), channel_id=1, source_target_pairs={{0,2},{2,0},{1,3},{3,1},{4,6},{6,4},{5,7},{7,5},{8,10},{10,8},{9,1... | collective-permute-start | bytes 1572872 | tf_op jit(solution)/shard_map/ppermute | solution.py:49
  84.1 13.9 %collective-permute-start.6 = (bf16[256,1024]{1,0:T(8,128)(2,1)}, bf16[256,1024]{1,0:T(8,128)(2,1)}, u32[]{:S(2)}, u32[]{:S(2)}) collective-permute-start(bf16[256,1024]{1,0:T(8,128)(2,1)} %multiply_convert_fusion.1), channel_id=1, source_target_pairs={{0,16},{4,20},{8,24},{12,28},{16,0},{20,4},{24,8},{28,12},{32,48},... | collective-permute-start | bytes 1572872 | tf_op jit(solution)/shard_map/ppermute | solution.py:53
  90.0 14.4 %collective-permute-start.7 = (bf16[256,1024]{1,0:T(8,128)(2,1)}, bf16[256,1024]{1,0:T(8,128)(2,1)}, u32[]{:S(2)}, u32[]{:S(2)}) collective-permute-start(bf16[256,1024]{1,0:T(8,128)(2,1)} %multiply_convert_fusion.1), channel_id=1, source_target_pairs={{0,1},{1,0},{2,3},{3,2},{4,5},{5,4},{6,7},{7,6},{8,9},{9,8},{10,11... | collective-permute-start | bytes 1572872 | tf_op jit(solution)/shard_map/ppermute | solution.py:45
  120.0 2.7 %collective-permute-start.9 = (bf16[512,1024]{1,0:T(8,128)(2,1)S(1)}, bf16[512,1024]{1,0:T(8,128)(2,1)S(1)}, u32[]{:S(2)}, u32[]{:S(2)}) collective-permute-start(bf16[512,1024]{1,0:T(8,128)(2,1)S(1)} %get-tuple-element.76), channel_id=1, source_target_pairs={{0,1},{1,0},{2,3},{3,2},{4,5},{5,4},{6,7},{7,6},{8,9},{9,8},{10,11... | collective-permute-start | bytes 3145736 | tf_op jit(solution)/shard_map/ppermute | solution.py:45
  123.3 14.2 %collective-permute-start.10 = (bf16[256,1024]{1,0:T(8,128)(2,1)S(1)}, bf16[256,1024]{1,0:T(8,128)(2,1)S(1)}, u32[]{:S(2)}, u32[]{:S(2)}) collective-permute-start(bf16[256,1024]{1,0:T(8,128)(2,1)S(1)} %slice.363), channel_id=1, source_target_pairs={{0,16},{4,20},{8,24},{12,28},{16,0},{20,4},{24,8},{28,12},{32,48},... | collective-permute-start | bytes 1572872 | tf_op jit(solution)/shard_map/ppermute | solution.py:53
  138.4 15.4 %collective-permute-start.11 = (bf16[256,1024]{1,0:T(8,128)(2,1)}, bf16[256,1024]{1,0:T(8,128)(2,1)}, u32[]{:S(2)}, u32[]{:S(2)}) collective-permute-start(bf16[256,1024]{1,0:T(8,128)(2,1)} %convert_add_fusion.3), channel_id=1, source_target_pairs={{0,2},{2,0},{1,3},{3,1},{4,6},{6,4},{5,7},{7,5},{8,10},{10,8},{9,1... | collective-permute-start | bytes 1572872 | tf_op jit(solution)/shard_map/ppermute | solution.py:49
  142.1 55.1 %all-to-all-start.2 = ((bf16[16,2,32,1728]{3,2,1,0:T(8,128)(2,1)}), bf16[16,2,32,1728]{3,2,1,0:T(8,128)(2,1)}, u32[]{:S(2)}, u32[]{:S(2)}) async-start(bf16[16,2,32,1728]{3,2,1,0:T(8,128)(2,1)} %get-tuple-element.85), calls=%async_computation.2 | async-start | bytes 7340032 | tf_op jit(solution)/shard_map/all_to_all | solution.py:98
  157.8 14.2 %collective-permute-start.15 = (f32[512,1024]{1,0:T(8,128)}, f32[512,1024]{1,0:T(8,128)}, u32[]{:S(2)}, u32[]{:S(2)}) collective-permute-start(f32[512,1024]{1,0:T(8,128)} %get-tuple-element.99), channel_id=1, source_target_pairs={{0,1},{1,0},{2,3},{3,2},{4,5},{5,4},{6,7},{7,6},{8,9},{9,8},{10,11... | collective-permute-start | bytes 6291464 | tf_op jit(solution)/shard_map/ppermute | solution.py:45
  171.5 5.9 %collective-permute-start.13 = (f32[256,1024]{1,0:T(8,128)S(1)}, f32[256,1024]{1,0:T(8,128)S(1)}, u32[]{:S(2)}, u32[]{:S(2)}) collective-permute-start(f32[256,1024]{1,0:T(8,128)S(1)} %constant_dynamic-slice_fusion), channel_id=1, source_target_pairs={{0,1},{1,0},{2,3},{3,2},{4,5},{5,4},{6,7},{7,6},{8,9},{9,8},{10,11... | collective-permute-start | bytes 3145736 | tf_op jit(solution)/shard_map/ppermute | solution.py:45
  174.2 23.0 %collective-permute-start.16 = (bf16[256,1024]{1,0:T(8,128)(2,1)S(1)}, bf16[256,1024]{1,0:T(8,128)(2,1)}, u32[]{:S(2)}, u32[]{:S(2)}) collective-permute-start(bf16[256,1024]{1,0:T(8,128)(2,1)S(1)} %slice.362), channel_id=1, source_target_pairs={{0,16},{4,20},{8,24},{12,28},{16,0},{20,4},{24,8},{28,12},{32,48},... | collective-permute-start | bytes 1572872 | tf_op jit(solution)/shard_map/ppermute | solution.py:53
  197.2 11.5 %collective-permute-start.14 = (bf16[256,1024]{1,0:T(8,128)(2,1)S(1)}, bf16[256,1024]{1,0:T(8,128)(2,1)}, u32[]{:S(2)}, u32[]{:S(2)}) collective-permute-start(bf16[256,1024]{1,0:T(8,128)(2,1)S(1)} %dynamic-slice_add_fusion), channel_id=1, source_target_pairs={{0,2},{2,0},{1,3},{3,1},{4,6},{6,4},{5,7},{7,5},{8,10},{10,8},{9,1... | collective-permute-start | bytes 1572872 | tf_op jit(solution)/shard_map/ppermute | solution.py:49
  198.4 36.7 %all-to-all-start.3 = ((bf16[16,2,32,1152]{3,2,1,0:T(8,128)(2,1)}), bf16[16,2,32,1152]{3,2,1,0:T(8,128)(2,1)S(1)}, u32[]{:S(2)}, u32[]{:S(2)}) async-start(bf16[16,2,32,1152]{3,2,1,0:T(8,128)(2,1)} %pad_maximum_fusion), calls=%async_computation.3 | async-start | bytes 4718592 | tf_op jit(solution)/shard_map/all_to_all | solution.py:98
  213.1 13.6 %collective-permute-start.17 = (bf16[256,1024]{1,0:T(8,128)(2,1)S(1)}, bf16[256,1024]{1,0:T(8,128)(2,1)S(1)}, u32[]{:S(2)}, u32[]{:S(2)}) collective-permute-start(bf16[256,1024]{1,0:T(8,128)(2,1)S(1)} %slice_add_fusion), channel_id=1, source_target_pairs={{0,2},{2,0},{1,3},{3,1},{4,6},{6,4},{5,7},{7,5},{8,10},{10,8},{9,1... | collective-permute-start | bytes 1572872 | tf_op jit(solution)/shard_map/ppermute | solution.py:49
  213.6 13.1 %collective-permute-start.21 = (f32[32,1728]{1,0:T(8,128)S(1)}, f32[32,1728]{1,0:T(8,128)S(1)}, u32[]{:S(2)}, u32[]{:S(2)}) collective-permute-start(f32[32,1728]{1,0:T(8,128)S(1)} %get-tuple-element.183), channel_id=1, source_target_pairs={{0,16},{4,20},{8,24},{12,28},{16,0},{20,4},{24,8},{28,12},{32,48},... | collective-permute-start | bytes 663560 | tf_op jit(solution)/shard_map/ppermute | solution.py:53
  228.6 2.8 %collective-permute-start.18 = (f32[256,1024]{1,0:T(8,128)S(1)}, f32[256,1024]{1,0:T(8,128)S(1)}, u32[]{:S(2)}, u32[]{:S(2)}) collective-permute-start(f32[256,1024]{1,0:T(8,128)S(1)} %get-tuple-element.175), channel_id=1, source_target_pairs={{0,1},{1,0},{2,3},{3,2},{4,5},{5,4},{6,7},{7,6},{8,9},{9,8},{10,11... | collective-permute-start | bytes 3145736 | tf_op jit(solution)/shard_map/ppermute | solution.py:45
  228.7 4.3 %collective-permute-start.19 = (f32[256,1024]{1,0:T(8,128)S(1)}, f32[256,1024]{1,0:T(8,128)S(1)}, u32[]{:S(2)}, u32[]{:S(2)}) collective-permute-start(f32[256,1024]{1,0:T(8,128)S(1)} %get-tuple-element.174), channel_id=1, source_target_pairs={{0,1},{1,0},{2,3},{3,2},{4,5},{5,4},{6,7},{7,6},{8,9},{9,8},{10,11... | collective-permute-start | bytes 3145736 | tf_op jit(solution)/shard_map/ppermute | solution.py:45
  235.6 5.2 %collective-permute-start.20 = (f32[32,1152]{1,0:T(8,128)S(1)}, f32[32,1152]{1,0:T(8,128)S(1)}, u32[]{:S(2)}, u32[]{:S(2)}) collective-permute-start(f32[32,1152]{1,0:T(8,128)S(1)} %dynamic-slice_bitcast_fusion.4), channel_id=1, source_target_pairs={{0,16},{4,20},{8,24},{12,28},{16,0},{20,4},{24,8},{28,12},{32,48},... | collective-permute-start | bytes 442376 | tf_op jit(solution)/shard_map/ppermute | solution.py:53
  (60 other events, 376.4 us)
